TPU v7x, 512 devices: a whole 4x8x8 slice. The times are simulated.
512 devices in a mesh: group: 32 (over x_hi, y, core), member: 16 (over x_lo, z).
Axes of the slice: x: 4 (x_hi: 2, x_lo: 2; x = x_hi * 2 + x_lo), y: 8, z: 8, core: 2. Of those that a mesh axis runs over, the one named last changes fastest.
Arguments:
- images: bfloat16 [16384, 1152], P(('group', 'member')), may hold values from -1.1953125 to 1.1953125
- texts: bfloat16 [16384, 1152], P(('group', 'member')), may hold values from -1.1953125 to 1.1953125
Outputs:
- image_grad: float32 [16384, 1152], P(('group', 'member'))
- text_grad: float32 [16384, 1152], P(('group', 'member'))
All inputs are finite; a program needn't handle non-finite values.
Results may differ from a plain program's by a relative error of at most 0.039.
Values may be sent and summed in bfloat16 or wider, within the bound.
No kernel may reach another device: no remote copies, remote signals or barrier semaphores. Data moves between devices by JAX's collectives and lax.ppermute only.
A program may use at most 64 MiB of HBM per device.

v0:
```python
import jax
import jax.numpy as jnp
from jax import lax
from jax.sharding import PartitionSpec as P

logit_scale = 30.0
logit_bias = -5.0
epsilon = 1e-06


def unit_rows(raw):
    wide = raw.astype(jnp.float32)
    inverse = lax.rsqrt(jnp.sum(wide * wide, axis=1, keepdims=True) + epsilon)
    return (wide * inverse, inverse)


def tile_coef(img_block, txt_block, group_idx, member_idx, rows):
    scores = jnp.dot(img_block, txt_block.T, preferred_element_type=jnp.float32)
    logits = logit_scale * scores + logit_bias
    img_pos = jnp.arange(img_block.shape[0], dtype=jnp.int32)[:, None]
    txt_pos = jnp.arange(txt_block.shape[0], dtype=jnp.int32)[None, :]
    same = (
        (txt_pos // rows == group_idx)
        & (img_pos // rows == member_idx)
        & (txt_pos % rows == img_pos % rows)
    )
    label = same.astype(jnp.float32)
    return (logit_scale * (jax.nn.sigmoid(logits) - label)).astype(jnp.bfloat16)


def raw_grad(unit_sum, unit, inverse):
    along = jnp.sum(unit_sum * unit, axis=1, keepdims=True)
    return inverse * (unit_sum - along * unit)


def local(images, texts):
    rows = images.shape[0]
    img_unit, img_inv = unit_rows(images)
    txt_unit, txt_inv = unit_rows(texts)
    img_bf = img_unit.astype(jnp.bfloat16)
    txt_bf = txt_unit.astype(jnp.bfloat16)
    group_idx = lax.axis_index("group")
    member_idx = lax.axis_index("member")
    img_block = lax.all_gather(img_bf, "member", axis=0, tiled=True)
    txt_block = lax.all_gather(txt_bf, "group", axis=0, tiled=True)
    coef = tile_coef(img_block, txt_block, group_idx, member_idx, rows)
    part = coef
    img_sum = lax.psum_scatter(
        jnp.dot(part, txt_block, preferred_element_type=jnp.float32).astype(jnp.bfloat16),
        "member",
        scatter_dimension=0,
        tiled=True,
    ).astype(jnp.float32)
    part = coef
    txt_sum = lax.psum_scatter(
        lax.dot_general(
            part, img_block, (((0,), (0,)), ((), ())), preferred_element_type=jnp.float32
        ).astype(jnp.bfloat16),
        "group",
        scatter_dimension=0,
        tiled=True,
    ).astype(jnp.float32)
    return (raw_grad(img_sum, img_unit, img_inv), raw_grad(txt_sum, txt_unit, txt_inv))


def solution(mesh):
    placed = (P(("group", "member"), None), P(("group", "member"), None))
    return jax.shard_map(
        local,
        mesh=mesh,
        in_specs=placed,
        out_specs=(P(("group", "member"), None), P(("group", "member"), None)),
        check_vma=False,
    )
```

profile of v0, /device:TPU:6, one launch (start us, length us, event | category | flops | bytes accessed | tf_op | source)
XLA Modules:
  0.0 392.1 jit_solution(4815848267783327775)
XLA Ops:
  7.2 0.0 all-gather.3.cloned.1.call-start
  7.2 1.0 fusion.4
  8.2 1.6 fusion.3
  9.8 0.0 all-gather.3.cloned.1.call-update
  9.9 0.0 all-gather.5.cloned.1.call-start
  9.9 1.0 fusion.5
  10.9 1.6 fusion.1
  12.5 0.0 all-gather.5.cloned.1.call-update
  12.6 0.0 reduce-scatter.3.cloned.1.call-start
  12.7 75.0 %all-gather.3.cloned.1.call-done = bf16[512,1152]{1,0:T(8,128)(2,1)} async-done(((bf16[32,1152]{1,0:T(8,128)(2,1)}), bf16[512,1152]{1,0:T(8,128)(2,1)}) %all-gather.3.cloned.1.call-update) | async-done | bytes 1179664 | tf_op jit(solution)/shard_map/all_gather | solution.py:44
  87.7 86.5 %all-gather.5.cloned.1.call-done = bf16[1024,1152]{1,0:T(8,128)(2,1)} async-done(((bf16[32,1152]{1,0:T(8,128)(2,1)}), bf16[1024,1152]{1,0:T(8,128)(2,1)}) %all-gather.5.cloned.1.call-update) | async-done | bytes 2359312 | tf_op jit(solution)/shard_map/all_gather | solution.py:45
  174.2 0.0 copy-start.2
  174.2 4.3 %multiply_convert_fusion = bf16[512,1024]{1,0:T(8,128)(2,1)S(1)} fusion(bf16[512,1152]{1,0:T(8,128)(2,1)} %all-gather.3.cloned.1.call-done, bf16[1024,1152]{1,0:T(8,128)(2,1)} %all-gather.5.cloned.1.call-done, s32[1024]{0:T(1024)S(1)} %fusion.10, s32[512]{0:T(512)S(1)} %fusion.18, pred[1024]{0:T(1024)(128)(4,1)S(1)} %fusion.16, pred[512]{0:T(512)(128)(4,1)S(1)} %fusion.22), kind=kOutput, calls=%fused_computation.2 | convolution fusion | flops 1214251008 | bytes 4595200 | tf_op jit(solution)/shard_map/dot_general | solution.py:18
  178.5 0.0 copy-done.2
  178.5 0.0 copy-start.3
  178.5 2.5 convolution_convert_fusion.1
  181.0 0.0 reduce-scatter.3.cloned.1.call-update
  181.0 0.0 reduce-scatter.5.cloned.1.call-start
  181.1 0.0 copy-done.3
  181.1 3.0 convolution_convert_fusion
  184.1 0.0 copy-start
  184.1 0.0 copy-start.1
  184.1 0.0 reduce-scatter.5.cloned.1.call-update
  184.1 70.3 %reduce-scatter.3.cloned.1.call-done = bf16[32,1152]{1,0:T(8,128)(2,1)} async-done(((bf16[512,1152]{1,0:T(8,128)(2,1)}), bf16[32,1152]{1,0:T(8,128)(2,1)}) %reduce-scatter.3.cloned.1.call-update) | async-done | bytes 73744 | tf_op jit(solution)/shard_map/reduce_scatter | solution.py:48
  254.5 0.0 copy-done
  254.5 1.1 fusion.6
  255.5 1.6 fusion.7
  257.2 125.7 %reduce-scatter.5.cloned.1.call-done = bf16[32,1152]{1,0:T(8,128)(2,1)} async-done(((bf16[1024,1152]{1,0:T(8,128)(2,1)}), bf16[32,1152]{1,0:T(8,128)(2,1)}) %reduce-scatter.5.cloned.1.call-update) | async-done | bytes 73744 | tf_op jit(solution)/shard_map/reduce_scatter | solution.py:55
  382.9 0.0 copy-done.1
  382.9 1.1 fusion.8
  383.9 1.6 fusion.9
  (6 shorter events, 0.0 us)
Async XLA Ops:
  7.2 80.5 %all-gather.3.cloned.1.call-start = ((), (), s32[]{:S(2)}) async-start(), calls=%async_computation.2 | async-start | bytes 1253376 | tf_op jit(solution)/shard_map/all_gather | solution.py:44
  9.9 164.3 %all-gather.5.cloned.1.call-start = ((), (), s32[]{:S(2)}) async-start(), calls=%async_computation.3 | async-start | bytes 2433024 | tf_op jit(solution)/shard_map/all_gather | solution.py:45
  12.6 241.9 %reduce-scatter.3.cloned.1.call-start = ((), (), s32[]{:S(2)}) async-start(), calls=%async_computation.4 | async-start | bytes 1253376 | tf_op jit(solution)/shard_map/reduce_scatter | solution.py:48
  174.2 4.3 %copy-start.2 = (bf16[1024,1152]{1,0:T(8,128)(2,1)S(1)}, bf16[1024,1152]{1,0:T(8,128)(2,1)}, u32[]{:S(2)}) copy-start(bf16[1024,1152]{1,0:T(8,128)(2,1)} %all-gather.5.cloned.1.call-done) | copy-start | bytes 7077892
  178.5 2.6 copy-start.3
  181.0 201.8 %reduce-scatter.5.cloned.1.call-start = ((), (), s32[]{:S(2)}) async-start(), calls=%async_computation.5 | async-start | bytes 2433024 | tf_op jit(solution)/shard_map/reduce_scatter | solution.py:55
  184.1 70.4 %copy-start = (bf16[32,1152]{1,0:T(8,128)(2,1)S(1)}, bf16[32,1152]{1,0:T(8,128)(2,1)}, u32[]{:S(2)}) copy-start(bf16[32,1152]{1,0:T(8,128)(2,1)} %param.2) | copy-start | bytes 221188
  184.1 198.8 %copy-start.1 = (bf16[32,1152]{1,0:T(8,128)(2,1)S(1)}, bf16[32,1152]{1,0:T(8,128)(2,1)}, u32[]{:S(2)}) copy-start(bf16[32,1152]{1,0:T(8,128)(2,1)} %param.3) | copy-start | bytes 221188
Sparse Core Ops, SparseCore 0:
  10.7 76.9 all-gather.2
  91.6 82.5 all-gather.4
  181.2 73.2 reduce-scatter.2
  259.0 123.7 reduce-scatter.4
where the time goes:
time: 394 us; the launch traced here: 392 us
  waiting for transfers between devices  358 us (91%)
  between operations  13.8 us (4%)
  other arithmetic  10.7 us (3%)
  matrix products  9.8 us (2%)
    reduce_scatter x1, waiting for transfers between devices, local(): lax.psum_scatter(lax.dot_general(part, img_block, (((0,), (0,)), ((), ())...  126 us
    all_gather x1, waiting for transfers between devices, local(): txt_block = lax.all_gather(txt_bf, 'group', axis=0, tiled=True)  86.5 us
    all_gather x1, waiting for transfers between devices, local(): img_block = lax.all_gather(img_bf, 'member', axis=0, tiled=True)  75 us
    reduce_scatter x1, waiting for transfers between devices, local(): lax.psum_scatter(jnp.dot(part, txt_block, preferred_element_type=jnp.floa...  70.3 us
  transfers between devices with their start and end apart: 4, of which 4 were waited for; matrix products, arithmetic and copies ran while one was open for 2% of the time, Pallas kernels for 0%

commit v1 on v0

v1 whole, which is shorter than its diff:
```python
import jax
import jax.numpy as jnp
from jax import lax
from jax.sharding import Mesh, PartitionSpec as P

logit_scale = 30.0
logit_bias = -5.0
epsilon = 1e-06

AXES = ("xh", "y", "core", "xl", "z")
SIZES = (2, 8, 2, 2, 8)
ALL = P(AXES, None)
SWAP = [(0, 1), (1, 0)]


def index_of(xh, y, core, xl, z):
    return (((xh * 8 + y) * 2 + core) * 2 + xl) * 8 + z


def line_groups():
    groups = []
    for xh in range(2):
        for y in range(8):
            groups.append([index_of(xh, y, 0, xl, z) for xl in range(2) for z in range(8)])
    for pair in range(2):
        for z in range(8):
            groups.append([index_of(xh, y, 1, xh ^ pair, z) for xh in range(2) for y in range(8)])
    return groups


def unit_rows(raw):
    wide = raw.astype(jnp.float32)
    inverse = lax.rsqrt(jnp.sum(wide * wide, axis=1, keepdims=True) + epsilon)
    return (wide * inverse, inverse)


def raw_grad(unit_sum, unit, inverse):
    along = jnp.sum(unit_sum * unit, axis=1, keepdims=True)
    return inverse * (unit_sum - along * unit)


def exchange(blocks, groups):
    return lax.all_to_all(
        blocks, AXES, split_axis=0, concat_axis=0, axis_index_groups=groups, tiled=True
    )


def local(images, texts):
    rows, width = images.shape
    half, full = 16 * rows, 32 * rows
    xh, y, core, xl, z = (lax.axis_index(name) for name in AXES)
    first = core == 0
    groups = line_groups()

    own = jnp.where(first, images, texts)
    other = lax.ppermute(jnp.where(first, texts, images), "core", SWAP)
    pair = jnp.where(
        first, jnp.concatenate([own, other], 0), jnp.concatenate([other, own], 0)
    )
    unit, inverse = unit_rows(pair)
    unit_bf = unit.astype(jnp.bfloat16)
    line = exchange(jnp.concatenate([unit_bf] * 16, 0), groups)

    near = lax.ppermute(line[:half], "core", SWAP)
    far = lax.ppermute(line[half:], "core", [(0, 1)])
    img = jnp.where(first, line, jnp.concatenate([near, far], 0))
    txt = jnp.where(first, near, line[half:])

    scores = jnp.dot(img, txt.T, preferred_element_type=jnp.float32)
    logits = logit_scale * scores + logit_bias
    img_pos = jnp.arange(full, dtype=jnp.int32)[:, None] - (xl * 8 + z) * (2 * rows)
    txt_pos = (
        jnp.arange(half, dtype=jnp.int32)[None, :] + core * half - (xh * 8 + y) * (2 * rows)
    )
    same = (img_pos == txt_pos) & (img_pos >= 0) & (img_pos < 2 * rows)
    label = same.astype(jnp.float32)
    coef = (logit_scale * (jax.nn.sigmoid(logits) - label)).astype(jnp.bfloat16)

    img_part = jnp.dot(coef, txt, preferred_element_type=jnp.float32)
    txt_part = lax.dot_general(
        coef, img, (((0,), (0,)), ((), ())), preferred_element_type=jnp.float32
    )
    img_bf = img_part.astype(jnp.bfloat16)
    txt_bf = txt_part.astype(jnp.bfloat16)
    near = lax.ppermute(jnp.where(first, txt_bf, img_bf[:half]), "core", SWAP)
    far = lax.ppermute(img_bf[half:], "core", [(1, 0)])
    img_all = jnp.concatenate([near, far], 0).astype(jnp.float32) + img_part
    txt_all = jnp.concatenate([near, txt_bf], 0)
    parts = exchange(jnp.where(first, img_all.astype(jnp.bfloat16), txt_all), groups)
    total = jnp.sum(parts.reshape(16, 2 * rows, width).astype(jnp.float32), axis=0)
    grad = raw_grad(total, unit, inverse)
    kept = jnp.where(first, grad[:rows], grad[rows:])
    got = lax.ppermute(jnp.where(first, grad[rows:], grad[:rows]), "core", SWAP)
    return (jnp.where(first, kept, got), jnp.where(first, got, kept))


def solution(mesh):
    fine = Mesh(mesh.devices.reshape(SIZES), AXES)
    return jax.shard_map(
        local, mesh=fine, in_specs=(ALL, ALL), out_specs=(ALL, ALL), check_vma=False
    )
```

time: 394 us -> 122 us (0.31)
  the two profiles are of different devices: /device:TPU:6 before, /device:TPU:1 now
where the time goes in v1:
time: 122 us
  blocking collectives  74.6 us (61%)
  starting transfers between devices  20.4 us (17%)
  waiting for transfers between devices  8.77 us (7%)
  matrix products  8.2 us (7%)
  other arithmetic  7.18 us (6%)
  local copies, waits for them, and re-layouts  1.64 us (1%)
    all_to_all x2, blocking collectives, exchange(): lax.all_to_all(blocks, AXES, split_axis=0, concat_axis=0, axis_index_grou...  74.6 us
    ppermute x1, starting transfers between devices, local(): other = lax.ppermute(jnp.where(first, texts, images), 'core', SWAP)  8.79 us
    ppermute x1, starting transfers between devices, local(): near = lax.ppermute(line[:half], 'core', SWAP)  4.42 us
    dot_general x1, matrix products, local(): scores = jnp.dot(img, txt.T, preferred_element_type=jnp.float32)  3.78 us
    dot_general x1, matrix products, local(): img_part = jnp.dot(coef, txt, preferred_element_type=jnp.float32)  2.82 us
  transfers between devices with their start and end apart: 6, of which 6 were waited for; matrix products, arithmetic and copies ran while one was open for 0% of the time, Pallas kernels for 0%

profile of v1, /device:TPU:1, one launch (start us, length us, event | category | flops | bytes accessed | tf_op | source)
XLA Modules:
  0.0 121.6 jit_solution(2741424890121098055)
XLA Ops:
  0.6 0.9 broadcast_select_fusion.5
  1.6 8.8 %collective-permute-start = (bf16[32,1152]{1,0:T(8,128)(2,1)S(1)}, bf16[32,1152]{1,0:T(8,128)(2,1)S(1)}, u32[]{:S(2)}, u32[]{:S(2)}) collective-permute-start(bf16[32,1152]{1,0:T(8,128)(2,1)S(1)} %get-tuple-element.8), channel_id=1, source_target_pairs={{0,16},{16,0},{1,17},{17,1},{2,18},{18,2},{3,19},{19,3},{4,20},{20... | collective-permute-start | bytes 221192 | tf_op jit(solution)/shard_map/ppermute | solution.py:56
  10.4 0.9 collective-permute-done
  11.3 0.1 fusion.8
  11.4 0.1 constant_dynamic-update-slice_fusion.15
  11.5 0.1 constant_dynamic-update-slice_fusion.14
  11.6 0.1 constant_dynamic-update-slice_fusion.13
  11.7 0.1 constant_dynamic-update-slice_fusion.12
  11.8 0.1 constant_dynamic-update-slice_fusion.11
  11.9 0.1 constant_dynamic-update-slice_fusion.10
  12.0 0.1 constant_dynamic-update-slice_fusion.9
  12.1 0.1 constant_dynamic-update-slice_fusion.8
  12.2 0.1 constant_dynamic-update-slice_fusion.7
  12.3 0.1 constant_dynamic-update-slice_fusion.6
  12.4 0.1 constant_dynamic-update-slice_fusion.5
  12.5 0.1 constant_dynamic-update-slice_fusion.4
  12.6 0.1 constant_dynamic-update-slice_fusion.3
  12.7 0.1 constant_dynamic-update-slice_fusion.2
  12.8 0.1 constant_dynamic-update-slice_fusion.1
  12.9 0.1 constant_dynamic-update-slice_fusion
  13.0 34.7 %all_to_all.21 = bf16[16,64,1152]{2,1,0:T(8,128)(2,1)S(1)} all-to-all(bf16[16,64,1152]{2,1,0:T(8,128)(2,1)S(1)} %bitcast.11), channel_id=1, replica_groups={{0,1,2,3,4,5,6,7,8,9,10,11,12,13,14,15},{32,33,34,35,36,37,38,39,40,41,..., dimensions={0} | all-to-all | bytes 4718592 | tf_op jit(solution)/shard_map/all_to_all | solution.py:43
  47.8 1.6 %fusion.12 = (bf16[8,64,1152]{2,1,0:T(8,128)(2,1)}, bf16[8,64,1152]{2,1,0:T(8,128)(2,1)}) fusion(bf16[16,64,1152]{2,1,0:T(8,128)(2,1)S(1)} %all_to_all.21), kind=kLoop, calls=%fused_computation.49 | loop fusion | bytes 4718592 | tf_op jit(solution)/shard_map/slice | solution.py:64
  49.4 4.4 %collective-permute-start.1 = (bf16[512,1152]{1,0:T(8,128)(2,1)}, bf16[512,1152]{1,0:T(8,128)(2,1)}, u32[]{:S(2)}, u32[]{:S(2)}) collective-permute-start(bf16[512,1152]{1,0:T(8,128)(2,1)} %bitcast.2), channel_id=1, source_target_pairs={{0,16},{16,0},{1,17},{17,1},{2,18},{18,2},{3,19},{19,3},{4,20},{20... | collective-permute-start | bytes 3538952 | tf_op jit(solution)/shard_map/ppermute | solution.py:64
  53.8 1.3 %collective-permute-start.2 = (bf16[512,1152]{1,0:T(8,128)(2,1)}, bf16[512,1152]{1,0:T(8,128)(2,1)}, u32[]{:S(2)}, u32[]{:S(2)}) collective-permute-start(bf16[512,1152]{1,0:T(8,128)(2,1)} %bitcast.3), channel_id=1, source_target_pairs={{0,16},{1,17},{2,18},{3,19},{4,20},{5,21},{6,22},{7,23},{8,24},{9,... | collective-permute-start | bytes 3538952 | tf_op jit(solution)/shard_map/ppermute | solution.py:65
  55.2 1.4 %collective-permute-done.1 = bf16[512,1152]{1,0:T(8,128)(2,1)} collective-permute-done((bf16[512,1152]{1,0:T(8,128)(2,1)}, bf16[512,1152]{1,0:T(8,128)(2,1)}, u32[]{:S(2)}, u32[]{:S(2)}) %collective-permute-start.1) | collective-permute-done | bytes 1179680 | tf_op jit(solution)/shard_map/ppermute | solution.py:64
  56.6 2.3 %collective-permute-done.2 = bf16[512,1152]{1,0:T(8,128)(2,1)} collective-permute-done((bf16[512,1152]{1,0:T(8,128)(2,1)}, bf16[512,1152]{1,0:T(8,128)(2,1)}, u32[]{:S(2)}, u32[]{:S(2)}) %collective-permute-start.2) | collective-permute-done | bytes 1179680 | tf_op jit(solution)/shard_map/ppermute | solution.py:65
  58.9 2.2 %maximum_select_fusion = bf16[1024,1152]{1,0:T(8,128)(2,1)S(1)} fusion(bf16[512,1152]{1,0:T(8,128)(2,1)} %collective-permute-done.2, bf16[512,1152]{1,0:T(8,128)(2,1)} %collective-permute-done.1, bf16[16,64,1152]{2,1,0:T(8,128)(2,1)S(1)} %all_to_all.21, pred[]{:T(512)S(6)} %eq.16), kind=kLoop, calls=%fused_computation.6 | loop fusion | flops 5898240 | bytes 7077889 | tf_op jit(solution)/shard_map/jit(_where)/select_n | solution.py:66
  61.1 3.8 %multiply_convert_fusion = bf16[1024,512]{1,0:T(8,128)(2,1)S(1)} fusion(bf16[1024,1152]{1,0:T(8,128)(2,1)S(1)} %maximum_select_fusion, s32[512]{0:T(512)S(1)} %add_subtract_fusion, s32[1024]{0:T(1024)S(1)} %iota_subtract_fusion, pred[1024]{0:T(1024)(128)(4,1)S(1)} %get-tuple-element.12, pred[1024]{0:T(1024)(128)(4,1)S(1)} %get-tuple-element.13, ...), kind=kOutput, calls=%fused_computation.7 | convolution fusion | flops 1214840832 | bytes 5775361 | tf_op jit(solution)/shard_map/dot_general | solution.py:69
  64.9 1.6 %convolution_convert_fusion = bf16[512,1152]{1,0:T(8,128)(2,1)S(1)} fusion(bf16[1024,512]{1,0:T(8,128)(2,1)S(1)} %multiply_convert_fusion, bf16[1024,1152]{1,0:T(8,128)(2,1)S(1)} %maximum_select_fusion), kind=kOutput, calls=%fused_computation.2 | convolution fusion | flops 1208549376 | bytes 4587520 | tf_op jit(solution)/shard_map/dot_general | solution.py:80
  66.5 2.8 %fusion.13 = (bf16[1024,1152]{1,0:T(8,128)(2,1)S(1)}, f32[1024,1152]{1,0:T(8,128)S(1)}) fusion(bf16[1024,512]{1,0:T(8,128)(2,1)S(1)} %multiply_convert_fusion, bf16[512,1152]{1,0:T(8,128)(2,1)} %collective-permute-done.1, bf16[512,1152]{1,0:T(8,128)(2,1)} %bitcast.3, pred[]{:T(512)S(6)} %eq.16), kind=kOutput, calls=%fused_computation.50 | convolution fusion | flops 1209729024 | bytes 10485761 | tf_op jit(solution)/shard_map/dot_general | solution.py:79
  69.3 0.3 fusion.11
  69.6 2.1 %collective-permute-start.4 = (bf16[512,1152]{1,0:T(8,128)(2,1)S(1)}, bf16[512,1152]{1,0:T(8,128)(2,1)S(1)}, u32[]{:S(2)}, u32[]{:S(2)}) collective-permute-start(bf16[512,1152]{1,0:T(8,128)(2,1)S(1)} %get-tuple-element.2), channel_id=1, source_target_pairs={{16,0},{17,1},{18,2},{19,3},{20,4},{21,5},{22,6},{23,7},{24,8},{25... | collective-permute-start | bytes 3538952 | tf_op jit(solution)/shard_map/ppermute | solution.py:86
  71.7 1.9 %collective-permute-start.3 = (bf16[512,1152]{1,0:T(8,128)(2,1)S(1)}, bf16[512,1152]{1,0:T(8,128)(2,1)S(1)}, u32[]{:S(2)}, u32[]{:S(2)}) collective-permute-start(bf16[512,1152]{1,0:T(8,128)(2,1)S(1)} %get-tuple-element.3), channel_id=1, source_target_pairs={{0,16},{16,0},{1,17},{17,1},{2,18},{18,2},{3,19},{19,3},{4,20},{20... | collective-permute-start | bytes 3538952 | tf_op jit(solution)/shard_map/ppermute | solution.py:85
  73.6 0.5 collective-permute-done.4
  74.0 2.4 %collective-permute-done.3 = bf16[512,1152]{1,0:T(8,128)(2,1)S(1)} collective-permute-done((bf16[512,1152]{1,0:T(8,128)(2,1)S(1)}, bf16[512,1152]{1,0:T(8,128)(2,1)S(1)}, u32[]{:S(2)}, u32[]{:S(2)}) %collective-permute-start.3) | collective-permute-done | bytes 1179680 | tf_op jit(solution)/shard_map/ppermute | solution.py:85
  76.4 0.6 fusion
  77.0 39.9 %all_to_all.22 = bf16[16,64,1152]{2,1,0:T(8,128)(2,1)S(1)} all-to-all(bf16[16,64,1152]{2,1,0:T(8,128)(2,1)S(1)} %bitcast.10), channel_id=1, replica_groups={{0,1,2,3,4,5,6,7,8,9,10,11,12,13,14,15},{32,33,34,35,36,37,38,39,40,41,..., dimensions={0} | all-to-all | bytes 4718592 | tf_op jit(solution)/shard_map/all_to_all | solution.py:43
  116.9 0.3 convert_reduce_fusion
  117.2 0.2 fusion.5
  117.4 0.1 fusion.7
  117.6 1.9 %collective-permute-start.5 = (f32[32,1152]{1,0:T(8,128)S(1)}, f32[32,1152]{1,0:T(8,128)S(1)}, u32[]{:S(2)}, u32[]{:S(2)}) collective-permute-start(f32[32,1152]{1,0:T(8,128)S(1)} %slice_select_fusion.1), channel_id=1, source_target_pairs={{0,16},{16,0},{1,17},{17,1},{2,18},{18,2},{3,19},{19,3},{4,20},{20... | collective-permute-start | bytes 442376 | tf_op jit(solution)/shard_map/ppermute | solution.py:93
  119.5 1.3 %collective-permute-done.5 = f32[32,1152]{1,0:T(8,128)S(1)} collective-permute-done((f32[32,1152]{1,0:T(8,128)S(1)}, f32[32,1152]{1,0:T(8,128)S(1)}, u32[]{:S(2)}, u32[]{:S(2)}) %collective-permute-start.5) | collective-permute-done | bytes 147488 | tf_op jit(solution)/shard_map/ppermute | solution.py:93
  120.9 0.7 broadcast_select_fusion.3
  (5 shorter events, 0.0 us)
Async XLA Ops:
  1.6 9.7 %collective-permute-start = (bf16[32,1152]{1,0:T(8,128)(2,1)S(1)}, bf16[32,1152]{1,0:T(8,128)(2,1)S(1)}, u32[]{:S(2)}, u32[]{:S(2)}) collective-permute-start(bf16[32,1152]{1,0:T(8,128)(2,1)S(1)} %get-tuple-element.8), channel_id=1, source_target_pairs={{0,16},{16,0},{1,17},{17,1},{2,18},{18,2},{3,19},{19,3},{4,20},{20... | collective-permute-start | bytes 221192 | tf_op jit(solution)/shard_map/ppermute | solution.py:56
  49.4 7.2 %collective-permute-start.1 = (bf16[512,1152]{1,0:T(8,128)(2,1)}, bf16[512,1152]{1,0:T(8,128)(2,1)}, u32[]{:S(2)}, u32[]{:S(2)}) collective-permute-start(bf16[512,1152]{1,0:T(8,128)(2,1)} %bitcast.2), channel_id=1, source_target_pairs={{0,16},{16,0},{1,17},{17,1},{2,18},{18,2},{3,19},{19,3},{4,20},{20... | collective-permute-start | bytes 3538952 | tf_op jit(solution)/shard_map/ppermute | solution.py:64
  53.8 5.1 %collective-permute-start.2 = (bf16[512,1152]{1,0:T(8,128)(2,1)}, bf16[512,1152]{1,0:T(8,128)(2,1)}, u32[]{:S(2)}, u32[]{:S(2)}) collective-permute-start(bf16[512,1152]{1,0:T(8,128)(2,1)} %bitcast.3), channel_id=1, source_target_pairs={{0,16},{1,17},{2,18},{3,19},{4,20},{5,21},{6,22},{7,23},{8,24},{9,... | collective-permute-start | bytes 3538952 | tf_op jit(solution)/shard_map/ppermute | solution.py:65
  69.6 4.5 %collective-permute-start.4 = (bf16[512,1152]{1,0:T(8,128)(2,1)S(1)}, bf16[512,1152]{1,0:T(8,128)(2,1)S(1)}, u32[]{:S(2)}, u32[]{:S(2)}) collective-permute-start(bf16[512,1152]{1,0:T(8,128)(2,1)S(1)} %get-tuple-element.2), channel_id=1, source_target_pairs={{16,0},{17,1},{18,2},{19,3},{20,4},{21,5},{22,6},{23,7},{24,8},{25... | collective-permute-start | bytes 3538952 | tf_op jit(solution)/shard_map/ppermute | solution.py:86
  71.7 4.7 %collective-permute-start.3 = (bf16[512,1152]{1,0:T(8,128)(2,1)S(1)}, bf16[512,1152]{1,0:T(8,128)(2,1)S(1)}, u32[]{:S(2)}, u32[]{:S(2)}) collective-permute-start(bf16[512,1152]{1,0:T(8,128)(2,1)S(1)} %get-tuple-element.3), channel_id=1, source_target_pairs={{0,16},{16,0},{1,17},{17,1},{2,18},{18,2},{3,19},{19,3},{4,20},{20... | collective-permute-start | bytes 3538952 | tf_op jit(solution)/shard_map/ppermute | solution.py:85
  117.6 3.3 %collective-permute-start.5 = (f32[32,1152]{1,0:T(8,128)S(1)}, f32[32,1152]{1,0:T(8,128)S(1)}, u32[]{:S(2)}, u32[]{:S(2)}) collective-permute-start(f32[32,1152]{1,0:T(8,128)S(1)} %slice_select_fusion.1), channel_id=1, source_target_pairs={{0,16},{16,0},{1,17},{17,1},{2,18},{18,2},{3,19},{19,3},{4,20},{20... | collective-permute-start | bytes 442376 | tf_op jit(solution)/shard_map/ppermute | solution.py:93

commit v2 on v1

v2 whole, which is shorter than its diff:
```python
import jax
import jax.numpy as jnp
from jax import lax
from jax.sharding import Mesh, PartitionSpec as P

logit_scale = 30.0
logit_bias = -5.0
epsilon = 1e-06

AXES = ("xh", "y", "core", "xl", "z")
SIZES = (2, 8, 2, 2, 8)
ALL = P(AXES, None)
SWAP = [(0, 1), (1, 0)]


def index_of(xh, y, core, xl, z):
    return (((xh * 8 + y) * 2 + core) * 2 + xl) * 8 + z


def devices():
    for xh in range(2):
        for y in range(8):
            for core in range(2):
                for xl in range(2):
                    for z in range(8):
                        yield xh, y, core, xl, z


def line_step(step):
    pairs = []
    for xh, y, core, xl, z in devices():
        to = (xh, y, core, xl, (z + step) % 8) if core == 0 else (xh, (y + step) % 8, core, xl, z)
        pairs.append((index_of(xh, y, core, xl, z), index_of(*to)))
    return pairs


def across_x():
    pairs = []
    for xh, y, core, xl, z in devices():
        to = (xh ^ core, y, core, 1 - xl, z)
        pairs.append((index_of(xh, y, core, xl, z), index_of(*to)))
    return pairs


def send(block, pairs):
    return lax.ppermute(block, AXES, pairs)


def unit_rows(raw):
    wide = raw.astype(jnp.float32)
    inverse = lax.rsqrt(jnp.sum(wide * wide, axis=1, keepdims=True) + epsilon)
    return (wide * inverse, inverse)


def raw_grad(unit_sum, unit, inverse):
    along = jnp.sum(unit_sum * unit, axis=1, keepdims=True)
    return inverse * (unit_sum - along * unit)


def pull(mine, theirs, own_pairs):
    scores = lax.dot_general(
        mine, theirs, (((1,), (1,)), ((), ())), preferred_element_type=jnp.float32
    )
    chance = jax.nn.sigmoid(logit_scale * scores + logit_bias)
    if own_pairs:
        row = lax.broadcasted_iota(jnp.int32, chance.shape, 0)
        column = lax.broadcasted_iota(jnp.int32, chance.shape, 1)
        chance = chance - ((row == column) & (row < own_pairs)).astype(jnp.float32)
    coef = (logit_scale * chance).astype(jnp.bfloat16)
    return jnp.dot(coef, theirs, preferred_element_type=jnp.float32)


def local(images, texts):
    rows, width = images.shape
    chip = 2 * rows
    first = lax.axis_index("core") == 0
    bf = jnp.bfloat16

    own = jnp.where(first, images, texts)
    other = lax.ppermute(jnp.where(first, texts, images), "core", SWAP)
    pair = jnp.where(
        first, jnp.concatenate([own, other], 0), jnp.concatenate([other, own], 0)
    )
    unit, inverse = unit_rows(pair)
    unit_bf = unit.astype(bf)

    up3 = send(unit_bf, line_step(-3))
    down3 = send(unit_bf, line_step(3))
    three = jnp.concatenate([unit_bf, up3, down3], 0)
    far_three = send(three, across_x())
    up1 = send(three, line_step(-1))
    down1 = send(three[: 2 * chip], line_step(1))
    five = jnp.concatenate([up1, down1], 0)
    far_five = send(five, across_x())

    mine = jnp.concatenate([three, five, far_three], 0)
    theirs = lax.ppermute(mine, "core", SWAP)
    their_five = lax.ppermute(far_five, "core", SWAP)

    near_sum = pull(mine, theirs, chip)
    far_sum = pull(far_five, theirs, 0) + pull(far_five, their_five, 0)
    back_five = send(far_sum.astype(bf), across_x())
    near_sum = near_sum + pull(mine, their_five, 0)
    back_three = send(near_sum[8 * chip :].astype(bf), across_x())

    sum_five = (near_sum[3 * chip : 8 * chip] + back_five.astype(jnp.float32)).astype(bf)
    from_down = send(sum_five[: 3 * chip], line_step(1)).astype(jnp.float32)
    from_up = send(sum_five[3 * chip :], line_step(-1)).astype(jnp.float32)
    sum_three = near_sum[: 3 * chip] + back_three.astype(jnp.float32) + from_down
    sum_two = sum_three[: 2 * chip] + from_up
    from_down = send(sum_two[chip:].astype(bf), line_step(3))
    from_up = send(sum_three[2 * chip :].astype(bf), line_step(-3))
    total = sum_two[:chip] + from_down.astype(jnp.float32) + from_up.astype(jnp.float32)

    grad = raw_grad(total, unit, inverse)
    kept = jnp.where(first, grad[:rows], grad[rows:])
    got = lax.ppermute(jnp.where(first, grad[rows:], grad[:rows]), "core", SWAP)
    return (jnp.where(first, kept, got), jnp.where(first, got, kept))


def solution(mesh):
    fine = Mesh(mesh.devices.reshape(SIZES), AXES)
    return jax.shard_map(
        local, mesh=fine, in_specs=(ALL, ALL), out_specs=(ALL, ALL), check_vma=False
    )
```

time: 122 us -> 122 us (level)
  the two profiles are of different devices: /device:TPU:1 before, /device:TPU:9 now
where the time goes in v2:
time: 122 us; the launch traced here: 121 us
  starting transfers between devices  56.7 us (46%)
  waiting for transfers between devices  41.9 us (34%)
  matrix products  17.7 us (15%)
  other arithmetic  3.94 us (3%)
    ppermute x12, starting transfers between devices, send(): return lax.ppermute(block, AXES, pairs)  41.8 us
    ppermute x12, waiting for transfers between devices, send(): return lax.ppermute(block, AXES, pairs)  39.6 us
    dot_general x4, matrix products, pull(): return jnp.dot(coef, theirs, preferred_element_type=jnp.float32)  17.7 us
    ppermute x1, starting transfers between devices, local(): theirs = lax.ppermute(mine, 'core', SWAP)  8.46 us
    ppermute x1, starting transfers between devices, local(): other = lax.ppermute(jnp.where(first, texts, images), 'core', SWAP)  2.58 us
  transfers between devices with their start and end apart: 16, of which 12 were waited for; matrix products, arithmetic and copies ran while one was open for 13% of the time, Pallas kernels for 0%

profile of v2, /device:TPU:9, one launch (start us, length us, event | category | flops | bytes accessed | tf_op | source)
XLA Modules:
  0.0 121.4 jit_solution(6152240261060391474)
XLA Ops:
  0.6 0.9 broadcast_select_fusion.2
  1.6 2.6 %collective-permute-start = (bf16[32,1152]{1,0:T(8,128)(2,1)S(1)}, bf16[32,1152]{1,0:T(8,128)(2,1)S(1)}, u32[]{:S(2)}, u32[]{:S(2)}) collective-permute-start(bf16[32,1152]{1,0:T(8,128)(2,1)S(1)} %get-tuple-element.6), channel_id=1, source_target_pairs={{0,16},{16,0},{1,17},{17,1},{2,18},{18,2},{3,19},{19,3},{4,20},{20... | collective-permute-start | bytes 221192 | tf_op jit(solution)/shard_map/ppermute | solution.py:80
  4.2 0.9 collective-permute-done
  5.1 0.1 fusion.39
  5.2 0.1 constant_dynamic-update-slice_fusion.5
  5.3 6.4 %collective-permute-start.2 = (bf16[64,1152]{1,0:T(8,128)(2,1)S(1)}, bf16[64,1152]{1,0:T(8,128)(2,1)S(1)}, u32[]{:S(2)}, u32[]{:S(2)}) collective-permute-start(bf16[64,1152]{1,0:T(8,128)(2,1)S(1)} %get-tuple-element.3), channel_id=1, source_target_pairs={{0,3},{1,4},{2,5},{3,6},{4,7},{5,0},{6,1},{7,2},{8,11},{9,12},{10,... | collective-permute-start | bytes 442376 | tf_op jit(solution)/shard_map/ppermute | solution.py:46
  11.8 1.9 %collective-permute-start.1 = (bf16[64,1152]{1,0:T(8,128)(2,1)S(1)}, bf16[64,1152]{1,0:T(8,128)(2,1)S(1)}, u32[]{:S(2)}, u32[]{:S(2)}) collective-permute-start(bf16[64,1152]{1,0:T(8,128)(2,1)S(1)} %get-tuple-element.3), channel_id=1, source_target_pairs={{0,5},{1,6},{2,7},{3,0},{4,1},{5,2},{6,3},{7,4},{8,13},{9,14},{10,... | collective-permute-start | bytes 442376 | tf_op jit(solution)/shard_map/ppermute | solution.py:46
  13.7 3.3 %collective-permute-done.2 = bf16[64,1152]{1,0:T(8,128)(2,1)S(1)} collective-permute-done((bf16[64,1152]{1,0:T(8,128)(2,1)S(1)}, bf16[64,1152]{1,0:T(8,128)(2,1)S(1)}, u32[]{:S(2)}, u32[]{:S(2)}) %collective-permute-start.2) | collective-permute-done | bytes 147488 | tf_op jit(solution)/shard_map/ppermute | solution.py:46
  17.0 6.8 %collective-permute-done.1 = bf16[64,1152]{1,0:T(8,128)(2,1)S(1)} collective-permute-done((bf16[64,1152]{1,0:T(8,128)(2,1)S(1)}, bf16[64,1152]{1,0:T(8,128)(2,1)S(1)}, u32[]{:S(2)}, u32[]{:S(2)}) %collective-permute-start.1) | collective-permute-done | bytes 147488 | tf_op jit(solution)/shard_map/ppermute | solution.py:46
  23.9 4.4 %collective-permute-start.5 = (bf16[192,1152]{1,0:T(8,128)(2,1)S(1)}, bf16[192,1152]{1,0:T(8,128)(2,1)S(1)}, u32[]{:S(2)}, u32[]{:S(2)}) collective-permute-start(bf16[192,1152]{1,0:T(8,128)(2,1)S(1)} %pad_maximum_fusion.1), channel_id=1, source_target_pairs={{0,8},{1,9},{2,10},{3,11},{4,12},{5,13},{6,14},{7,15},{8,0},{9,1},... | collective-permute-start | bytes 1327112 | tf_op jit(solution)/shard_map/ppermute | solution.py:46
  28.3 1.9 %collective-permute-start.3 = (bf16[192,1152]{1,0:T(8,128)(2,1)S(1)}, bf16[192,1152]{1,0:T(8,128)(2,1)S(1)}, u32[]{:S(2)}, u32[]{:S(2)}) collective-permute-start(bf16[192,1152]{1,0:T(8,128)(2,1)S(1)} %pad_maximum_fusion.1), channel_id=1, source_target_pairs={{0,7},{1,0},{2,1},{3,2},{4,3},{5,4},{6,5},{7,6},{8,15},{9,8},{10,9... | collective-permute-start | bytes 1327112 | tf_op jit(solution)/shard_map/ppermute | solution.py:46
  30.2 3.4 %collective-permute-start.4 = (bf16[128,1152]{1,0:T(8,128)(2,1)S(1)}, bf16[128,1152]{1,0:T(8,128)(2,1)S(1)}, u32[]{:S(2)}, u32[]{:S(2)}) collective-permute-start(bf16[128,1152]{1,0:T(8,128)(2,1)S(1)} %pad_maximum_fusion.2), channel_id=1, source_target_pairs={{0,1},{1,2},{2,3},{3,4},{4,5},{5,6},{6,7},{7,0},{8,9},{9,10},{10,1... | collective-permute-start | bytes 884744 | tf_op jit(solution)/shard_map/ppermute | solution.py:46
  33.6 4.0 %collective-permute-done.3 = bf16[192,1152]{1,0:T(8,128)(2,1)S(1)} collective-permute-done((bf16[192,1152]{1,0:T(8,128)(2,1)S(1)}, bf16[192,1152]{1,0:T(8,128)(2,1)S(1)}, u32[]{:S(2)}, u32[]{:S(2)}) %collective-permute-start.3) | collective-permute-done | bytes 442400 | tf_op jit(solution)/shard_map/ppermute | solution.py:46
  37.7 0.3 collective-permute-done.4
  38.0 0.0 collective-permute-done.5
  38.1 0.0 copy-start
  38.1 8.5 %collective-permute-start.6 = (bf16[704,1152]{1,0:T(8,128)(2,1)S(1)}, bf16[704,1152]{1,0:T(8,128)(2,1)S(1)}, u32[]{:S(2)}, u32[]{:S(2)}) collective-permute-start(bf16[704,1152]{1,0:T(8,128)(2,1)S(1)} %constant_dynamic-update-slice_fusion), channel_id=1, source_target_pairs={{0,16},{16,0},{1,17},{17,1},{2,18},{18,2},{3,19},{19,3},{4,20},{20... | collective-permute-start | bytes 4866056 | tf_op jit(solution)/shard_map/ppermute | solution.py:97
  46.6 0.1 pad_maximum_fusion
  46.6 3.7 %collective-permute-start.7 = (bf16[320,1152]{1,0:T(8,128)(2,1)S(1)}, bf16[320,1152]{1,0:T(8,128)(2,1)}, u32[]{:S(2)}, u32[]{:S(2)}) collective-permute-start(bf16[320,1152]{1,0:T(8,128)(2,1)S(1)} %pad_maximum_fusion), channel_id=1, source_target_pairs={{0,8},{1,9},{2,10},{3,11},{4,12},{5,13},{6,14},{7,15},{8,0},{9,1},... | collective-permute-start | bytes 2211848 | tf_op jit(solution)/shard_map/ppermute | solution.py:46
  50.4 9.8 %collective-permute-done.7 = bf16[320,1152]{1,0:T(8,128)(2,1)} collective-permute-done((bf16[320,1152]{1,0:T(8,128)(2,1)S(1)}, bf16[320,1152]{1,0:T(8,128)(2,1)}, u32[]{:S(2)}, u32[]{:S(2)}) %collective-permute-start.7) | collective-permute-done | bytes 737312 | tf_op jit(solution)/shard_map/ppermute | solution.py:46
  60.1 1.9 %collective-permute-start.8 = (bf16[320,1152]{1,0:T(8,128)(2,1)}, bf16[320,1152]{1,0:T(8,128)(2,1)}, u32[]{:S(2)}, u32[]{:S(2)}) collective-permute-start(bf16[320,1152]{1,0:T(8,128)(2,1)} %collective-permute-done.7), channel_id=1, source_target_pairs={{0,16},{16,0},{1,17},{17,1},{2,18},{18,2},{3,19},{19,3},{4,20},{20... | collective-permute-start | bytes 2211848 | tf_op jit(solution)/shard_map/ppermute | solution.py:98
  62.1 0.0 collective-permute-done.6
  62.1 3.9 %fusion.24 = f32[320,1152]{1,0:T(8,128)} fusion(bf16[704,1152]{1,0:T(8,128)(2,1)S(1)} %collective-permute-done.6, bf16[320,1152]{1,0:T(8,128)(2,1)} %collective-permute-done.7), kind=kOutput, calls=%fused_computation.32 | convolution fusion | flops 1039667200 | bytes 3833856 | tf_op jit(solution)/shard_map/dot_general | solution.py:70
  65.9 0.0 collective-permute-done.8
  65.9 4.1 %fusion = bf16[320,1152]{1,0:T(8,128)(2,1)} fusion(f32[320,1152]{1,0:T(8,128)} %fusion.24, bf16[320,1152]{1,0:T(8,128)(2,1)} %collective-permute-done.8, bf16[320,1152]{1,0:T(8,128)(2,1)} %collective-permute-done.7), kind=kOutput, calls=%fused_computation.2 | convolution fusion | flops 473313280 | bytes 3686400 | tf_op jit(solution)/shard_map/dot_general | solution.py:70
  70.0 3.7 %collective-permute-start.10 = (bf16[320,1152]{1,0:T(8,128)(2,1)}, bf16[320,1152]{1,0:T(8,128)(2,1)}, u32[]{:S(2)}, u32[]{:S(2)}) collective-permute-start(bf16[320,1152]{1,0:T(8,128)(2,1)} %fusion), channel_id=1, source_target_pairs={{0,8},{1,9},{2,10},{3,11},{4,12},{5,13},{6,14},{7,15},{8,0},{9,1},... | collective-permute-start | bytes 2211848 | tf_op jit(solution)/shard_map/ppermute | solution.py:46
  73.8 4.8 %fusion.25 = f32[704,1152]{1,0:T(8,128)} fusion(bf16[704,1152]{1,0:T(8,128)(2,1)S(1)} %collective-permute-done.6, bf16[704,1152]{1,0:T(8,128)(2,1)S(1)} %constant_dynamic-update-slice_fusion, pred[704]{0:T(1024)(128)(4,1)S(1)} %iota_compare_fusion.1), kind=kOutput, calls=%fused_computation.33 | convolution fusion | flops 2289250304 | bytes 6488768 | tf_op jit(solution)/shard_map/dot_general | solution.py:70
  78.6 4.9 %convolution_add_fusion = f32[704,1152]{1,0:T(8,128)S(1)} fusion(f32[704,1152]{1,0:T(8,128)} %fusion.25, bf16[320,1152]{1,0:T(8,128)(2,1)} %collective-permute-done.8, bf16[704,1152]{1,0:T(8,128)(2,1)} %copy-done), kind=kOutput, calls=%fused_computation | convolution fusion | flops 1040478208 | bytes 8847360 | tf_op jit(solution)/shard_map/dot_general | solution.py:70
  83.6 0.1 slice.91
  83.6 2.8 %collective-permute-start.9 = (bf16[192,1152]{1,0:T(8,128)(2,1)S(1)}, bf16[192,1152]{1,0:T(8,128)(2,1)S(1)}, u32[]{:S(2)}, u32[]{:S(2)}) collective-permute-start(bf16[192,1152]{1,0:T(8,128)(2,1)S(1)} %slice.91), channel_id=1, source_target_pairs={{0,8},{1,9},{2,10},{3,11},{4,12},{5,13},{6,14},{7,15},{8,0},{9,1},... | collective-permute-start | bytes 1327112 | tf_op jit(solution)/shard_map/ppermute | solution.py:46
  86.4 0.0 collective-permute-done.10
  86.4 1.3 %fusion.2 = bf16[320,1152]{1,0:T(8,128)(2,1)S(1)} fusion(f32[704,1152]{1,0:T(8,128)S(1)} %convolution_add_fusion, bf16[320,1152]{1,0:T(8,128)(2,1)} %collective-permute-done.10), kind=kLoop, calls=%fused_computation.7 | loop fusion | flops 1105920 | bytes 2949120 | tf_op jit(solution)/shard_map/convert_element_type | solution.py:106
  87.7 3.2 %collective-permute-start.11 = (bf16[192,1152]{1,0:T(8,128)(2,1)S(1)}, bf16[192,1152]{1,0:T(8,128)(2,1)S(1)}, u32[]{:S(2)}, u32[]{:S(2)}) collective-permute-start(bf16[192,1152]{1,0:T(8,128)(2,1)S(1)} %slice.54), channel_id=1, source_target_pairs={{0,1},{1,2},{2,3},{3,4},{4,5},{5,6},{6,7},{7,0},{8,9},{9,10},{10,1... | collective-permute-start | bytes 1327112 | tf_op jit(solution)/shard_map/ppermute | solution.py:46
  91.0 2.1 %collective-permute-start.12 = (bf16[128,1152]{1,0:T(8,128)(2,1)S(1)}, bf16[128,1152]{1,0:T(8,128)(2,1)S(1)}, u32[]{:S(2)}, u32[]{:S(2)}) collective-permute-start(bf16[128,1152]{1,0:T(8,128)(2,1)S(1)} %slice.56), channel_id=1, source_target_pairs={{0,7},{1,0},{2,1},{3,2},{4,3},{5,4},{6,5},{7,6},{8,15},{9,8},{10,9... | collective-permute-start | bytes 884744 | tf_op jit(solution)/shard_map/ppermute | solution.py:46
  93.1 1.1 collective-permute-done.9
  94.2 2.9 %collective-permute-done.11 = bf16[192,1152]{1,0:T(8,128)(2,1)S(1)} collective-permute-done((bf16[192,1152]{1,0:T(8,128)(2,1)S(1)}, bf16[192,1152]{1,0:T(8,128)(2,1)S(1)}, u32[]{:S(2)}, u32[]{:S(2)}) %collective-permute-start.11) | collective-permute-done | bytes 442400 | tf_op jit(solution)/shard_map/ppermute | solution.py:46
  97.1 0.2 fusion.26
  97.3 1.4 %collective-permute-done.12 = bf16[128,1152]{1,0:T(8,128)(2,1)S(1)} collective-permute-done((bf16[128,1152]{1,0:T(8,128)(2,1)S(1)}, bf16[128,1152]{1,0:T(8,128)(2,1)S(1)}, u32[]{:S(2)}, u32[]{:S(2)}) %collective-permute-start.12) | collective-permute-done | bytes 294944 | tf_op jit(solution)/shard_map/ppermute | solution.py:46
  98.6 0.1 slice_add_fusion.2
  98.7 6.3 %collective-permute-start.13 = (bf16[64,1152]{1,0:T(8,128)(2,1)S(1)}, bf16[64,1152]{1,0:T(8,128)(2,1)S(1)}, u32[]{:S(2)}, u32[]{:S(2)}) collective-permute-start(bf16[64,1152]{1,0:T(8,128)(2,1)S(1)} %slice.93), channel_id=1, source_target_pairs={{0,3},{1,4},{2,5},{3,6},{4,7},{5,0},{6,1},{7,2},{8,11},{9,12},{10,... | collective-permute-start | bytes 442376 | tf_op jit(solution)/shard_map/ppermute | solution.py:46
  105.1 2.0 %collective-permute-start.14 = (bf16[64,1152]{1,0:T(8,128)(2,1)S(1)}, bf16[64,1152]{1,0:T(8,128)(2,1)S(1)}, u32[]{:S(2)}, u32[]{:S(2)}) collective-permute-start(bf16[64,1152]{1,0:T(8,128)(2,1)S(1)} %slice.92), channel_id=1, source_target_pairs={{0,5},{1,6},{2,7},{3,0},{4,1},{5,2},{6,3},{7,4},{8,13},{9,14},{10,... | collective-permute-start | bytes 442376 | tf_op jit(solution)/shard_map/ppermute | solution.py:46
  107.0 3.8 %collective-permute-done.13 = bf16[64,1152]{1,0:T(8,128)(2,1)S(1)} collective-permute-done((bf16[64,1152]{1,0:T(8,128)(2,1)S(1)}, bf16[64,1152]{1,0:T(8,128)(2,1)S(1)}, u32[]{:S(2)}, u32[]{:S(2)}) %collective-permute-start.13) | collective-permute-done | bytes 147488 | tf_op jit(solution)/shard_map/ppermute | solution.py:46
  110.8 6.2 %collective-permute-done.14 = bf16[64,1152]{1,0:T(8,128)(2,1)S(1)} collective-permute-done((bf16[64,1152]{1,0:T(8,128)(2,1)S(1)}, bf16[64,1152]{1,0:T(8,128)(2,1)S(1)}, u32[]{:S(2)}, u32[]{:S(2)}) %collective-permute-start.14) | collective-permute-done | bytes 147488 | tf_op jit(solution)/shard_map/ppermute | solution.py:46
  117.1 0.2 fusion.36
  117.3 0.1 fusion.38
  117.4 1.9 %collective-permute-start.15 = (f32[32,1152]{1,0:T(8,128)S(1)}, f32[32,1152]{1,0:T(8,128)S(1)}, u32[]{:S(2)}, u32[]{:S(2)}) collective-permute-start(f32[32,1152]{1,0:T(8,128)S(1)} %slice_select_fusion), channel_id=1, source_target_pairs={{0,16},{16,0},{1,17},{17,1},{2,18},{18,2},{3,19},{19,3},{4,20},{20... | collective-permute-start | bytes 442376 | tf_op jit(solution)/shard_map/ppermute | solution.py:117
  119.4 1.3 %collective-permute-done.15 = f32[32,1152]{1,0:T(8,128)S(1)} collective-permute-done((f32[32,1152]{1,0:T(8,128)S(1)}, f32[32,1152]{1,0:T(8,128)S(1)}, u32[]{:S(2)}, u32[]{:S(2)}) %collective-permute-start.15) | collective-permute-done | bytes 147488 | tf_op jit(solution)/shard_map/ppermute | solution.py:117
  120.7 0.7 broadcast_select_fusion
  (15 shorter events, 0.3 us)
Async XLA Ops:
  1.6 3.5 %collective-permute-start = (bf16[32,1152]{1,0:T(8,128)(2,1)S(1)}, bf16[32,1152]{1,0:T(8,128)(2,1)S(1)}, u32[]{:S(2)}, u32[]{:S(2)}) collective-permute-start(bf16[32,1152]{1,0:T(8,128)(2,1)S(1)} %get-tuple-element.6), channel_id=1, source_target_pairs={{0,16},{16,0},{1,17},{17,1},{2,18},{18,2},{3,19},{19,3},{4,20},{20... | collective-permute-start | bytes 221192 | tf_op jit(solution)/shard_map/ppermute | solution.py:80
  5.3 11.7 %collective-permute-start.2 = (bf16[64,1152]{1,0:T(8,128)(2,1)S(1)}, bf16[64,1152]{1,0:T(8,128)(2,1)S(1)}, u32[]{:S(2)}, u32[]{:S(2)}) collective-permute-start(bf16[64,1152]{1,0:T(8,128)(2,1)S(1)} %get-tuple-element.3), channel_id=1, source_target_pairs={{0,3},{1,4},{2,5},{3,6},{4,7},{5,0},{6,1},{7,2},{8,11},{9,12},{10,... | collective-permute-start | bytes 442376 | tf_op jit(solution)/shard_map/ppermute | solution.py:46
  11.8 12.1 %collective-permute-start.1 = (bf16[64,1152]{1,0:T(8,128)(2,1)S(1)}, bf16[64,1152]{1,0:T(8,128)(2,1)S(1)}, u32[]{:S(2)}, u32[]{:S(2)}) collective-permute-start(bf16[64,1152]{1,0:T(8,128)(2,1)S(1)} %get-tuple-element.3), channel_id=1, source_target_pairs={{0,5},{1,6},{2,7},{3,0},{4,1},{5,2},{6,3},{7,4},{8,13},{9,14},{10,... | collective-permute-start | bytes 442376 | tf_op jit(solution)/shard_map/ppermute | solution.py:46
  23.9 14.2 %collective-permute-start.5 = (bf16[192,1152]{1,0:T(8,128)(2,1)S(1)}, bf16[192,1152]{1,0:T(8,128)(2,1)S(1)}, u32[]{:S(2)}, u32[]{:S(2)}) collective-permute-start(bf16[192,1152]{1,0:T(8,128)(2,1)S(1)} %pad_maximum_fusion.1), channel_id=1, source_target_pairs={{0,8},{1,9},{2,10},{3,11},{4,12},{5,13},{6,14},{7,15},{8,0},{9,1},... | collective-permute-start | bytes 1327112 | tf_op jit(solution)/shard_map/ppermute | solution.py:46
  28.3 9.3 %collective-permute-start.3 = (bf16[192,1152]{1,0:T(8,128)(2,1)S(1)}, bf16[192,1152]{1,0:T(8,128)(2,1)S(1)}, u32[]{:S(2)}, u32[]{:S(2)}) collective-permute-start(bf16[192,1152]{1,0:T(8,128)(2,1)S(1)} %pad_maximum_fusion.1), channel_id=1, source_target_pairs={{0,7},{1,0},{2,1},{3,2},{4,3},{5,4},{6,5},{7,6},{8,15},{9,8},{10,9... | collective-permute-start | bytes 1327112 | tf_op jit(solution)/shard_map/ppermute | solution.py:46
  30.2 7.8 %collective-permute-start.4 = (bf16[128,1152]{1,0:T(8,128)(2,1)S(1)}, bf16[128,1152]{1,0:T(8,128)(2,1)S(1)}, u32[]{:S(2)}, u32[]{:S(2)}) collective-permute-start(bf16[128,1152]{1,0:T(8,128)(2,1)S(1)} %pad_maximum_fusion.2), channel_id=1, source_target_pairs={{0,1},{1,2},{2,3},{3,4},{4,5},{5,6},{6,7},{7,0},{8,9},{9,10},{10,1... | collective-permute-start | bytes 884744 | tf_op jit(solution)/shard_map/ppermute | solution.py:46
  38.1 35.7 %copy-start = (bf16[704,1152]{1,0:T(8,128)(2,1)}, bf16[704,1152]{1,0:T(8,128)(2,1)S(1)}, u32[]{:S(2)}) copy-start(bf16[704,1152]{1,0:T(8,128)(2,1)S(1)} %constant_dynamic-update-slice_fusion) | copy-start | bytes 4866052
  38.1 24.0 %collective-permute-start.6 = (bf16[704,1152]{1,0:T(8,128)(2,1)S(1)}, bf16[704,1152]{1,0:T(8,128)(2,1)S(1)}, u32[]{:S(2)}, u32[]{:S(2)}) collective-permute-start(bf16[704,1152]{1,0:T(8,128)(2,1)S(1)} %constant_dynamic-update-slice_fusion), channel_id=1, source_target_pairs={{0,16},{16,0},{1,17},{17,1},{2,18},{18,2},{3,19},{19,3},{4,20},{20... | collective-permute-start | bytes 4866056 | tf_op jit(solution)/shard_map/ppermute | solution.py:97
  46.6 13.5 %collective-permute-start.7 = (bf16[320,1152]{1,0:T(8,128)(2,1)S(1)}, bf16[320,1152]{1,0:T(8,128)(2,1)}, u32[]{:S(2)}, u32[]{:S(2)}) collective-permute-start(bf16[320,1152]{1,0:T(8,128)(2,1)S(1)} %pad_maximum_fusion), channel_id=1, source_target_pairs={{0,8},{1,9},{2,10},{3,11},{4,12},{5,13},{6,14},{7,15},{8,0},{9,1},... | collective-permute-start | bytes 2211848 | tf_op jit(solution)/shard_map/ppermute | solution.py:46
  60.1 5.8 %collective-permute-start.8 = (bf16[320,1152]{1,0:T(8,128)(2,1)}, bf16[320,1152]{1,0:T(8,128)(2,1)}, u32[]{:S(2)}, u32[]{:S(2)}) collective-permute-start(bf16[320,1152]{1,0:T(8,128)(2,1)} %collective-permute-done.7), channel_id=1, source_target_pairs={{0,16},{16,0},{1,17},{17,1},{2,18},{18,2},{3,19},{19,3},{4,20},{20... | collective-permute-start | bytes 2211848 | tf_op jit(solution)/shard_map/ppermute | solution.py:98
  70.0 16.4 %collective-permute-start.10 = (bf16[320,1152]{1,0:T(8,128)(2,1)}, bf16[320,1152]{1,0:T(8,128)(2,1)}, u32[]{:S(2)}, u32[]{:S(2)}) collective-permute-start(bf16[320,1152]{1,0:T(8,128)(2,1)} %fusion), channel_id=1, source_target_pairs={{0,8},{1,9},{2,10},{3,11},{4,12},{5,13},{6,14},{7,15},{8,0},{9,1},... | collective-permute-start | bytes 2211848 | tf_op jit(solution)/shard_map/ppermute | solution.py:46
  83.6 10.6 %collective-permute-start.9 = (bf16[192,1152]{1,0:T(8,128)(2,1)S(1)}, bf16[192,1152]{1,0:T(8,128)(2,1)S(1)}, u32[]{:S(2)}, u32[]{:S(2)}) collective-permute-start(bf16[192,1152]{1,0:T(8,128)(2,1)S(1)} %slice.91), channel_id=1, source_target_pairs={{0,8},{1,9},{2,10},{3,11},{4,12},{5,13},{6,14},{7,15},{8,0},{9,1},... | collective-permute-start | bytes 1327112 | tf_op jit(solution)/shard_map/ppermute | solution.py:46
  87.7 9.3 %collective-permute-start.11 = (bf16[192,1152]{1,0:T(8,128)(2,1)S(1)}, bf16[192,1152]{1,0:T(8,128)(2,1)S(1)}, u32[]{:S(2)}, u32[]{:S(2)}) collective-permute-start(bf16[192,1152]{1,0:T(8,128)(2,1)S(1)} %slice.54), channel_id=1, source_target_pairs={{0,1},{1,2},{2,3},{3,4},{4,5},{5,6},{6,7},{7,0},{8,9},{9,10},{10,1... | collective-permute-start | bytes 1327112 | tf_op jit(solution)/shard_map/ppermute | solution.py:46
  91.0 7.6 %collective-permute-start.12 = (bf16[128,1152]{1,0:T(8,128)(2,1)S(1)}, bf16[128,1152]{1,0:T(8,128)(2,1)S(1)}, u32[]{:S(2)}, u32[]{:S(2)}) collective-permute-start(bf16[128,1152]{1,0:T(8,128)(2,1)S(1)} %slice.56), channel_id=1, source_target_pairs={{0,7},{1,0},{2,1},{3,2},{4,3},{5,4},{6,5},{7,6},{8,15},{9,8},{10,9... | collective-permute-start | bytes 884744 | tf_op jit(solution)/shard_map/ppermute | solution.py:46
  98.7 12.1 %collective-permute-start.13 = (bf16[64,1152]{1,0:T(8,128)(2,1)S(1)}, bf16[64,1152]{1,0:T(8,128)(2,1)S(1)}, u32[]{:S(2)}, u32[]{:S(2)}) collective-permute-start(bf16[64,1152]{1,0:T(8,128)(2,1)S(1)} %slice.93), channel_id=1, source_target_pairs={{0,3},{1,4},{2,5},{3,6},{4,7},{5,0},{6,1},{7,2},{8,11},{9,12},{10,... | collective-permute-start | bytes 442376 | tf_op jit(solution)/shard_map/ppermute | solution.py:46
  105.1 12.0 %collective-permute-start.14 = (bf16[64,1152]{1,0:T(8,128)(2,1)S(1)}, bf16[64,1152]{1,0:T(8,128)(2,1)S(1)}, u32[]{:S(2)}, u32[]{:S(2)}) collective-permute-start(bf16[64,1152]{1,0:T(8,128)(2,1)S(1)} %slice.92), channel_id=1, source_target_pairs={{0,5},{1,6},{2,7},{3,0},{4,1},{5,2},{6,3},{7,4},{8,13},{9,14},{10,... | collective-permute-start | bytes 442376 | tf_op jit(solution)/shard_map/ppermute | solution.py:46
  117.4 3.3 %collective-permute-start.15 = (f32[32,1152]{1,0:T(8,128)S(1)}, f32[32,1152]{1,0:T(8,128)S(1)}, u32[]{:S(2)}, u32[]{:S(2)}) collective-permute-start(f32[32,1152]{1,0:T(8,128)S(1)} %slice_select_fusion), channel_id=1, source_target_pairs={{0,16},{16,0},{1,17},{17,1},{2,18},{18,2},{3,19},{19,3},{4,20},{20... | collective-permute-start | bytes 442376 | tf_op jit(solution)/shard_map/ppermute | solution.py:117

commit v3 on v1

v3 whole, which is shorter than its diff:
```python
import jax
import jax.numpy as jnp
from jax import lax
from jax.experimental import pallas as pl
from jax.experimental.pallas import tpu as pltpu
from jax.sharding import Mesh, PartitionSpec as P

logit_scale = 30.0
logit_bias = -5.0
epsilon = 1e-06

AXES = ("xh", "y", "core", "xl", "z")
SIZES = (2, 8, 2, 2, 8)
ALL = P(AXES, None)
SWAP = [(0, 1), (1, 0)]
LINE = 8


def index_of(xh, y, core, xl, z):
    return (((xh * 8 + y) * 2 + core) * 2 + xl) * 8 + z


def line_groups():
    groups = []
    for xh in range(2):
        for xl in range(2):
            for at in range(8):
                groups.append([index_of(xh, at, 0, xl, z) for z in range(8)])
                groups.append([index_of(xh, y, 1, xl, at) for y in range(8)])
    return groups


def across_x():
    pairs = []
    for xh in range(2):
        for y in range(8):
            for core in range(2):
                for xl in range(2):
                    for z in range(8):
                        pairs.append(
                            (index_of(xh, y, core, xl, z), index_of(xh ^ core, y, core, 1 - xl, z))
                        )
    return pairs


def unit_rows(raw):
    wide = raw.astype(jnp.float32)
    inverse = lax.rsqrt(jnp.sum(wide * wide, axis=1, keepdims=True) + epsilon)
    return (wide * inverse, inverse)


def raw_grad(unit_sum, unit, inverse):
    along = jnp.sum(unit_sum * unit, axis=1, keepdims=True)
    return inverse * (unit_sum - along * unit)


def pull_kernel(labelled, added, *refs):
    refs = list(refs)
    at_ref = refs.pop(0) if labelled else None
    mine_ref, theirs_ref = refs[0], refs[1]
    out_ref = refs[-1]
    scores = lax.dot_general(
        mine_ref[...],
        theirs_ref[...],
        (((1,), (1,)), ((), ())),
        preferred_element_type=jnp.float32,
    )
    chance = 1.0 / (1.0 + jnp.exp(-logit_bias - logit_scale * scores))
    if labelled:
        block = scores.shape[0]
        row = lax.broadcasted_iota(jnp.int32, scores.shape, 0) + (
            pl.program_id(0) * block - at_ref[0]
        )
        column = lax.broadcasted_iota(jnp.int32, scores.shape, 1) - at_ref[1]
        same = (row == column) & (row >= 0) & (row < at_ref[2])
        chance = chance - same.astype(jnp.float32)
    coef = (logit_scale * chance).astype(jnp.bfloat16)
    terms = jnp.dot(coef, theirs_ref[...], preferred_element_type=jnp.float32)
    if added:
        terms = terms + refs[2][...]
    out_ref[...] = terms.astype(out_ref.dtype)


def pull(mine, theirs, at=None, so_far=None, dtype=jnp.float32, block=256):
    rows, width = mine.shape
    block_spec = pl.BlockSpec((block, width), lambda i: (i, 0))
    whole_spec = pl.BlockSpec(theirs.shape, lambda i: (0, 0))
    args, specs = [mine, theirs], [block_spec, whole_spec]
    if at is not None:
        args.insert(0, at)
        specs.insert(0, pl.BlockSpec(memory_space=pltpu.SMEM))
    if so_far is not None:
        args.append(so_far)
        specs.append(block_spec)

    def kernel(*refs):
        pull_kernel(at is not None, so_far is not None, *refs)

    pairs = rows * theirs.shape[0]
    return pl.pallas_call(
        kernel,
        out_shape=jax.ShapeDtypeStruct((rows, width), dtype),
        grid=(rows // block,),
        in_specs=specs,
        out_specs=block_spec,
        compiler_params=pltpu.CompilerParams(vmem_limit_bytes=32 * 2**20),
        cost_estimate=pl.CostEstimate(
            flops=4 * pairs * width, bytes_accessed=8 * rows * width, transcendentals=2 * pairs
        ),
    )(*args)


def local(images, texts):
    rows, width = images.shape
    line = LINE * rows
    f32, bf = jnp.float32, jnp.bfloat16
    core = lax.axis_index("core")
    first = core == 0
    y, z = lax.axis_index("y"), lax.axis_index("z")
    my_place, their_place = jnp.where(first, z, y), jnp.where(first, y, z)
    groups, partners = line_groups(), across_x()

    def trade(blocks):
        return lax.all_to_all(
            blocks, AXES, split_axis=0, concat_axis=0, axis_index_groups=groups, tiled=True
        )

    def copies(block):
        return jnp.broadcast_to(block[None], (LINE, *block.shape)).reshape(-1, width)

    def swap_x(block):
        return lax.ppermute(block, AXES, partners)

    def swap_core(block):
        return lax.ppermute(block, "core", SWAP)

    def line_sum(blocks, size):
        return jnp.sum(blocks.reshape(LINE, size, width).astype(f32), axis=0)

    unit_a, inverse_a = unit_rows(jnp.where(first, images, texts))
    rows_a = unit_a.astype(bf)
    line_a = trade(copies(rows_a))
    unit_b, inverse_b = unit_rows(swap_core(jnp.where(first, texts, images)))
    rows_b = unit_b.astype(bf)
    both_b = jnp.concatenate([rows_b, swap_x(rows_b)], 0)

    mine_b = trade(copies(both_b))
    mine_a = jnp.concatenate([line_a, swap_x(line_a)], 0)
    theirs_a = swap_core(mine_a)
    sum_a = pull(mine_a, theirs_a)

    at_ab = jnp.stack([my_place * rows, their_place * 2 * rows, rows]).astype(jnp.int32)
    at_ba = jnp.stack([my_place * 2 * rows, their_place * rows, rows]).astype(jnp.int32)
    theirs_b = swap_core(mine_b)
    sum_b = pull(mine_b, theirs_a, at=at_ba)
    sum_b = pull(mine_b, theirs_b, so_far=sum_b, dtype=bf)

    back_b = trade(sum_b)
    sum_a = pull(mine_a, theirs_b, at=at_ab, so_far=sum_a)
    back_x = swap_x(sum_a[line:].astype(bf))
    back_a = trade((sum_a[:line] + back_x.astype(f32)).astype(bf))

    total_b = line_sum(back_b, 2 * rows)
    total_b = total_b[:rows] + swap_x(total_b[rows:].astype(bf)).astype(f32)
    got = swap_core(raw_grad(total_b, unit_b, inverse_b))
    kept = raw_grad(line_sum(back_a, rows), unit_a, inverse_a)
    return (jnp.where(first, kept, got), jnp.where(first, got, kept))


def solution(mesh):
    fine = Mesh(mesh.devices.reshape(SIZES), AXES)
    return jax.shard_map(
        local, mesh=fine, in_specs=(ALL, ALL), out_specs=(ALL, ALL), check_vma=False
    )
```

time: 122 us -> 113 us (0.926)
  blocking collectives: 74.6 us -> 0 us
  starting transfers between devices: 20.4 us -> 54 us
  waiting for transfers between devices: 8.77 us -> 36.9 us
  Pallas kernels: 0 us -> 11.6 us
  matrix products: 8.2 us -> 0 us
  other arithmetic: 7.18 us -> 4.96 us
  local copies, waits for them, and re-layouts: 1.64 us -> 3.76 us
    all_to_all x2 -> x0, blocking collectives: 74.6 us -> none  [exchange(): lax.all_to_all(blocks, AXES, split_axis=0, concat_axis=0, axis_index_grou...]
    all_to_all x0 -> x4, starting transfers between devices: none -> 19.9 us  [trade(): lax.all_to_all(blocks, AXES, split_axis=0, concat_axis=0, axis_index_grou...]
    ppermute x6 -> x8, waiting for transfers between devices: 8.77 us -> 23.9 us  [the longest x4 23.9 us: swap_x(): return lax.ppermute(block, AXES, partners)]
    ppermute x6 -> x8, starting transfers between devices: 20.4 us -> 34 us  [the longest x4 20.6 us: swap_core(): return lax.ppermute(block, 'core', SWAP)]
    all_to_all x0 -> x4, waiting for transfers between devices: none -> 13 us  [trade(): lax.all_to_all(blocks, AXES, split_axis=0, concat_axis=0, axis_index_grou...]
    pallas_call x0 -> x4, Pallas kernels: none -> 11.6 us  [pull(): pl.pallas_call(kernel, out_shape=jax.ShapeDtypeStruct((rows, width), dtyp...]
    dot_general x3 -> x0, matrix products: 8.2 us -> none  [the longest x1 3.78 us: local(): scores = jnp.dot(img, txt.T, preferred_element_type=jnp.float32)]
    select_n x4 -> x1, other arithmetic: 3.75 us -> 0.91 us  [local(): unit_b, inverse_b = unit_rows(swap_core(jnp.where(first, texts, images)))]
  transfers between devices with their start and end apart: 6 -> 12, of which waited for: 6 -> 8; matrix products, arithmetic and copies ran while one was open for 0% -> 4% of each run, Pallas kernels for 0% -> 7%
where the time goes in v3:
time: 113 us; the launch traced here: 112 us
  starting transfers between devices  54 us (48%)
  waiting for transfers between devices  36.9 us (33%)
  Pallas kernels  11.6 us (10%)
  other arithmetic  4.96 us (4%)
  local copies, waits for them, and re-layouts  3.76 us (3%)
    ppermute x4, waiting for transfers between devices, swap_x(): return lax.ppermute(block, AXES, partners)  23.9 us
    ppermute x4, starting transfers between devices, swap_core(): return lax.ppermute(block, 'core', SWAP)  20.6 us
    all_to_all x4, starting transfers between devices, trade(): lax.all_to_all(blocks, AXES, split_axis=0, concat_axis=0, axis_index_grou...  19.9 us
    ppermute x4, starting transfers between devices, swap_x(): return lax.ppermute(block, AXES, partners)  13.4 us
    all_to_all x4, waiting for transfers between devices, trade(): lax.all_to_all(blocks, AXES, split_axis=0, concat_axis=0, axis_index_grou...  13 us
    pallas_call x4, Pallas kernels, pull(): pl.pallas_call(kernel, out_shape=jax.ShapeDtypeStruct((rows, width), dtyp...  11.6 us
  transfers between devices with their start and end apart: 12, of which 8 were waited for; matrix products, arithmetic and copies ran while one was open for 4% of the time, Pallas kernels for 7%

profile of v3, /device:TPU:1, one launch (start us, length us, event | category | flops | bytes accessed | tf_op | source)
XLA Modules:
  0.0 112.0 jit_solution(3193824164215416947)
XLA Ops:
  0.6 0.9 broadcast_select_fusion
  1.5 8.8 %collective-permute-start.1 = (bf16[32,1152]{1,0:T(8,128)(2,1)S(1)}, bf16[32,1152]{1,0:T(8,128)(2,1)S(1)}, u32[]{:S(2)}, u32[]{:S(2)}) collective-permute-start(bf16[32,1152]{1,0:T(8,128)(2,1)S(1)} %broadcast_select_fusion), channel_id=1, source_target_pairs={{0,16},{16,0},{1,17},{17,1},{2,18},{18,2},{3,19},{19,3},{4,20},{20... | collective-permute-start | bytes 221192 | tf_op jit(solution)/shard_map/ppermute | solution.py:135
  10.3 1.0 fusion.10
  11.4 0.6 copy-done.1
  12.0 0.1 fusion.6
  12.1 0.9 broadcast_in_dim.4
  13.0 3.5 %all-to-all-start = ((bf16[8,32,1152]{2,1,0:T(8,128)(2,1)}), bf16[8,32,1152]{2,1,0:T(8,128)(2,1)S(1)}, u32[]{:S(2)}, u32[]{:S(2)}) async-start(bf16[8,32,1152]{2,1,0:T(8,128)(2,1)} %broadcast_in_dim.4), calls=%async_computation | async-start | bytes 1179648 | tf_op jit(solution)/shard_map/all_to_all | solution.py:124
  16.5 0.0 copy-start.3
  16.5 0.1 fusion.14
  16.7 0.1 fusion.3
  16.8 2.3 %collective-permute-start.2 = (bf16[32,1152]{1,0:T(8,128)(2,1)S(1)}, bf16[32,1152]{1,0:T(8,128)(2,1)S(1)}, u32[]{:S(2)}, u32[]{:S(2)}) collective-permute-start(bf16[32,1152]{1,0:T(8,128)(2,1)S(1)} %fusion.3), channel_id=1, source_target_pairs={{0,8},{1,9},{2,10},{3,11},{4,12},{5,13},{6,14},{7,15},{8,0},{9,1},... | collective-permute-start | bytes 221192 | tf_op jit(solution)/shard_map/ppermute | solution.py:132
  19.0 4.2 %collective-permute-done.2 = bf16[32,1152]{1,0:T(8,128)(2,1)S(1)} collective-permute-done((bf16[32,1152]{1,0:T(8,128)(2,1)S(1)}, bf16[32,1152]{1,0:T(8,128)(2,1)S(1)}, u32[]{:S(2)}, u32[]{:S(2)}) %collective-permute-start.2) | collective-permute-done | bytes 73760 | tf_op jit(solution)/shard_map/ppermute | solution.py:132
  23.2 6.0 %all-to-all-done = bf16[8,32,1152]{2,1,0:T(8,128)(2,1)S(1)} async-done(((bf16[8,32,1152]{2,1,0:T(8,128)(2,1)}), bf16[8,32,1152]{2,1,0:T(8,128)(2,1)S(1)}, u32[]{:S(2)}, u32[]{:S(2)}) %all-to-all-start) | async-done | bytes 589856 | tf_op jit(solution)/shard_map/all_to_all | solution.py:124
  29.3 1.2 %broadcast_in_dim.5 = bf16[8,64,1152]{2,1,0:T(8,128)(2,1)} broadcast(bf16[64,1152]{1,0:T(8,128)(2,1)S(1)} %pad_maximum_fusion.1), dimensions={1,2} | broadcast | bytes 1327104 | tf_op jit(solution)/shard_map/broadcast_in_dim | solution.py:129
  30.4 3.6 %all-to-all-start.1 = ((bf16[8,64,1152]{2,1,0:T(8,128)(2,1)}), bf16[8,64,1152]{2,1,0:T(8,128)(2,1)S(1)}, u32[]{:S(2)}, u32[]{:S(2)}) async-start(bf16[8,64,1152]{2,1,0:T(8,128)(2,1)} %broadcast_in_dim.5), calls=%async_computation.1 | async-start | bytes 2359296 | tf_op jit(solution)/shard_map/all_to_all | solution.py:124
  34.0 2.4 %collective-permute-start = (bf16[256,1152]{1,0:T(8,128)(2,1)S(1)}, bf16[256,1152]{1,0:T(8,128)(2,1)S(1)}, u32[]{:S(2)}, u32[]{:S(2)}) collective-permute-start(bf16[256,1152]{1,0:T(8,128)(2,1)S(1)} %bitcast.12), channel_id=1, source_target_pairs={{0,8},{1,9},{2,10},{3,11},{4,12},{5,13},{6,14},{7,15},{8,0},{9,1},... | collective-permute-start | bytes 1769480 | tf_op jit(solution)/shard_map/ppermute | solution.py:132
  36.4 9.7 %collective-permute-done = bf16[256,1152]{1,0:T(8,128)(2,1)S(1)} collective-permute-done((bf16[256,1152]{1,0:T(8,128)(2,1)S(1)}, bf16[256,1152]{1,0:T(8,128)(2,1)S(1)}, u32[]{:S(2)}, u32[]{:S(2)}) %collective-permute-start) | collective-permute-done | bytes 589856 | tf_op jit(solution)/shard_map/ppermute | solution.py:132
  46.1 0.1 pad_maximum_fusion.refs_0_.refs_1_
  46.2 4.2 %collective-permute-start.4 = (bf16[512,1152]{1,0:T(8,128)(2,1)S(1)}, bf16[512,1152]{1,0:T(8,128)(2,1)S(1)}, u32[]{:S(2)}, u32[]{:S(2)}) collective-permute-start(bf16[512,1152]{1,0:T(8,128)(2,1)S(1)} %pad_maximum_fusion.refs_0_.refs_1_), channel_id=1, source_target_pairs={{0,16},{16,0},{1,17},{17,1},{2,18},{18,2},{3,19},{19,3},{4,20},{20... | collective-permute-start | bytes 3538952 | tf_op jit(solution)/shard_map/ppermute | solution.py:135
  50.4 2.7 %all-to-all-done.1 = bf16[8,64,1152]{2,1,0:T(8,128)(2,1)S(1)} async-done(((bf16[8,64,1152]{2,1,0:T(8,128)(2,1)}), bf16[8,64,1152]{2,1,0:T(8,128)(2,1)S(1)}, u32[]{:S(2)}, u32[]{:S(2)}) %all-to-all-start.1) | async-done | bytes 1179680 | tf_op jit(solution)/shard_map/all_to_all | solution.py:124
  53.1 5.7 %collective-permute-start.3 = (bf16[512,1152]{1,0:T(8,128)(2,1)S(1)}, bf16[512,1152]{1,0:T(8,128)(2,1)}, u32[]{:S(2)}, u32[]{:S(2)}) collective-permute-start(bf16[512,1152]{1,0:T(8,128)(2,1)S(1)} %bitcast.8), channel_id=1, source_target_pairs={{0,16},{16,0},{1,17},{17,1},{2,18},{18,2},{3,19},{19,3},{4,20},{20... | collective-permute-start | bytes 3538952 | tf_op jit(solution)/shard_map/ppermute | solution.py:135
  58.8 0.1 pad_add_fusion.refs_0_
  58.9 0.0 collective-permute-done.4.refs_1_.refs_2_
  58.9 2.7 %shard_map.43.refs_2_ = f32[512,1152]{1,0:T(8,128)S(1)} custom-call(s32[3]{0:T(128)S(1)} %pad_add_fusion.refs_0_, bf16[512,1152]{1,0:T(8,128)(2,1)S(1)} %bitcast.9, bf16[512,1152]{1,0:T(8,128)(2,1)S(1)} %collective-permute-done.4.refs_1_.refs_2_), custom_call_target="tpu_custom_call" | custom-call | flops 1207959552 | bytes 4718592 | tf_op jit(solution)/shard_map/pallas_call | solution.py:100
  61.6 0.0 collective-permute-done.3.refs_2_.refs_1_
  61.6 3.4 %shard_map.44 = bf16[512,1152]{1,0:T(8,128)(2,1)S(1)} custom-call(bf16[512,1152]{1,0:T(8,128)(2,1)S(1)} %bitcast.10, bf16[512,1152]{1,0:T(8,128)(2,1)} %collective-permute-done.3.refs_2_.refs_1_, f32[512,1152]{1,0:T(8,128)S(1)} %shard_map.43.refs_2_), custom_call_target="tpu_custom_call" | custom-call | flops 1207959552 | bytes 4718592 | tf_op jit(solution)/shard_map/pallas_call | solution.py:100
  65.0 1.0 copy-done
  66.0 6.8 %all-to-all-start.3 = ((bf16[8,64,1152]{2,1,0:T(8,128)(2,1)}), bf16[8,64,1152]{2,1,0:T(8,128)(2,1)S(1)}, u32[]{:S(2)}, u32[]{:S(2)}) async-start(bf16[8,64,1152]{2,1,0:T(8,128)(2,1)} %bitcast.11), calls=%async_computation.3 | async-start | bytes 2359296 | tf_op jit(solution)/shard_map/all_to_all | solution.py:124
  72.8 0.1 pad_add_fusion.1.refs_0_
  72.9 2.1 %shard_map.41.refs_3_ = f32[512,1152]{1,0:T(8,128)S(1)} custom-call(bf16[512,1152]{1,0:T(8,128)(2,1)S(1)} %pad_maximum_fusion.refs_0_.refs_1_, bf16[512,1152]{1,0:T(8,128)(2,1)S(1)} %collective-permute-done.4.refs_1_.refs_2_), custom_call_target="tpu_custom_call" | custom-call | flops 1207959552 | bytes 4718592 | tf_op jit(solution)/shard_map/pallas_call | solution.py:100
  75.0 3.4 %shard_map.42 = f32[512,1152]{1,0:T(8,128)S(1)} custom-call(s32[3]{0:T(128)S(1)} %pad_add_fusion.1.refs_0_, bf16[512,1152]{1,0:T(8,128)(2,1)S(1)} %pad_maximum_fusion.refs_0_.refs_1_, bf16[512,1152]{1,0:T(8,128)(2,1)} %collective-permute-done.3.refs_2_.refs_1_, f32[512,1152]{1,0:T(8,128)S(1)} %shard_map.41.refs_3_), custom_call_target="tpu_custom_call" | custom-call | flops 1207959552 | bytes 4718592 | tf_op jit(solution)/shard_map/pallas_call | solution.py:100
  78.5 0.1 slice.32
  78.5 4.4 %collective-permute-start.5 = (bf16[256,1152]{1,0:T(8,128)(2,1)S(1)}, bf16[256,1152]{1,0:T(8,128)(2,1)S(1)}, u32[]{:S(2)}, u32[]{:S(2)}) collective-permute-start(bf16[256,1152]{1,0:T(8,128)(2,1)S(1)} %slice.32), channel_id=1, source_target_pairs={{0,8},{1,9},{2,10},{3,11},{4,12},{5,13},{6,14},{7,15},{8,0},{9,1},... | collective-permute-start | bytes 1769480 | tf_op jit(solution)/shard_map/ppermute | solution.py:132
  82.9 7.7 %collective-permute-done.5 = bf16[256,1152]{1,0:T(8,128)(2,1)S(1)} collective-permute-done((bf16[256,1152]{1,0:T(8,128)(2,1)S(1)}, bf16[256,1152]{1,0:T(8,128)(2,1)S(1)}, u32[]{:S(2)}, u32[]{:S(2)}) %collective-permute-start.5) | collective-permute-done | bytes 589856 | tf_op jit(solution)/shard_map/ppermute | solution.py:132
  90.7 0.9 fusion
  91.6 0.5 all-to-all-done.3
  92.1 6.0 %all-to-all-start.2 = ((bf16[8,32,1152]{2,1,0:T(8,128)(2,1)}), bf16[8,32,1152]{2,1,0:T(8,128)(2,1)S(1)}, u32[]{:S(2)}, u32[]{:S(2)}) async-start(bf16[8,32,1152]{2,1,0:T(8,128)(2,1)} %bitcast.4), calls=%async_computation.2 | async-start | bytes 1179648 | tf_op jit(solution)/shard_map/all_to_all | solution.py:124
  98.1 0.2 convert_reduce_fusion
  98.2 0.0 copy-start.2
  98.3 4.4 %collective-permute-start.6 = (bf16[32,1152]{1,0:T(8,128)(2,1)S(1)}, bf16[32,1152]{1,0:T(8,128)(2,1)S(1)}, u32[]{:S(2)}, u32[]{:S(2)}) collective-permute-start(bf16[32,1152]{1,0:T(8,128)(2,1)S(1)} %slice.33), channel_id=1, source_target_pairs={{0,8},{1,9},{2,10},{3,11},{4,12},{5,13},{6,14},{7,15},{8,0},{9,1},... | collective-permute-start | bytes 221192 | tf_op jit(solution)/shard_map/ppermute | solution.py:132
  102.7 2.2 %collective-permute-done.6 = bf16[32,1152]{1,0:T(8,128)(2,1)S(1)} collective-permute-done((bf16[32,1152]{1,0:T(8,128)(2,1)S(1)}, bf16[32,1152]{1,0:T(8,128)(2,1)S(1)}, u32[]{:S(2)}, u32[]{:S(2)}) %collective-permute-start.6) | collective-permute-done | bytes 73760 | tf_op jit(solution)/shard_map/ppermute | solution.py:132
  104.9 0.2 fusion.11
  105.1 0.1 fusion.13
  105.2 1.9 %collective-permute-start.7 = (f32[32,1152]{1,0:T(8,128)S(1)}, f32[32,1152]{1,0:T(8,128)S(1)}, u32[]{:S(2)}, u32[]{:S(2)}) collective-permute-start(f32[32,1152]{1,0:T(8,128)S(1)} %fusion.13), channel_id=1, source_target_pairs={{0,16},{16,0},{1,17},{17,1},{2,18},{18,2},{3,19},{19,3},{4,20},{20... | collective-permute-start | bytes 442376 | tf_op jit(solution)/shard_map/ppermute | solution.py:135
  107.1 3.8 %all-to-all-done.2 = bf16[8,32,1152]{2,1,0:T(8,128)(2,1)S(1)} async-done(((bf16[8,32,1152]{2,1,0:T(8,128)(2,1)}), bf16[8,32,1152]{2,1,0:T(8,128)(2,1)S(1)}, u32[]{:S(2)}, u32[]{:S(2)}) %all-to-all-start.2) | async-done | bytes 589856 | tf_op jit(solution)/shard_map/all_to_all | solution.py:124
  110.9 0.1 convert_reduce_fusion.1
  111.0 0.2 fusion.7
  111.2 0.8 fusion.15
  (12 shorter events, 0.1 us)
Async XLA Ops:
  1.5 15.0 %collective-permute-start.1 = (bf16[32,1152]{1,0:T(8,128)(2,1)S(1)}, bf16[32,1152]{1,0:T(8,128)(2,1)S(1)}, u32[]{:S(2)}, u32[]{:S(2)}) collective-permute-start(bf16[32,1152]{1,0:T(8,128)(2,1)S(1)} %broadcast_select_fusion), channel_id=1, source_target_pairs={{0,16},{16,0},{1,17},{17,1},{2,18},{18,2},{3,19},{19,3},{4,20},{20... | collective-permute-start | bytes 221192 | tf_op jit(solution)/shard_map/ppermute | solution.py:135
  11.4 0.6 copy-start.1
  13.0 16.3 %all-to-all-start = ((bf16[8,32,1152]{2,1,0:T(8,128)(2,1)}), bf16[8,32,1152]{2,1,0:T(8,128)(2,1)S(1)}, u32[]{:S(2)}, u32[]{:S(2)}) async-start(bf16[8,32,1152]{2,1,0:T(8,128)(2,1)} %broadcast_in_dim.4), calls=%async_computation | async-start | bytes 1179648 | tf_op jit(solution)/shard_map/all_to_all | solution.py:124
  16.5 13.9 %copy-start.3 = (bf16[32,1152]{1,0:T(8,128)(2,1)}, bf16[32,1152]{1,0:T(8,128)(2,1)S(1)}, u32[]{:S(2)}) copy-start(bf16[32,1152]{1,0:T(8,128)(2,1)S(1)} %collective-permute-done.1) | copy-start | bytes 221188
  16.8 6.4 %collective-permute-start.2 = (bf16[32,1152]{1,0:T(8,128)(2,1)S(1)}, bf16[32,1152]{1,0:T(8,128)(2,1)S(1)}, u32[]{:S(2)}, u32[]{:S(2)}) collective-permute-start(bf16[32,1152]{1,0:T(8,128)(2,1)S(1)} %fusion.3), channel_id=1, source_target_pairs={{0,8},{1,9},{2,10},{3,11},{4,12},{5,13},{6,14},{7,15},{8,0},{9,1},... | collective-permute-start | bytes 221192 | tf_op jit(solution)/shard_map/ppermute | solution.py:132
  30.4 22.7 %all-to-all-start.1 = ((bf16[8,64,1152]{2,1,0:T(8,128)(2,1)}), bf16[8,64,1152]{2,1,0:T(8,128)(2,1)S(1)}, u32[]{:S(2)}, u32[]{:S(2)}) async-start(bf16[8,64,1152]{2,1,0:T(8,128)(2,1)} %broadcast_in_dim.5), calls=%async_computation.1 | async-start | bytes 2359296 | tf_op jit(solution)/shard_map/all_to_all | solution.py:124
  34.0 12.1 %collective-permute-start = (bf16[256,1152]{1,0:T(8,128)(2,1)S(1)}, bf16[256,1152]{1,0:T(8,128)(2,1)S(1)}, u32[]{:S(2)}, u32[]{:S(2)}) collective-permute-start(bf16[256,1152]{1,0:T(8,128)(2,1)S(1)} %bitcast.12), channel_id=1, source_target_pairs={{0,8},{1,9},{2,10},{3,11},{4,12},{5,13},{6,14},{7,15},{8,0},{9,1},... | collective-permute-start | bytes 1769480 | tf_op jit(solution)/shard_map/ppermute | solution.py:132
  46.2 12.7 %collective-permute-start.4 = (bf16[512,1152]{1,0:T(8,128)(2,1)S(1)}, bf16[512,1152]{1,0:T(8,128)(2,1)S(1)}, u32[]{:S(2)}, u32[]{:S(2)}) collective-permute-start(bf16[512,1152]{1,0:T(8,128)(2,1)S(1)} %pad_maximum_fusion.refs_0_.refs_1_), channel_id=1, source_target_pairs={{0,16},{16,0},{1,17},{17,1},{2,18},{18,2},{3,19},{19,3},{4,20},{20... | collective-permute-start | bytes 3538952 | tf_op jit(solution)/shard_map/ppermute | solution.py:135
  53.1 8.5 %collective-permute-start.3 = (bf16[512,1152]{1,0:T(8,128)(2,1)S(1)}, bf16[512,1152]{1,0:T(8,128)(2,1)}, u32[]{:S(2)}, u32[]{:S(2)}) collective-permute-start(bf16[512,1152]{1,0:T(8,128)(2,1)S(1)} %bitcast.8), channel_id=1, source_target_pairs={{0,16},{16,0},{1,17},{17,1},{2,18},{18,2},{3,19},{19,3},{4,20},{20... | collective-permute-start | bytes 3538952 | tf_op jit(solution)/shard_map/ppermute | solution.py:135
  65.0 1.0 copy-start
  66.0 26.0 %all-to-all-start.3 = ((bf16[8,64,1152]{2,1,0:T(8,128)(2,1)}), bf16[8,64,1152]{2,1,0:T(8,128)(2,1)S(1)}, u32[]{:S(2)}, u32[]{:S(2)}) async-start(bf16[8,64,1152]{2,1,0:T(8,128)(2,1)} %bitcast.11), calls=%async_computation.3 | async-start | bytes 2359296 | tf_op jit(solution)/shard_map/all_to_all | solution.py:124
  78.5 12.1 %collective-permute-start.5 = (bf16[256,1152]{1,0:T(8,128)(2,1)S(1)}, bf16[256,1152]{1,0:T(8,128)(2,1)S(1)}, u32[]{:S(2)}, u32[]{:S(2)}) collective-permute-start(bf16[256,1152]{1,0:T(8,128)(2,1)S(1)} %slice.32), channel_id=1, source_target_pairs={{0,8},{1,9},{2,10},{3,11},{4,12},{5,13},{6,14},{7,15},{8,0},{9,1},... | collective-permute-start | bytes 1769480 | tf_op jit(solution)/shard_map/ppermute | solution.py:132
  92.1 12.8 %copy-start.4 = (bf16[32,1152]{1,0:T(8,128)(2,1)S(1)}, bf16[32,1152]{1,0:T(8,128)(2,1)}, u32[]{:S(2)}) copy-start(bf16[32,1152]{1,0:T(8,128)(2,1)} %copy-done.3) | copy-start | bytes 221188
  92.1 18.9 %all-to-all-start.2 = ((bf16[8,32,1152]{2,1,0:T(8,128)(2,1)}), bf16[8,32,1152]{2,1,0:T(8,128)(2,1)S(1)}, u32[]{:S(2)}, u32[]{:S(2)}) async-start(bf16[8,32,1152]{2,1,0:T(8,128)(2,1)} %bitcast.4), calls=%async_computation.2 | async-start | bytes 1179648 | tf_op jit(solution)/shard_map/all_to_all | solution.py:124
  98.2 12.8 %copy-start.2 = (bf16[32,1152]{1,0:T(8,128)(2,1)S(1)}, bf16[32,1152]{1,0:T(8,128)(2,1)}, u32[]{:S(2)}) copy-start(bf16[32,1152]{1,0:T(8,128)(2,1)} %copy-done.1) | copy-start | bytes 221188
  98.3 6.6 %collective-permute-start.6 = (bf16[32,1152]{1,0:T(8,128)(2,1)S(1)}, bf16[32,1152]{1,0:T(8,128)(2,1)S(1)}, u32[]{:S(2)}, u32[]{:S(2)}) collective-permute-start(bf16[32,1152]{1,0:T(8,128)(2,1)S(1)} %slice.33), channel_id=1, source_target_pairs={{0,8},{1,9},{2,10},{3,11},{4,12},{5,13},{6,14},{7,15},{8,0},{9,1},... | collective-permute-start | bytes 221192 | tf_op jit(solution)/shard_map/ppermute | solution.py:132
  105.2 6.0 %collective-permute-start.7 = (f32[32,1152]{1,0:T(8,128)S(1)}, f32[32,1152]{1,0:T(8,128)S(1)}, u32[]{:S(2)}, u32[]{:S(2)}) collective-permute-start(f32[32,1152]{1,0:T(8,128)S(1)} %fusion.13), channel_id=1, source_target_pairs={{0,16},{16,0},{1,17},{17,1},{2,18},{18,2},{3,19},{19,3},{4,20},{20... | collective-permute-start | bytes 442376 | tf_op jit(solution)/shard_map/ppermute | solution.py:135

commit v4 on v3

v4 whole, which is shorter than its diff:
```python
import functools

import jax
import jax.numpy as jnp
from jax import lax
from jax.experimental import pallas as pl
from jax.experimental.pallas import tpu as pltpu
from jax.sharding import Mesh, PartitionSpec as P

logit_scale = 30.0
logit_bias = -5.0
epsilon = 1e-06

AXES = ("xh", "y", "core", "xl", "z")
SIZES = (2, 8, 2, 2, 8)
ALL = P(AXES, None)
SWAP = [(0, 1), (1, 0)]
LINE = 8

IN_VMEM = pl.BlockSpec(memory_space=pltpu.VMEM)
IN_HBM = pl.BlockSpec(memory_space=pltpu.HBM)
IN_SMEM = pl.BlockSpec(memory_space=pltpu.SMEM)
PARAMS = pltpu.CompilerParams(vmem_limit_bytes=16 * 2**20)


def index_of(xh, y, core, xl, z):
    return (((xh * 8 + y) * 2 + core) * 2 + xl) * 8 + z


def line_groups():
    groups = []
    for xh in range(2):
        for xl in range(2):
            for at in range(8):
                groups.append([index_of(xh, at, 0, xl, z) for z in range(8)])
                groups.append([index_of(xh, y, 1, xl, at) for y in range(8)])
    return groups


def across_x(role, core_to):
    pairs = []
    for xh in range(2):
        for y in range(8):
            for core in range(2):
                for xl in range(2):
                    for z in range(8):
                        to = (xh ^ role(core), y, core_to(core), 1 - xl, z)
                        pairs.append((index_of(xh, y, core, xl, z), index_of(*to)))
    return pairs


def unit_rows(raw):
    wide = raw.astype(jnp.float32)
    inverse = lax.rsqrt(jnp.sum(wide * wide, axis=1, keepdims=True) + epsilon)
    return (wide * inverse, inverse)


def raw_grad(unit_sum, raw):
    unit, inverse = unit_rows(raw)
    along = jnp.sum(unit_sum * unit, axis=1, keepdims=True)
    return inverse * (unit_sum - along * unit)


def fill(sources, out_ref, sems):
    copies, at = [], 0
    for _ in range(LINE):
        for source in sources:
            target = out_ref.at[pl.ds(at, source.shape[0])]
            copies.append(pltpu.make_async_copy(source, target, sems.at[len(copies)]))
            at += source.shape[0]
    for copy in copies:
        copy.start()
    for copy in copies:
        copy.wait()


def open_kernel(
    core_ref, images_hbm, texts_hbm, copies_ref, other_ref, images_ref, texts_ref, unit_ref, sems
):
    first = core_ref[0] == 0
    loads = [
        pltpu.make_async_copy(images_hbm, images_ref, sems.at[0]),
        pltpu.make_async_copy(texts_hbm, texts_ref, sems.at[1]),
    ]
    for load in loads:
        load.start()
    for load in loads:
        load.wait()
    img = unit_rows(images_ref[...])[0].astype(jnp.bfloat16)
    txt = unit_rows(texts_ref[...])[0].astype(jnp.bfloat16)
    unit_ref[...] = jnp.where(first, img, txt)
    other_ref[...] = jnp.where(first, txt, img)
    fill([unit_ref], copies_ref, sems)


def open_rows(core, images, texts):
    rows, width = images.shape
    return pl.pallas_call(
        open_kernel,
        out_shape=(
            jax.ShapeDtypeStruct((LINE * rows, width), jnp.bfloat16),
            jax.ShapeDtypeStruct((rows, width), jnp.bfloat16),
        ),
        in_specs=[IN_SMEM, IN_HBM, IN_HBM],
        out_specs=(IN_HBM, IN_VMEM),
        scratch_shapes=[pltpu.VMEM((rows, width), jnp.bfloat16)] * 3
        + [pltpu.SemaphoreType.DMA((LINE,))],
        compiler_params=PARAMS,
    )(core, images, texts)


def copies_kernel(one_ref, two_ref, out_ref, sems):
    fill([one_ref, two_ref], out_ref, sems)


def copies(one, two):
    rows, width = one.shape
    return pl.pallas_call(
        copies_kernel,
        out_shape=jax.ShapeDtypeStruct((2 * LINE * rows, width), one.dtype),
        in_specs=[IN_VMEM, IN_VMEM],
        out_specs=IN_HBM,
        scratch_shapes=[pltpu.SemaphoreType.DMA((2 * LINE,))],
        compiler_params=PARAMS,
    )(one, two)


def pull_kernel(parts, labelled, added, *refs):
    refs = list(refs)
    at_ref = refs.pop(0) if labelled else None
    mine_ref = refs.pop(0)
    terms = None
    for part in range(parts):
        theirs_ref = refs.pop(0)
        scores = lax.dot_general(
            mine_ref[...],
            theirs_ref[...],
            (((1,), (1,)), ((), ())),
            preferred_element_type=jnp.float32,
        )
        chance = 1.0 / (1.0 + jnp.exp(-logit_bias - logit_scale * scores))
        if labelled and part == parts - 1:
            row = lax.broadcasted_iota(jnp.int32, scores.shape, 0) - at_ref[0]
            column = lax.broadcasted_iota(jnp.int32, scores.shape, 1) - at_ref[1]
            same = (row == column) & (row >= 0) & (row < at_ref[2])
            chance = jnp.where(same, chance - 1.0, chance)
        coef = (logit_scale * chance).astype(jnp.bfloat16)
        if part < parts - 1:
            new = jnp.dot(coef, theirs_ref[...], preferred_element_type=jnp.float32)
            terms = new if terms is None else terms + new
    so_far_ref = refs.pop(0) if added else None
    out_ref = refs.pop(0)
    stores = []
    blocks = 2 if refs else 1
    size = mine_ref.shape[0] // blocks
    for block in range(blocks):
        rows = slice(block * size, (block + 1) * size)
        total = jnp.dot(coef[rows], theirs_ref[...], preferred_element_type=jnp.float32)
        if terms is not None:
            total = total + terms[rows]
        if added:
            total = total + so_far_ref[rows].astype(jnp.float32)
        if not refs:
            out_ref[rows] = total.astype(out_ref.dtype)
            continue
        stage_ref, sems = refs
        stage_ref[rows] = total.astype(stage_ref.dtype)
        stores.append(pltpu.make_async_copy(stage_ref.at[rows], out_ref.at[rows], sems.at[block]))
        stores[-1].start()
    for store in stores:
        store.wait()


def pull(mine, theirs, at=None, so_far=None, dtype=jnp.float32, to_hbm=False):
    rows, width = mine.shape
    args = [mine, *theirs]
    specs = [IN_VMEM] * len(args)
    if at is not None:
        args.insert(0, at)
        specs.insert(0, IN_SMEM)
    if so_far is not None:
        args.append(so_far)
        specs.append(IN_VMEM)
    pairs = rows * sum(part.shape[0] for part in theirs)
    return pl.pallas_call(
        functools.partial(pull_kernel, len(theirs), at is not None, so_far is not None),
        out_shape=jax.ShapeDtypeStruct((rows, width), dtype),
        in_specs=specs,
        out_specs=IN_HBM if to_hbm else IN_VMEM,
        scratch_shapes=[pltpu.VMEM((rows, width), dtype), pltpu.SemaphoreType.DMA((2,))]
        if to_hbm
        else [],
        compiler_params=PARAMS,
        cost_estimate=pl.CostEstimate(
            flops=4 * pairs * width, bytes_accessed=8 * rows * width, transcendentals=2 * pairs
        ),
    )(*args)


def add_kernel(one_ref, two_ref, out_ref, stage_ref, sem):
    stage_ref[...] = (one_ref[...] + two_ref[...].astype(jnp.float32)).astype(jnp.bfloat16)
    copy = pltpu.make_async_copy(stage_ref, out_ref, sem)
    copy.start()
    copy.wait()


def add_rows(one, two):
    return pl.pallas_call(
        add_kernel,
        out_shape=jax.ShapeDtypeStruct(one.shape, jnp.bfloat16),
        in_specs=[IN_VMEM, IN_VMEM],
        out_specs=IN_HBM,
        scratch_shapes=[pltpu.VMEM(one.shape, jnp.bfloat16), pltpu.SemaphoreType.DMA(())],
        compiler_params=PARAMS,
    )(one, two)


def line_sum(back_ref, start, rows, step):
    total = back_ref[start : start + rows].astype(jnp.float32)
    for place in range(1, LINE):
        at = place * step + start
        total = total + back_ref[at : at + rows].astype(jnp.float32)
    return total


def sum_kernel(back_ref, near_ref, far_ref):
    rows = near_ref.shape[0]
    near_ref[...] = line_sum(back_ref, 0, rows, 2 * rows)
    far_ref[...] = line_sum(back_ref, rows, rows, 2 * rows).astype(far_ref.dtype)


def sum_rows(back):
    shape = (back.shape[0] // (2 * LINE), back.shape[1])
    return pl.pallas_call(
        sum_kernel,
        out_shape=(
            jax.ShapeDtypeStruct(shape, jnp.float32),
            jax.ShapeDtypeStruct(shape, jnp.bfloat16),
        ),
        in_specs=[IN_VMEM],
        out_specs=(IN_VMEM, IN_VMEM),
        compiler_params=PARAMS,
    )(back)


def close_kernel(core_ref, back_ref, near_ref, far_ref, images_ref, texts_ref, img_ref, txt_ref):
    first = core_ref[0] == 0
    rows = near_ref.shape[0]
    kept = line_sum(back_ref, 0, rows, rows)
    got = near_ref[...] + far_ref[...].astype(jnp.float32)
    img_ref[...] = raw_grad(jnp.where(first, kept, got), images_ref[...])
    txt_ref[...] = raw_grad(jnp.where(first, got, kept), texts_ref[...])


def close_rows(core, back, near, far, images, texts):
    shape = jax.ShapeDtypeStruct(near.shape, jnp.float32)
    return pl.pallas_call(
        close_kernel,
        out_shape=(shape, shape),
        in_specs=[IN_SMEM] + [IN_VMEM] * 5,
        out_specs=(IN_VMEM, IN_VMEM),
        compiler_params=PARAMS,
    )(core, back, near, far, images, texts)


def in_hbm(array):
    return pltpu.with_memory_space_constraint(array, pltpu.HBM)


def in_vmem(array):
    return pltpu.with_memory_space_constraint(array, pltpu.VMEM)


def local(images, texts):
    rows = images.shape[0]
    bf = jnp.bfloat16
    core = lax.axis_index("core")
    first = core == 0
    y, z = lax.axis_index("y"), lax.axis_index("z")
    my_place, their_place = jnp.where(first, z, y), jnp.where(first, y, z)
    groups = line_groups()
    same_core = across_x(lambda at: at, lambda at: at)
    to_gather = across_x(lambda at: 1 - at, lambda at: 1 - at)
    to_owner = across_x(lambda at: at, lambda at: 1 - at)
    core = core.astype(jnp.int32).reshape(1)

    def trade(blocks):
        return lax.all_to_all(
            blocks, AXES, split_axis=0, concat_axis=0, axis_index_groups=groups, tiled=True
        )

    def send_x(block, pairs):
        return lax.ppermute(block, AXES, pairs)

    def swap_core(block):
        return lax.ppermute(block, "core", SWAP)

    copies_a, other = open_rows(core, in_hbm(images), in_hbm(texts))
    near_a = trade(copies_a)
    from_x = send_x(other, to_gather)
    mine_b = trade(copies(swap_core(other), from_x))
    far_a = send_x(near_a, same_core)
    theirs_a = swap_core(jnp.concatenate([near_a, far_a], 0))

    at_ab = jnp.stack([my_place * rows, their_place * 2 * rows, rows]).astype(jnp.int32)
    at_ba = jnp.stack([my_place * 2 * rows, their_place * rows, rows]).astype(jnp.int32)
    theirs_b = in_vmem(swap_core(mine_b))
    sum_b = pull(mine_b, [theirs_a], at=at_ba, dtype=bf)
    back_b = trade(pull(mine_b, [theirs_b], so_far=sum_b, dtype=bf, to_hbm=True))

    back_x = send_x(pull(in_hbm(far_a), [theirs_a, theirs_b], dtype=bf, to_hbm=True), same_core)
    sum_a = pull(in_hbm(near_a), [theirs_a, theirs_b], at=at_ab)
    back_a = trade(add_rows(sum_a, back_x))

    near, far = sum_rows(back_b)
    far = send_x(far, to_owner)
    return close_rows(core, back_a, swap_core(near), far, images, texts)


def solution(mesh):
    fine = Mesh(mesh.devices.reshape(SIZES), AXES)
    return jax.shard_map(
        local, mesh=fine, in_specs=(ALL, ALL), out_specs=(ALL, ALL), check_vma=False
    )
```

time: 113 us -> 104 us (0.920)
  the two profiles are of different devices: /device:TPU:1 before, /device:TPU:6 now
where the time goes in v4:
time: 104 us; the launch traced here: 103 us
  starting transfers between devices  41.3 us (40%)
  waiting for transfers between devices  41.1 us (40%)
  Pallas kernels  16.6 us (16%)
  other arithmetic  1.35 us (1%)
  local copies, waits for them, and re-layouts  1.29 us (1%)
    all_to_all x4, starting transfers between devices, trade(): lax.all_to_all(blocks, AXES, split_axis=0, concat_axis=0, axis_index_grou...  23.1 us
    all_to_all x4, waiting for transfers between devices, trade(): lax.all_to_all(blocks, AXES, split_axis=0, concat_axis=0, axis_index_grou...  22.8 us
    ppermute x4, waiting for transfers between devices, send_x(): return lax.ppermute(block, AXES, pairs)  18 us
    pallas_call x4, Pallas kernels, pull(): pl.pallas_call(functools.partial(pull_kernel, len(theirs), at is not None...  11.4 us
    ppermute x4, starting transfers between devices, swap_core(): return lax.ppermute(block, 'core', SWAP)  9.15 us
    ppermute x4, starting transfers between devices, send_x(): return lax.ppermute(block, AXES, pairs)  9.07 us
  transfers between devices with their start and end apart: 12, of which 8 were waited for; matrix products, arithmetic and copies ran while one was open for 1% of the time, Pallas kernels for 11%

profile of v4, /device:TPU:6, one launch (start us, length us, event | category | flops | bytes accessed | tf_op | source)
XLA Modules:
  0.0 102.5 jit_solution(2126886490488243596)
XLA Ops:
  0.6 1.9 %shard_map.41 = (bf16[256,1152]{1,0:T(8,128)(2,1)}, bf16[32,1152]{1,0:T(8,128)(2,1)S(1)}) custom-call(s32[1]{0:T(128)} %bitcast.core_ref, bf16[32,1152]{1,0:T(8,128)(2,1)} %images_ref.1, bf16[32,1152]{1,0:T(8,128)(2,1)} %texts_ref.1), custom_call_target="tpu_custom_call" | custom-call | tf_op jit(solution)/shard_map/pallas_call | solution.py:98
  2.6 10.3 %all-to-all-start = ((bf16[8,32,1152]{2,1,0:T(8,128)(2,1)}), bf16[8,32,1152]{2,1,0:T(8,128)(2,1)S(1)}, u32[]{:S(2)}, u32[]{:S(2)}) async-start(bf16[8,32,1152]{2,1,0:T(8,128)(2,1)} %bitcast.3), calls=%async_computation | async-start | bytes 1179648 | tf_op jit(solution)/shard_map/all_to_all | solution.py:288
  12.9 1.9 %collective-permute-start.2 = (bf16[32,1152]{1,0:T(8,128)(2,1)S(1)}, bf16[32,1152]{1,0:T(8,128)(2,1)S(1)}, u32[]{:S(2)}, u32[]{:S(2)}) collective-permute-start(bf16[32,1152]{1,0:T(8,128)(2,1)S(1)} %get-tuple-element.7), channel_id=1, source_target_pairs={{0,16},{16,0},{1,17},{17,1},{2,18},{18,2},{3,19},{19,3},{4,20},{20... | collective-permute-start | bytes 221192 | tf_op jit(solution)/shard_map/ppermute | solution.py:296
  14.8 2.5 %collective-permute-start.3 = (bf16[32,1152]{1,0:T(8,128)(2,1)S(1)}, bf16[32,1152]{1,0:T(8,128)(2,1)S(1)}, u32[]{:S(2)}, u32[]{:S(2)}) collective-permute-start(bf16[32,1152]{1,0:T(8,128)(2,1)S(1)} %get-tuple-element.7), channel_id=1, source_target_pairs={{0,280},{1,281},{2,282},{3,283},{4,284},{5,285},{6,286},{7,287},{8... | collective-permute-start | bytes 221192 | tf_op jit(solution)/shard_map/ppermute | solution.py:293
  17.3 0.0 collective-permute-done.2.one_ref
  17.3 3.2 %collective-permute-done.3.two_ref = bf16[32,1152]{1,0:T(8,128)(2,1)S(1)} collective-permute-done((bf16[32,1152]{1,0:T(8,128)(2,1)S(1)}, bf16[32,1152]{1,0:T(8,128)(2,1)S(1)}, u32[]{:S(2)}, u32[]{:S(2)}) %collective-permute-start.3) | collective-permute-done | bytes 73760 | tf_op jit(solution)/shard_map/ppermute | solution.py:293
  20.5 1.2 %shard_map.42 = bf16[512,1152]{1,0:T(8,128)(2,1)} custom-call(bf16[32,1152]{1,0:T(8,128)(2,1)S(1)} %collective-permute-done.2.one_ref, bf16[32,1152]{1,0:T(8,128)(2,1)S(1)} %collective-permute-done.3.two_ref), custom_call_target="tpu_custom_call" | custom-call | tf_op jit(solution)/shard_map/pallas_call | solution.py:118
  21.7 5.2 %all-to-all-done = bf16[8,32,1152]{2,1,0:T(8,128)(2,1)S(1)} async-done(((bf16[8,32,1152]{2,1,0:T(8,128)(2,1)}), bf16[8,32,1152]{2,1,0:T(8,128)(2,1)S(1)}, u32[]{:S(2)}, u32[]{:S(2)}) %all-to-all-start) | async-done | bytes 589856 | tf_op jit(solution)/shard_map/all_to_all | solution.py:288
  26.9 0.0 copy-start.4
  26.9 3.6 %all-to-all-start.1 = ((bf16[8,64,1152]{2,1,0:T(8,128)(2,1)}), bf16[8,64,1152]{2,1,0:T(8,128)(2,1)S(1)}, u32[]{:S(2)}, u32[]{:S(2)}) async-start(bf16[8,64,1152]{2,1,0:T(8,128)(2,1)} %bitcast.5), calls=%async_computation.1 | async-start | bytes 2359296 | tf_op jit(solution)/shard_map/all_to_all | solution.py:288
  30.5 2.7 %collective-permute-start = (bf16[256,1152]{1,0:T(8,128)(2,1)S(1)}, bf16[256,1152]{1,0:T(8,128)(2,1)S(1)}, u32[]{:S(2)}, u32[]{:S(2)}) collective-permute-start(bf16[256,1152]{1,0:T(8,128)(2,1)S(1)} %bitcast.18), channel_id=1, source_target_pairs={{0,8},{1,9},{2,10},{3,11},{4,12},{5,13},{6,14},{7,15},{8,0},{9,1},... | collective-permute-start | bytes 1769480 | tf_op jit(solution)/shard_map/ppermute | solution.py:293
  33.2 9.0 %collective-permute-done.refs_0_ = bf16[256,1152]{1,0:T(8,128)(2,1)S(1)} collective-permute-done((bf16[256,1152]{1,0:T(8,128)(2,1)S(1)}, bf16[256,1152]{1,0:T(8,128)(2,1)S(1)}, u32[]{:S(2)}, u32[]{:S(2)}) %collective-permute-start) | collective-permute-done | bytes 589856 | tf_op jit(solution)/shard_map/ppermute | solution.py:293
  42.2 0.0 copy-done.4
  42.2 0.0 copy-start.5
  42.2 1.2 %pad_maximum_fusion = bf16[512,1152]{1,0:T(8,128)(2,1)} fusion(bf16[256,1152]{1,0:T(8,128)(2,1)S(1)} %collective-permute-done.refs_0_, bf16[256,1152]{1,0:T(8,128)(2,1)S(1)} %bitcast.19), kind=kLoop, calls=%fused_computation | loop fusion | flops 2359296 | bytes 2359296 | tf_op jit(solution)/shard_map/concatenate | solution.py:303
  43.5 0.0 copy-done.5
  43.5 2.3 %collective-permute-start.1 = (bf16[512,1152]{1,0:T(8,128)(2,1)}, bf16[512,1152]{1,0:T(8,128)(2,1)S(1)}, u32[]{:S(2)}, u32[]{:S(2)}) collective-permute-start(bf16[512,1152]{1,0:T(8,128)(2,1)} %pad_maximum_fusion), channel_id=1, source_target_pairs={{0,16},{16,0},{1,17},{17,1},{2,18},{18,2},{3,19},{19,3},{4,20},{20... | collective-permute-start | bytes 3538952 | tf_op jit(solution)/shard_map/ppermute | solution.py:296
  45.8 5.0 %all-to-all-done.1 = bf16[8,64,1152]{2,1,0:T(8,128)(2,1)S(1)} async-done(((bf16[8,64,1152]{2,1,0:T(8,128)(2,1)}), bf16[8,64,1152]{2,1,0:T(8,128)(2,1)S(1)}, u32[]{:S(2)}, u32[]{:S(2)}) %all-to-all-start.1) | async-done | bytes 1179680 | tf_op jit(solution)/shard_map/all_to_all | solution.py:288
  50.7 1.9 %collective-permute-start.4 = (bf16[512,1152]{1,0:T(8,128)(2,1)S(1)}, bf16[512,1152]{1,0:T(8,128)(2,1)S(1)}, u32[]{:S(2)}, u32[]{:S(2)}) collective-permute-start(bf16[512,1152]{1,0:T(8,128)(2,1)S(1)} %bitcast.14), channel_id=1, source_target_pairs={{0,16},{16,0},{1,17},{17,1},{2,18},{18,2},{3,19},{19,3},{4,20},{20... | collective-permute-start | bytes 3538952 | tf_op jit(solution)/shard_map/ppermute | solution.py:296
  52.7 0.1 pad_add_fusion.refs_0_
  52.8 0.0 collective-permute-done.1.refs_2_.refs_1_
  52.8 0.0 copy-start.2
  52.8 2.3 %shard_map.46.refs_2_ = bf16[512,1152]{1,0:T(8,128)(2,1)S(1)} custom-call(s32[3]{0:T(128)S(1)} %pad_add_fusion.refs_0_, bf16[512,1152]{1,0:T(8,128)(2,1)S(1)} %bitcast.15, bf16[512,1152]{1,0:T(8,128)(2,1)S(1)} %collective-permute-done.1.refs_2_.refs_1_), custom_call_target="tpu_custom_call" | custom-call | flops 1207959552 | bytes 4718592 | tf_op jit(solution)/shard_map/pallas_call | solution.py:185
  55.1 0.4 collective-permute-done.4.refs_3_.refs_2_.refs_1_
  55.5 2.6 %shard_map.47 = bf16[512,1152]{1,0:T(8,128)(2,1)} custom-call(bf16[512,1152]{1,0:T(8,128)(2,1)S(1)} %bitcast.16, bf16[512,1152]{1,0:T(8,128)(2,1)S(1)} %collective-permute-done.4.refs_3_.refs_2_.refs_1_, bf16[512,1152]{1,0:T(8,128)(2,1)S(1)} %shard_map.46.refs_2_), custom_call_target="tpu_custom_call" | custom-call | flops 1207959552 | bytes 4718592 | tf_op jit(solution)/shard_map/pallas_call | solution.py:185
  58.0 5.6 %all-to-all-start.3 = ((bf16[8,64,1152]{2,1,0:T(8,128)(2,1)}), bf16[8,64,1152]{2,1,0:T(8,128)(2,1)S(1)}, u32[]{:S(2)}, u32[]{:S(2)}) async-start(bf16[8,64,1152]{2,1,0:T(8,128)(2,1)} %bitcast.11), calls=%async_computation.3 | async-start | bytes 2359296 | tf_op jit(solution)/shard_map/all_to_all | solution.py:288
  63.6 0.0 copy-done.2
  63.6 3.6 %shard_map.44 = bf16[256,1152]{1,0:T(8,128)(2,1)} custom-call(bf16[256,1152]{1,0:T(8,128)(2,1)} %copy-done.5, bf16[512,1152]{1,0:T(8,128)(2,1)S(1)} %collective-permute-done.1.refs_2_.refs_1_, bf16[512,1152]{1,0:T(8,128)(2,1)S(1)} %collective-permute-done.4.refs_3_.refs_2_.refs_1_), custom_call_target="tpu_custom_call" | custom-call | flops 1207959552 | bytes 2359296 | tf_op jit(solution)/shard_map/pallas_call | solution.py:185
  67.2 1.9 %collective-permute-start.5 = (bf16[256,1152]{1,0:T(8,128)(2,1)}, bf16[256,1152]{1,0:T(8,128)(2,1)S(1)}, u32[]{:S(2)}, u32[]{:S(2)}) collective-permute-start(bf16[256,1152]{1,0:T(8,128)(2,1)} %shard_map.44), channel_id=1, source_target_pairs={{0,8},{1,9},{2,10},{3,11},{4,12},{5,13},{6,14},{7,15},{8,0},{9,1},... | collective-permute-start | bytes 1769480 | tf_op jit(solution)/shard_map/ppermute | solution.py:293
  69.1 0.1 pad_add_fusion.1.refs_0_
  69.2 0.0 copy-start.3
  69.2 1.3 %copy-done.3 = bf16[512,1152]{1,0:T(8,128)(2,1)S(1)} copy-done((bf16[512,1152]{1,0:T(8,128)(2,1)S(1)}, bf16[512,1152]{1,0:T(8,128)(2,1)}, u32[]{:S(2)}) %copy-start.3) | copy-done | bytes 1179672
  70.5 2.9 %shard_map.43.one_ref = f32[256,1152]{1,0:T(8,128)S(1)} custom-call(s32[3]{0:T(128)S(1)} %pad_add_fusion.1.refs_0_, bf16[256,1152]{1,0:T(8,128)(2,1)} %bitcast.20, bf16[512,1152]{1,0:T(8,128)(2,1)S(1)} %copy-done.3, bf16[512,1152]{1,0:T(8,128)(2,1)S(1)} %collective-permute-done.4.refs_3_.refs_2_.refs_1_), custom_call_target="tpu_custom_call" | custom-call | flops 1207959552 | bytes 2359296 | tf_op jit(solution)/shard_map/pallas_call | solution.py:185
  73.4 5.8 %collective-permute-done.5.two_ref = bf16[256,1152]{1,0:T(8,128)(2,1)S(1)} collective-permute-done((bf16[256,1152]{1,0:T(8,128)(2,1)}, bf16[256,1152]{1,0:T(8,128)(2,1)S(1)}, u32[]{:S(2)}, u32[]{:S(2)}) %collective-permute-start.5) | collective-permute-done | bytes 589856 | tf_op jit(solution)/shard_map/ppermute | solution.py:293
  79.2 1.0 shard_map.45
  80.2 3.8 %all-to-all-done.3 = bf16[8,64,1152]{2,1,0:T(8,128)(2,1)S(1)} async-done(((bf16[8,64,1152]{2,1,0:T(8,128)(2,1)}), bf16[8,64,1152]{2,1,0:T(8,128)(2,1)S(1)}, u32[]{:S(2)}, u32[]{:S(2)}) %all-to-all-start.3) | async-done | bytes 1179680 | tf_op jit(solution)/shard_map/all_to_all | solution.py:288
  84.0 0.0 copy-start
  84.0 0.0 copy-start.1
  84.0 3.7 %all-to-all-start.2 = ((bf16[8,32,1152]{2,1,0:T(8,128)(2,1)}), bf16[8,32,1152]{2,1,0:T(8,128)(2,1)S(1)}, u32[]{:S(2)}, u32[]{:S(2)}) async-start(bf16[8,32,1152]{2,1,0:T(8,128)(2,1)} %bitcast.7), calls=%async_computation.2 | async-start | bytes 1179648 | tf_op jit(solution)/shard_map/all_to_all | solution.py:288
  87.6 0.2 shard_map.48
  87.8 3.0 %collective-permute-start.6 = (f32[32,1152]{1,0:T(8,128)S(1)}, f32[32,1152]{1,0:T(8,128)S(1)}, u32[]{:S(2)}, u32[]{:S(2)}) collective-permute-start(f32[32,1152]{1,0:T(8,128)S(1)} %get-tuple-element.8), channel_id=1, source_target_pairs={{0,16},{16,0},{1,17},{17,1},{2,18},{18,2},{3,19},{19,3},{4,20},{20... | collective-permute-start | bytes 442376 | tf_op jit(solution)/shard_map/ppermute | solution.py:296
  90.8 1.9 %collective-permute-start.7 = (bf16[32,1152]{1,0:T(8,128)(2,1)S(1)}, bf16[32,1152]{1,0:T(8,128)(2,1)S(1)}, u32[]{:S(2)}, u32[]{:S(2)}) collective-permute-start(bf16[32,1152]{1,0:T(8,128)(2,1)S(1)} %get-tuple-element.9), channel_id=1, source_target_pairs={{0,24},{1,25},{2,26},{3,27},{4,28},{5,29},{6,30},{7,31},{8,16},{9,... | collective-permute-start | bytes 221192 | tf_op jit(solution)/shard_map/ppermute | solution.py:293
  92.8 8.8 %all-to-all-done.2 = bf16[8,32,1152]{2,1,0:T(8,128)(2,1)S(1)} async-done(((bf16[8,32,1152]{2,1,0:T(8,128)(2,1)}), bf16[8,32,1152]{2,1,0:T(8,128)(2,1)S(1)}, u32[]{:S(2)}, u32[]{:S(2)}) %all-to-all-start.2) | async-done | bytes 589856 | tf_op jit(solution)/shard_map/all_to_all | solution.py:288
  101.5 0.0 collective-permute-done.7.far_ref
  101.5 0.0 collective-permute-done.6.near_ref
  101.6 0.0 copy-done
  101.6 0.0 copy-done.1
  101.6 0.9 shard_map.49
Async XLA Ops:
  2.6 24.3 %all-to-all-start = ((bf16[8,32,1152]{2,1,0:T(8,128)(2,1)}), bf16[8,32,1152]{2,1,0:T(8,128)(2,1)S(1)}, u32[]{:S(2)}, u32[]{:S(2)}) async-start(bf16[8,32,1152]{2,1,0:T(8,128)(2,1)} %bitcast.3), calls=%async_computation | async-start | bytes 1179648 | tf_op jit(solution)/shard_map/all_to_all | solution.py:288
  12.9 4.4 %collective-permute-start.2 = (bf16[32,1152]{1,0:T(8,128)(2,1)S(1)}, bf16[32,1152]{1,0:T(8,128)(2,1)S(1)}, u32[]{:S(2)}, u32[]{:S(2)}) collective-permute-start(bf16[32,1152]{1,0:T(8,128)(2,1)S(1)} %get-tuple-element.7), channel_id=1, source_target_pairs={{0,16},{16,0},{1,17},{17,1},{2,18},{18,2},{3,19},{19,3},{4,20},{20... | collective-permute-start | bytes 221192 | tf_op jit(solution)/shard_map/ppermute | solution.py:296
  14.8 5.7 %collective-permute-start.3 = (bf16[32,1152]{1,0:T(8,128)(2,1)S(1)}, bf16[32,1152]{1,0:T(8,128)(2,1)S(1)}, u32[]{:S(2)}, u32[]{:S(2)}) collective-permute-start(bf16[32,1152]{1,0:T(8,128)(2,1)S(1)} %get-tuple-element.7), channel_id=1, source_target_pairs={{0,280},{1,281},{2,282},{3,283},{4,284},{5,285},{6,286},{7,287},{8... | collective-permute-start | bytes 221192 | tf_op jit(solution)/shard_map/ppermute | solution.py:293
  26.9 15.4 %copy-start.4 = (bf16[8,32,1152]{2,1,0:T(8,128)(2,1)}, bf16[8,32,1152]{2,1,0:T(8,128)(2,1)S(1)}, u32[]{:S(2)}) copy-start(bf16[8,32,1152]{2,1,0:T(8,128)(2,1)S(1)} %all-to-all-done) | copy-start | bytes 1769476
  26.9 23.8 %all-to-all-start.1 = ((bf16[8,64,1152]{2,1,0:T(8,128)(2,1)}), bf16[8,64,1152]{2,1,0:T(8,128)(2,1)S(1)}, u32[]{:S(2)}, u32[]{:S(2)}) async-start(bf16[8,64,1152]{2,1,0:T(8,128)(2,1)} %bitcast.5), calls=%async_computation.1 | async-start | bytes 2359296 | tf_op jit(solution)/shard_map/all_to_all | solution.py:288
  30.5 11.8 %collective-permute-start = (bf16[256,1152]{1,0:T(8,128)(2,1)S(1)}, bf16[256,1152]{1,0:T(8,128)(2,1)S(1)}, u32[]{:S(2)}, u32[]{:S(2)}) collective-permute-start(bf16[256,1152]{1,0:T(8,128)(2,1)S(1)} %bitcast.18), channel_id=1, source_target_pairs={{0,8},{1,9},{2,10},{3,11},{4,12},{5,13},{6,14},{7,15},{8,0},{9,1},... | collective-permute-start | bytes 1769480 | tf_op jit(solution)/shard_map/ppermute | solution.py:293
  42.2 1.2 %copy-start.5 = (bf16[256,1152]{1,0:T(8,128)(2,1)}, bf16[256,1152]{1,0:T(8,128)(2,1)S(1)}, u32[]{:S(2)}) copy-start(bf16[256,1152]{1,0:T(8,128)(2,1)S(1)} %collective-permute-done.refs_0_) | copy-start | bytes 1769476
  43.5 9.3 %collective-permute-start.1 = (bf16[512,1152]{1,0:T(8,128)(2,1)}, bf16[512,1152]{1,0:T(8,128)(2,1)S(1)}, u32[]{:S(2)}, u32[]{:S(2)}) collective-permute-start(bf16[512,1152]{1,0:T(8,128)(2,1)} %pad_maximum_fusion), channel_id=1, source_target_pairs={{0,16},{16,0},{1,17},{17,1},{2,18},{18,2},{3,19},{19,3},{4,20},{20... | collective-permute-start | bytes 3538952 | tf_op jit(solution)/shard_map/ppermute | solution.py:296
  50.7 4.7 %collective-permute-start.4 = (bf16[512,1152]{1,0:T(8,128)(2,1)S(1)}, bf16[512,1152]{1,0:T(8,128)(2,1)S(1)}, u32[]{:S(2)}, u32[]{:S(2)}) collective-permute-start(bf16[512,1152]{1,0:T(8,128)(2,1)S(1)} %bitcast.14), channel_id=1, source_target_pairs={{0,16},{16,0},{1,17},{17,1},{2,18},{18,2},{3,19},{19,3},{4,20},{20... | collective-permute-start | bytes 3538952 | tf_op jit(solution)/shard_map/ppermute | solution.py:296
  52.8 10.8 %copy-start.2 = (bf16[512,1152]{1,0:T(8,128)(2,1)}, bf16[512,1152]{1,0:T(8,128)(2,1)S(1)}, u32[]{:S(2)}) copy-start(bf16[512,1152]{1,0:T(8,128)(2,1)S(1)} %collective-permute-done.1.refs_2_.refs_1_) | copy-start | bytes 3538948
  58.0 25.9 %all-to-all-start.3 = ((bf16[8,64,1152]{2,1,0:T(8,128)(2,1)}), bf16[8,64,1152]{2,1,0:T(8,128)(2,1)S(1)}, u32[]{:S(2)}, u32[]{:S(2)}) async-start(bf16[8,64,1152]{2,1,0:T(8,128)(2,1)} %bitcast.11), calls=%async_computation.3 | async-start | bytes 2359296 | tf_op jit(solution)/shard_map/all_to_all | solution.py:288
  67.2 12.0 %collective-permute-start.5 = (bf16[256,1152]{1,0:T(8,128)(2,1)}, bf16[256,1152]{1,0:T(8,128)(2,1)S(1)}, u32[]{:S(2)}, u32[]{:S(2)}) collective-permute-start(bf16[256,1152]{1,0:T(8,128)(2,1)} %shard_map.44), channel_id=1, source_target_pairs={{0,8},{1,9},{2,10},{3,11},{4,12},{5,13},{6,14},{7,15},{8,0},{9,1},... | collective-permute-start | bytes 1769480 | tf_op jit(solution)/shard_map/ppermute | solution.py:293
  69.2 1.3 %copy-start.3 = (bf16[512,1152]{1,0:T(8,128)(2,1)S(1)}, bf16[512,1152]{1,0:T(8,128)(2,1)}, u32[]{:S(2)}) copy-start(bf16[512,1152]{1,0:T(8,128)(2,1)} %copy-done.2) | copy-start | bytes 3538948
  84.0 17.6 %copy-start = (bf16[32,1152]{1,0:T(8,128)(2,1)S(1)}, bf16[32,1152]{1,0:T(8,128)(2,1)}, u32[]{:S(2)}) copy-start(bf16[32,1152]{1,0:T(8,128)(2,1)} %images_ref.1) | copy-start | bytes 221188
  84.0 17.6 %copy-start.1 = (bf16[32,1152]{1,0:T(8,128)(2,1)S(1)}, bf16[32,1152]{1,0:T(8,128)(2,1)}, u32[]{:S(2)}) copy-start(bf16[32,1152]{1,0:T(8,128)(2,1)} %texts_ref.1) | copy-start | bytes 221188
  84.0 17.6 %all-to-all-start.2 = ((bf16[8,32,1152]{2,1,0:T(8,128)(2,1)}), bf16[8,32,1152]{2,1,0:T(8,128)(2,1)S(1)}, u32[]{:S(2)}, u32[]{:S(2)}) async-start(bf16[8,32,1152]{2,1,0:T(8,128)(2,1)} %bitcast.7), calls=%async_computation.2 | async-start | bytes 1179648 | tf_op jit(solution)/shard_map/all_to_all | solution.py:288
  87.8 13.8 %collective-permute-start.6 = (f32[32,1152]{1,0:T(8,128)S(1)}, f32[32,1152]{1,0:T(8,128)S(1)}, u32[]{:S(2)}, u32[]{:S(2)}) collective-permute-start(f32[32,1152]{1,0:T(8,128)S(1)} %get-tuple-element.8), channel_id=1, source_target_pairs={{0,16},{16,0},{1,17},{17,1},{2,18},{18,2},{3,19},{19,3},{4,20},{20... | collective-permute-start | bytes 442376 | tf_op jit(solution)/shard_map/ppermute | solution.py:296
  90.8 10.7 %collective-permute-start.7 = (bf16[32,1152]{1,0:T(8,128)(2,1)S(1)}, bf16[32,1152]{1,0:T(8,128)(2,1)S(1)}, u32[]{:S(2)}, u32[]{:S(2)}) collective-permute-start(bf16[32,1152]{1,0:T(8,128)(2,1)S(1)} %get-tuple-element.9), channel_id=1, source_target_pairs={{0,24},{1,25},{2,26},{3,27},{4,28},{5,29},{6,30},{7,31},{8,16},{9,... | collective-permute-start | bytes 221192 | tf_op jit(solution)/shard_map/ppermute | solution.py:293

commit v5 on v4

v5 whole, which is shorter than its diff:
```python
import functools

import jax
import jax.numpy as jnp
from jax import lax
from jax.experimental import pallas as pl
from jax.experimental.pallas import tpu as pltpu
from jax.sharding import Mesh, PartitionSpec as P

logit_scale = 30.0
logit_bias = -5.0
epsilon = 1e-06

AXES = ("xh", "y", "core", "xl", "z")
SIZES = (2, 8, 2, 2, 8)
ALL = P(AXES, None)
SWAP = [(0, 1), (1, 0)]
LINE = 8

IN_VMEM = pl.BlockSpec(memory_space=pltpu.VMEM)
IN_HBM = pl.BlockSpec(memory_space=pltpu.HBM)
IN_ANY = pl.BlockSpec(memory_space=pl.ANY)
IN_SMEM = pl.BlockSpec(memory_space=pltpu.SMEM)
PARAMS = pltpu.CompilerParams(vmem_limit_bytes=16 * 2**20)


def index_of(xh, y, core, xl, z):
    return (((xh * 8 + y) * 2 + core) * 2 + xl) * 8 + z


def line_groups(role):
    groups = []
    for core in range(2):
        for xh in range(2):
            for xl in range(2):
                for at in range(8):
                    if role(core) == 0:
                        groups.append([index_of(xh, at, core, xl, z) for z in range(8)])
                    else:
                        groups.append([index_of(xh, y, core, xl, at) for y in range(8)])
    return groups


def across_x(role):
    pairs = []
    for xh in range(2):
        for y in range(8):
            for core in range(2):
                for xl in range(2):
                    for z in range(8):
                        to = (xh ^ role(core), y, core, 1 - xl, z)
                        pairs.append((index_of(xh, y, core, xl, z), index_of(*to)))
    return pairs


def unit_rows(raw):
    wide = raw.astype(jnp.float32)
    inverse = lax.rsqrt(jnp.sum(wide * wide, axis=1, keepdims=True) + epsilon)
    return (wide * inverse, inverse)


def raw_grad(unit_sum, raw):
    unit, inverse = unit_rows(raw)
    along = jnp.sum(unit_sum * unit, axis=1, keepdims=True)
    return inverse * (unit_sum - along * unit)


def run_all(copies):
    for copy in copies:
        copy.start()
    for copy in copies:
        copy.wait()


def open_kernel(
    core_ref, images_hbm, texts_hbm, copies_ref, second_ref, images_ref, texts_ref, unit_ref, sems
):
    first = core_ref[0] == 0
    run_all(
        [
            pltpu.make_async_copy(images_hbm, images_ref, sems.at[0]),
            pltpu.make_async_copy(texts_hbm, texts_ref, sems.at[1]),
        ]
    )
    img = unit_rows(images_ref[...])[0].astype(jnp.bfloat16)
    txt = unit_rows(texts_ref[...])[0].astype(jnp.bfloat16)
    unit_ref[...] = jnp.where(first, img, txt)
    second_ref[...] = jnp.where(first, txt, img)
    run_all(
        [pltpu.make_async_copy(unit_ref, copies_ref.at[at], sems.at[at]) for at in range(LINE)]
    )


def open_rows(core, images, texts):
    shape = images.shape
    return pl.pallas_call(
        open_kernel,
        out_shape=(
            pltpu.HBM((LINE, *shape), jnp.bfloat16),
            jax.ShapeDtypeStruct(shape, jnp.bfloat16),
        ),
        in_specs=[IN_SMEM, IN_HBM, IN_HBM],
        out_specs=(IN_HBM, IN_VMEM),
        scratch_shapes=[pltpu.VMEM(shape, jnp.bfloat16)] * 3 + [pltpu.SemaphoreType.DMA((LINE,))],
        compiler_params=PARAMS,
    )(core, images, texts)


def copies_kernel(near_ref, far_ref, out_ref, sems):
    rows = near_ref.shape[0]
    copies = []
    for at in range(LINE):
        for half, ref in enumerate((near_ref, far_ref)):
            target = out_ref.at[at, pl.ds(half * rows, rows)]
            copies.append(pltpu.make_async_copy(ref, target, sems.at[2 * at + half]))
    run_all(copies)


def copies(near, far):
    rows, width = near.shape
    return pl.pallas_call(
        copies_kernel,
        out_shape=pltpu.HBM((LINE, 2 * rows, width), near.dtype),
        in_specs=[IN_VMEM, IN_VMEM],
        out_specs=IN_HBM,
        scratch_shapes=[pltpu.SemaphoreType.DMA((2 * LINE,))],
        compiler_params=PARAMS,
    )(near, far)


def hold_kernel(*refs):
    del refs


def hold(kept, after):
    return pl.pallas_call(
        hold_kernel,
        out_shape=jax.ShapeDtypeStruct(kept.shape, kept.dtype),
        in_specs=[IN_ANY] * (1 + len(after)),
        out_specs=IN_ANY,
        input_output_aliases={0: 0},
        compiler_params=PARAMS,
    )(kept, *after)


def block_of(ref, half):
    if half is not None:
        rows = ref.shape[1] // 2
        value = ref[:, half * rows : (half + 1) * rows, :]
    else:
        value = ref[...]
    return value.reshape(-1, value.shape[-1])


def pull_kernel(halves, parts, loads, labelled, added, waits, kind, *refs):
    refs = list(refs)
    at_ref = refs.pop(0) if labelled else None
    mine = [(refs.pop(0), half) for half in halves]
    theirs = [refs.pop(0) for _ in range(parts)]
    so_far_ref = refs.pop(0) if added else None
    if waits:
        refs.pop(0)
    out_ref = refs.pop(0)
    load = None
    if loads:
        loaded_ref, load_sem = refs.pop(0), refs.pop(0)
        load = pltpu.make_async_copy(theirs[-1], loaded_ref, load_sem)
        load.start()
        theirs[-1] = loaded_ref
    stores = []
    for block, (ref, half) in enumerate(mine):
        rows = block_of(ref, half)
        total = None
        for part, theirs_ref in enumerate(theirs):
            if load is not None and part == parts - 1:
                load.wait()
                load = None
            scores = lax.dot_general(
                rows,
                block_of(theirs_ref, None),
                (((1,), (1,)), ((), ())),
                preferred_element_type=jnp.float32,
            )
            chance = 1.0 / (1.0 + jnp.exp(-logit_bias - logit_scale * scores))
            if labelled == (block, part):
                row = lax.broadcasted_iota(jnp.int32, scores.shape, 0) - at_ref[0]
                column = lax.broadcasted_iota(jnp.int32, scores.shape, 1) - at_ref[1]
                same = (row == column) & (row >= 0) & (row < at_ref[2])
                chance = jnp.where(same, chance - 1.0, chance)
            coef = (logit_scale * chance).astype(jnp.bfloat16)
            if kind == "line" and part == parts - 1:
                break
            terms = jnp.dot(coef, block_of(theirs_ref, None), preferred_element_type=jnp.float32)
            total = terms if total is None else total + terms
        size = rows.shape[0]
        if kind == "vmem":
            if added:
                total = total + so_far_ref[block * size : (block + 1) * size].astype(jnp.float32)
            out_ref[block * size : (block + 1) * size] = total.astype(out_ref.dtype)
            continue
        stage_ref, sems = refs
        for half in range(2):
            rows = slice(half * size // 2, (half + 1) * size // 2)
            terms = jnp.dot(
                coef[rows], block_of(theirs[-1], None), preferred_element_type=jnp.float32
            )
            if total is not None:
                terms = terms + total[rows]
            if added:
                terms = terms + so_far_ref[rows].astype(jnp.float32)
            stage_ref[rows] = terms.astype(stage_ref.dtype)
            stores.append(
                pltpu.make_async_copy(stage_ref.at[rows], out_ref.at[rows], sems.at[half])
            )
            stores[-1].start()
    for store in stores:
        store.wait()


def pull(
    mine,
    theirs,
    at=None,
    labelled=None,
    so_far=None,
    after=None,
    load=False,
    kind="vmem",
    dtype=jnp.float32,
):
    halves = [half for _, half in mine]
    width = theirs[0].shape[-1]
    size = sum(part.size for part in theirs) // width
    rows = [part.size // width // (1 if half is None else 2) for part, half in mine]
    args = [part for part, _ in mine] + list(theirs)
    specs = [IN_VMEM] * len(args)
    if load:
        specs[-1] = IN_HBM
    if labelled:
        args.insert(0, at)
        specs.insert(0, IN_SMEM)
    if so_far is not None:
        args.append(so_far)
        specs.append(IN_VMEM)
    if after is not None:
        args.append(after)
        specs.append(IN_ANY)
    shape, scratch = (sum(rows), width), []
    if load:
        scratch += [pltpu.VMEM(theirs[-1].shape, jnp.bfloat16), pltpu.SemaphoreType.DMA(())]
    if kind == "line":
        scratch += [pltpu.VMEM(shape, dtype), pltpu.SemaphoreType.DMA((2,))]
    return pl.pallas_call(
        functools.partial(
            pull_kernel,
            halves,
            len(theirs),
            load,
            labelled,
            so_far is not None,
            after is not None,
            kind,
        ),
        out_shape=(jax.ShapeDtypeStruct if kind == "vmem" else pltpu.HBM)(shape, dtype),
        in_specs=specs,
        out_specs=IN_VMEM if kind == "vmem" else IN_HBM,
        scratch_shapes=scratch,
        compiler_params=PARAMS,
        cost_estimate=pl.CostEstimate(
            flops=4 * sum(rows) * size * width,
            bytes_accessed=8 * sum(rows) * width,
            transcendentals=2 * sum(rows) * size,
        ),
    )(*args)


def add_kernel(one_ref, two_ref, out_ref, stage_ref, sem):
    total = (one_ref[...] + two_ref[...].astype(jnp.float32)).astype(jnp.bfloat16)
    stage_ref[...] = total.reshape(stage_ref.shape)
    run_all([pltpu.make_async_copy(stage_ref, out_ref, sem)])


def add_rows(one, two):
    shape = (LINE, one.shape[0] // LINE, one.shape[1])
    return pl.pallas_call(
        add_kernel,
        out_shape=pltpu.HBM(shape, jnp.bfloat16),
        in_specs=[IN_VMEM, IN_VMEM],
        out_specs=IN_HBM,
        scratch_shapes=[pltpu.VMEM(shape, jnp.bfloat16), pltpu.SemaphoreType.DMA(())],
        compiler_params=PARAMS,
    )(one, two)


def line_sum(back_ref, start, rows):
    total = back_ref[0, start : start + rows].astype(jnp.float32)
    for place in range(1, LINE):
        total = total + back_ref[place, start : start + rows].astype(jnp.float32)
    return total


def sum_kernel(back_ref, near_ref, far_ref):
    rows = near_ref.shape[0]
    near_ref[...] = line_sum(back_ref, 0, rows)
    far_ref[...] = line_sum(back_ref, rows, rows).astype(far_ref.dtype)


def sum_rows(back):
    shape = (back.shape[1] // 2, back.shape[2])
    return pl.pallas_call(
        sum_kernel,
        out_shape=(
            jax.ShapeDtypeStruct(shape, jnp.float32),
            jax.ShapeDtypeStruct(shape, jnp.bfloat16),
        ),
        in_specs=[IN_VMEM],
        out_specs=(IN_VMEM, IN_VMEM),
        compiler_params=PARAMS,
    )(back)


def close_kernel(core_ref, near_ref, far_ref, back_ref, images_ref, texts_ref, img_ref, txt_ref):
    first = core_ref[0] == 0
    q_sum = near_ref[...] + far_ref[...].astype(jnp.float32)
    p_sum = line_sum(back_ref, 0, near_ref.shape[0])
    img_ref[...] = raw_grad(jnp.where(first, p_sum, q_sum), images_ref[...])
    txt_ref[...] = raw_grad(jnp.where(first, q_sum, p_sum), texts_ref[...])


def close_rows(core, near, far, back, images, texts):
    shape = jax.ShapeDtypeStruct(near.shape, jnp.float32)
    return pl.pallas_call(
        close_kernel,
        out_shape=(shape, shape),
        in_specs=[IN_SMEM] + [IN_VMEM] * 5,
        out_specs=(IN_VMEM, IN_VMEM),
        compiler_params=PARAMS,
    )(core, near, far, back, images, texts)


def in_hbm(array):
    return pltpu.with_memory_space_constraint(array, pltpu.HBM)


def in_vmem(array):
    return pltpu.with_memory_space_constraint(array, pltpu.VMEM)


def trade(blocks, role):
    return lax.all_to_all(
        blocks, AXES, split_axis=0, concat_axis=0, axis_index_groups=line_groups(role), tiled=True
    )


def swap_x(block, role):
    return lax.ppermute(block, AXES, across_x(role))


def p_role(core):
    return core


def q_role(core):
    return 1 - core


def local(images, texts):
    rows, width = images.shape
    bf = jnp.bfloat16
    core = lax.axis_index("core")
    y, z = lax.axis_index("y"), lax.axis_index("z")
    p_place, q_place = jnp.where(core == 0, z, y), jnp.where(core == 0, y, z)
    core = core.astype(jnp.int32).reshape(1)

    copies_p, own_q = open_rows(core, in_hbm(images), in_hbm(texts))
    near_p = trade(copies_p, p_role).reshape(-1, width)
    copies_q = copies(own_q, swap_x(own_q, q_role))
    near_p = hold(near_p, [in_hbm(copies_q)])
    mine_q = trade(copies_q, q_role)
    far_p = swap_x(near_p, p_role)
    theirs_p = in_hbm(lax.ppermute(jnp.concatenate([near_p, far_p], 0), "core", SWAP))

    at_pq = jnp.stack([p_place * rows, q_place * 2 * rows, rows]).astype(jnp.int32)
    at_qp = jnp.stack([q_place * 2 * rows, p_place * rows, rows]).astype(jnp.int32)
    all_q = [(mine_q, None)]
    theirs_q = in_vmem(lax.ppermute(mine_q.reshape(-1, width), "core", SWAP))
    sum_q = pull(all_q, [near_p, far_p], at=at_qp, labelled=(0, 0), after=theirs_p, dtype=bf)
    sum_q = pull(all_q, [theirs_q], so_far=sum_q, kind="line", dtype=bf)
    near, far = sum_rows(trade(sum_q.reshape(mine_q.shape), q_role))
    far = swap_x(far, q_role)

    others = [mine_q, theirs_p]
    back_p = swap_x(pull([(far_p, None)], others, load=True, dtype=bf), p_role)
    near_p = pull([(near_p, None)], others, at=at_pq, labelled=(0, 0), load=True)
    back_p = trade(add_rows(near_p, back_p), p_role)
    return close_rows(core, near, far, back_p, images, texts)


def solution(mesh):
    fine = Mesh(mesh.devices.reshape(SIZES), AXES)
    return jax.shard_map(
        local, mesh=fine, in_specs=(ALL, ALL), out_specs=(ALL, ALL), check_vma=False
    )
```

time: 104 us -> 105 us (level)
  waiting for transfers between devices: 41.1 us -> 46.4 us
  starting transfers between devices: 41.3 us -> 38.6 us
  local copies, waits for them, and re-layouts: 1.29 us -> 0.01 us
    ppermute x8 -> x6, starting transfers between devices: 18.2 us -> 14.1 us  [the longest x4 10.2 us: swap_x(): return lax.ppermute(block, AXES, across_x(role))]
    all_to_all x4, waiting for transfers between devices: 22.8 us -> 26.7 us  [trade(): lax.all_to_all(blocks, AXES, split_axis=0, concat_axis=0, axis_index_grou...]
    ppermute x8 -> x6, waiting for transfers between devices: 18.3 us -> 19.8 us  [the longest x4 19.4 us: swap_x(): return lax.ppermute(block, AXES, across_x(role))]
    all_to_all x4, starting transfers between devices: 23.1 us -> 24.5 us  [trade(): lax.all_to_all(blocks, AXES, split_axis=0, concat_axis=0, axis_index_grou...]
    unnamed x12 -> x4, local copies, waits for them, and re-layouts: 1.29 us -> 0.01 us
    pallas_call x7 -> x8, Pallas kernels: 15.5 us -> 15.7 us  [the longest x4 11.6 us: pull(): pl.pallas_call(functools.partial(pull_kernel, halves, len(theirs), load,...]
  transfers between devices with their start and end apart: 12 -> 10, of which waited for: 8 -> 8; matrix products, arithmetic and copies ran while one was open for 1% -> 1% of each run, Pallas kernels for 11% -> 11%
where the time goes in v5:
time: 105 us; the launch traced here: 104 us
  waiting for transfers between devices  46.4 us (44%)
  starting transfers between devices  38.6 us (37%)
  Pallas kernels  16.8 us (16%)
  other arithmetic  1.28 us (1%)
    all_to_all x4, waiting for transfers between devices, trade(): lax.all_to_all(blocks, AXES, split_axis=0, concat_axis=0, axis_index_grou...  26.7 us
    all_to_all x4, starting transfers between devices, trade(): lax.all_to_all(blocks, AXES, split_axis=0, concat_axis=0, axis_index_grou...  24.5 us
    ppermute x4, waiting for transfers between devices, swap_x(): return lax.ppermute(block, AXES, across_x(role))  19.4 us
    pallas_call x4, Pallas kernels, pull(): pl.pallas_call(functools.partial(pull_kernel, halves, len(theirs), load,...  11.6 us
    ppermute x4, starting transfers between devices, swap_x(): return lax.ppermute(block, AXES, across_x(role))  10.2 us
  transfers between devices with their start and end apart: 10, of which 8 were waited for; matrix products, arithmetic and copies ran while one was open for 1% of the time, Pallas kernels for 11%

profile of v5, /device:TPU:6, one launch (start us, length us, event | category | flops | bytes accessed | tf_op | source)
XLA Modules:
  0.0 103.9 jit_solution(2866650674569108635)
XLA Ops:
  0.6 2.0 %shard_map.41 = (bf16[8,32,1152]{2,1,0:T(8,128)(2,1)}, bf16[32,1152]{1,0:T(8,128)(2,1)S(1)}) custom-call(s32[1]{0:T(128)} %bitcast.core_ref, bf16[32,1152]{1,0:T(8,128)(2,1)} %images_ref.1, bf16[32,1152]{1,0:T(8,128)(2,1)} %texts_ref.1), custom_call_target="tpu_custom_call" | custom-call | tf_op jit(solution)/shard_map/pallas_call | solution.py:96
  2.6 10.3 %all-to-all-start.1 = ((bf16[8,32,1152]{2,1,0:T(8,128)(2,1)}), bf16[8,32,1152]{2,1,0:T(8,128)(2,1)S(1)}, u32[]{:S(2)}, u32[]{:S(2)}) async-start(bf16[8,32,1152]{2,1,0:T(8,128)(2,1)} %get-tuple-element.7), calls=%async_computation.1 | async-start | bytes 1179648 | tf_op jit(solution)/shard_map/all_to_all | solution.py:350
  12.9 2.4 %collective-permute-start = (bf16[32,1152]{1,0:T(8,128)(2,1)S(1)}, bf16[32,1152]{1,0:T(8,128)(2,1)S(1)}, u32[]{:S(2)}, u32[]{:S(2)}) collective-permute-start(bf16[32,1152]{1,0:T(8,128)(2,1)S(1)} %get-tuple-element.6.near_ref), channel_id=1, source_target_pairs={{0,264},{1,265},{2,266},{3,267},{4,268},{5,269},{6,270},{7,271},{8... | collective-permute-start | bytes 221192 | tf_op jit(solution)/shard_map/ppermute | solution.py:356
  15.3 5.1 %collective-permute-done.far_ref = bf16[32,1152]{1,0:T(8,128)(2,1)S(1)} collective-permute-done((bf16[32,1152]{1,0:T(8,128)(2,1)S(1)}, bf16[32,1152]{1,0:T(8,128)(2,1)S(1)}, u32[]{:S(2)}, u32[]{:S(2)}) %collective-permute-start) | collective-permute-done | bytes 73760 | tf_op jit(solution)/shard_map/ppermute | solution.py:356
  20.4 1.2 %shard_map.42.refs_1_ = bf16[8,64,1152]{2,1,0:T(8,128)(2,1)} custom-call(bf16[32,1152]{1,0:T(8,128)(2,1)S(1)} %get-tuple-element.6.near_ref, bf16[32,1152]{1,0:T(8,128)(2,1)S(1)} %collective-permute-done.far_ref), custom_call_target="tpu_custom_call" | custom-call | tf_op jit(solution)/shard_map/pallas_call | solution.py:121
  21.6 5.4 %all-to-all-done.1 = bf16[8,32,1152]{2,1,0:T(8,128)(2,1)S(1)} async-done(((bf16[8,32,1152]{2,1,0:T(8,128)(2,1)}), bf16[8,32,1152]{2,1,0:T(8,128)(2,1)S(1)}, u32[]{:S(2)}, u32[]{:S(2)}) %all-to-all-start.1) | async-done | bytes 589856 | tf_op jit(solution)/shard_map/all_to_all | solution.py:350
  26.9 7.1 %all-to-all-start = ((bf16[8,64,1152]{2,1,0:T(8,128)(2,1)}), bf16[8,64,1152]{2,1,0:T(8,128)(2,1)S(1)}, u32[]{:S(2)}, u32[]{:S(2)}) async-start(bf16[8,64,1152]{2,1,0:T(8,128)(2,1)} %shard_map.42.refs_1_), calls=%async_computation | async-start | bytes 2359296 | tf_op jit(solution)/shard_map/all_to_all | solution.py:350
  34.0 2.7 %collective-permute-start.2 = (bf16[256,1152]{1,0:T(8,128)(2,1)S(1)}, bf16[256,1152]{1,0:T(8,128)(2,1)S(1)}, u32[]{:S(2)}, u32[]{:S(2)}) collective-permute-start(bf16[256,1152]{1,0:T(8,128)(2,1)S(1)} %shard_map.43.refs_2_.refs_1_), channel_id=1, source_target_pairs={{0,8},{1,9},{2,10},{3,11},{4,12},{5,13},{6,14},{7,15},{8,0},{9,1},... | collective-permute-start | bytes 1769480 | tf_op jit(solution)/shard_map/ppermute | solution.py:356
  36.8 9.0 %collective-permute-done.2.refs_3_.refs_0_ = bf16[256,1152]{1,0:T(8,128)(2,1)S(1)} collective-permute-done((bf16[256,1152]{1,0:T(8,128)(2,1)S(1)}, bf16[256,1152]{1,0:T(8,128)(2,1)S(1)}, u32[]{:S(2)}, u32[]{:S(2)}) %collective-permute-start.2) | collective-permute-done | bytes 589856 | tf_op jit(solution)/shard_map/ppermute | solution.py:356
  45.8 1.1 %pad_maximum_fusion = bf16[512,1152]{1,0:T(8,128)(2,1)} fusion(bf16[256,1152]{1,0:T(8,128)(2,1)S(1)} %collective-permute-done.2.refs_3_.refs_0_, bf16[256,1152]{1,0:T(8,128)(2,1)S(1)} %shard_map.43.refs_2_.refs_1_), kind=kLoop, calls=%fused_computation | loop fusion | flops 2359296 | bytes 2359296 | tf_op jit(solution)/shard_map/concatenate | solution.py:381
  46.9 1.9 %collective-permute-start.3 = (bf16[512,1152]{1,0:T(8,128)(2,1)}, bf16[512,1152]{1,0:T(8,128)(2,1)}, u32[]{:S(2)}, u32[]{:S(2)}) collective-permute-start(bf16[512,1152]{1,0:T(8,128)(2,1)} %pad_maximum_fusion), channel_id=1, source_target_pairs={{0,16},{16,0},{1,17},{17,1},{2,18},{18,2},{3,19},{19,3},{4,20},{20... | collective-permute-start | bytes 3538952 | tf_op jit(solution)/shard_map/ppermute | solution.py:381
  48.8 5.5 %all-to-all-done.refs_1_.refs_0_.refs_2_ = bf16[8,64,1152]{2,1,0:T(8,128)(2,1)S(1)} async-done(((bf16[8,64,1152]{2,1,0:T(8,128)(2,1)}), bf16[8,64,1152]{2,1,0:T(8,128)(2,1)S(1)}, u32[]{:S(2)}, u32[]{:S(2)}) %all-to-all-start) | async-done | bytes 1179680 | tf_op jit(solution)/shard_map/all_to_all | solution.py:350
  54.4 1.9 %collective-permute-start.1 = (bf16[512,1152]{1,0:T(8,128)(2,1)S(1)}, bf16[512,1152]{1,0:T(8,128)(2,1)S(1)}, u32[]{:S(2)}, u32[]{:S(2)}) collective-permute-start(bf16[512,1152]{1,0:T(8,128)(2,1)S(1)} %bitcast.6), channel_id=1, source_target_pairs={{0,16},{16,0},{1,17},{17,1},{2,18},{18,2},{3,19},{19,3},{4,20},{20... | collective-permute-start | bytes 3538952 | tf_op jit(solution)/shard_map/ppermute | solution.py:386
  56.3 0.1 pad_add_fusion.1.refs_0_
  56.4 0.0 collective-permute-done.3.refs_4_.refs_3_.refs_2_
  56.4 2.4 %shard_map.44.refs_2_ = bf16[512,1152]{1,0:T(8,128)(2,1)S(1)} custom-call(s32[3]{0:T(128)S(1)} %pad_add_fusion.1.refs_0_, bf16[8,64,1152]{2,1,0:T(8,128)(2,1)S(1)} %all-to-all-done.refs_1_.refs_0_.refs_2_, bf16[256,1152]{1,0:T(8,128)(2,1)S(1)} %shard_map.43.refs_2_.refs_1_, bf16[256,1152]{1,0:T(8,128)(2,1)S(1)} %collective-permute-done.2.refs_3_.refs_0_, ...), custom_call_target="tpu_custom_call" | custom-call | flops 1207959552 | bytes 4718592 | tf_op jit(solution)/shard_map/pallas_call | solution.py:253
  58.8 0.3 collective-permute-done.1.refs_1_
  59.1 2.5 %shard_map.45 = bf16[512,1152]{1,0:T(8,128)(2,1)} custom-call(bf16[8,64,1152]{2,1,0:T(8,128)(2,1)S(1)} %all-to-all-done.refs_1_.refs_0_.refs_2_, bf16[512,1152]{1,0:T(8,128)(2,1)S(1)} %collective-permute-done.1.refs_1_, bf16[512,1152]{1,0:T(8,128)(2,1)S(1)} %shard_map.44.refs_2_), custom_call_target="tpu_custom_call" | custom-call | flops 1207959552 | bytes 4718592 | tf_op jit(solution)/shard_map/pallas_call | solution.py:253
  61.7 3.6 %all-to-all-start.2 = ((bf16[8,64,1152]{2,1,0:T(8,128)(2,1)}), bf16[8,64,1152]{2,1,0:T(8,128)(2,1)S(1)}, u32[]{:S(2)}, u32[]{:S(2)}) async-start(bf16[8,64,1152]{2,1,0:T(8,128)(2,1)} %bitcast.8), calls=%async_computation.2 | async-start | bytes 2359296 | tf_op jit(solution)/shard_map/all_to_all | solution.py:350
  65.2 3.1 %shard_map.48 = bf16[256,1152]{1,0:T(8,128)(2,1)S(1)} custom-call(bf16[256,1152]{1,0:T(8,128)(2,1)S(1)} %collective-permute-done.2.refs_3_.refs_0_, bf16[8,64,1152]{2,1,0:T(8,128)(2,1)S(1)} %all-to-all-done.refs_1_.refs_0_.refs_2_, bf16[512,1152]{1,0:T(8,128)(2,1)} %collective-permute-done.3.refs_4_.refs_3_.refs_2_), custom_call_target="tpu_custom_call" | custom-call | flops 1207959552 | bytes 2359296 | tf_op jit(solution)/shard_map/pallas_call | solution.py:253
  68.3 2.7 %collective-permute-start.5 = (bf16[256,1152]{1,0:T(8,128)(2,1)S(1)}, bf16[256,1152]{1,0:T(8,128)(2,1)S(1)}, u32[]{:S(2)}, u32[]{:S(2)}) collective-permute-start(bf16[256,1152]{1,0:T(8,128)(2,1)S(1)} %shard_map.48), channel_id=1, source_target_pairs={{0,8},{1,9},{2,10},{3,11},{4,12},{5,13},{6,14},{7,15},{8,0},{9,1},... | collective-permute-start | bytes 1769480 | tf_op jit(solution)/shard_map/ppermute | solution.py:356
  71.1 0.1 pad_add_fusion.refs_0_
  71.2 3.6 %shard_map.47.one_ref = f32[256,1152]{1,0:T(8,128)S(1)} custom-call(s32[3]{0:T(128)S(1)} %pad_add_fusion.refs_0_, bf16[256,1152]{1,0:T(8,128)(2,1)S(1)} %shard_map.43.refs_2_.refs_1_, bf16[8,64,1152]{2,1,0:T(8,128)(2,1)S(1)} %all-to-all-done.refs_1_.refs_0_.refs_2_, bf16[512,1152]{1,0:T(8,128)(2,1)} %collective-permute-done.3.refs_4_.refs_3_.refs_2_), custom_call_target="tpu_custom_call" | custom-call | flops 1207959552 | bytes 2359296 | tf_op jit(solution)/shard_map/pallas_call | solution.py:253
  74.8 5.3 %collective-permute-done.5.two_ref = bf16[256,1152]{1,0:T(8,128)(2,1)S(1)} collective-permute-done((bf16[256,1152]{1,0:T(8,128)(2,1)S(1)}, bf16[256,1152]{1,0:T(8,128)(2,1)S(1)}, u32[]{:S(2)}, u32[]{:S(2)}) %collective-permute-start.5) | collective-permute-done | bytes 589856 | tf_op jit(solution)/shard_map/ppermute | solution.py:356
  80.1 0.9 shard_map.49
  81.1 0.0 copy-start
  81.1 0.0 copy-start.1
  81.1 4.4 %all-to-all-done.2.back_ref = bf16[8,64,1152]{2,1,0:T(8,128)(2,1)S(1)} async-done(((bf16[8,64,1152]{2,1,0:T(8,128)(2,1)}), bf16[8,64,1152]{2,1,0:T(8,128)(2,1)S(1)}, u32[]{:S(2)}, u32[]{:S(2)}) %all-to-all-start.2) | async-done | bytes 1179680 | tf_op jit(solution)/shard_map/all_to_all | solution.py:350
  85.5 3.5 %all-to-all-start.3 = ((bf16[8,32,1152]{2,1,0:T(8,128)(2,1)}), bf16[8,32,1152]{2,1,0:T(8,128)(2,1)S(1)}, u32[]{:S(2)}, u32[]{:S(2)}) async-start(bf16[8,32,1152]{2,1,0:T(8,128)(2,1)} %shard_map.49), calls=%async_computation.3 | async-start | bytes 1179648 | tf_op jit(solution)/shard_map/all_to_all | solution.py:350
  89.1 0.2 shard_map.46
  89.2 2.4 %collective-permute-start.4 = (bf16[32,1152]{1,0:T(8,128)(2,1)S(1)}, bf16[32,1152]{1,0:T(8,128)(2,1)S(1)}, u32[]{:S(2)}, u32[]{:S(2)}) collective-permute-start(bf16[32,1152]{1,0:T(8,128)(2,1)S(1)} %get-tuple-element.9), channel_id=1, source_target_pairs={{0,264},{1,265},{2,266},{3,267},{4,268},{5,269},{6,270},{7,271},{8... | collective-permute-start | bytes 221192 | tf_op jit(solution)/shard_map/ppermute | solution.py:356
  91.6 11.3 %all-to-all-done.3.back_ref = bf16[8,32,1152]{2,1,0:T(8,128)(2,1)S(1)} async-done(((bf16[8,32,1152]{2,1,0:T(8,128)(2,1)}), bf16[8,32,1152]{2,1,0:T(8,128)(2,1)S(1)}, u32[]{:S(2)}, u32[]{:S(2)}) %all-to-all-start.3) | async-done | bytes 589856 | tf_op jit(solution)/shard_map/all_to_all | solution.py:350
  103.0 0.0 collective-permute-done.4.far_ref
  103.0 0.0 copy-done
  103.0 0.0 copy-done.1
  103.0 0.9 shard_map.50
  (1 shorter events, 0.0 us)
Async XLA Ops:
  2.6 24.3 %all-to-all-start.1 = ((bf16[8,32,1152]{2,1,0:T(8,128)(2,1)}), bf16[8,32,1152]{2,1,0:T(8,128)(2,1)S(1)}, u32[]{:S(2)}, u32[]{:S(2)}) async-start(bf16[8,32,1152]{2,1,0:T(8,128)(2,1)} %get-tuple-element.7), calls=%async_computation.1 | async-start | bytes 1179648 | tf_op jit(solution)/shard_map/all_to_all | solution.py:350
  12.9 7.4 %collective-permute-start = (bf16[32,1152]{1,0:T(8,128)(2,1)S(1)}, bf16[32,1152]{1,0:T(8,128)(2,1)S(1)}, u32[]{:S(2)}, u32[]{:S(2)}) collective-permute-start(bf16[32,1152]{1,0:T(8,128)(2,1)S(1)} %get-tuple-element.6.near_ref), channel_id=1, source_target_pairs={{0,264},{1,265},{2,266},{3,267},{4,268},{5,269},{6,270},{7,271},{8... | collective-permute-start | bytes 221192 | tf_op jit(solution)/shard_map/ppermute | solution.py:356
  26.9 27.5 %all-to-all-start = ((bf16[8,64,1152]{2,1,0:T(8,128)(2,1)}), bf16[8,64,1152]{2,1,0:T(8,128)(2,1)S(1)}, u32[]{:S(2)}, u32[]{:S(2)}) async-start(bf16[8,64,1152]{2,1,0:T(8,128)(2,1)} %shard_map.42.refs_1_), calls=%async_computation | async-start | bytes 2359296 | tf_op jit(solution)/shard_map/all_to_all | solution.py:350
  34.0 11.8 %collective-permute-start.2 = (bf16[256,1152]{1,0:T(8,128)(2,1)S(1)}, bf16[256,1152]{1,0:T(8,128)(2,1)S(1)}, u32[]{:S(2)}, u32[]{:S(2)}) collective-permute-start(bf16[256,1152]{1,0:T(8,128)(2,1)S(1)} %shard_map.43.refs_2_.refs_1_), channel_id=1, source_target_pairs={{0,8},{1,9},{2,10},{3,11},{4,12},{5,13},{6,14},{7,15},{8,0},{9,1},... | collective-permute-start | bytes 1769480 | tf_op jit(solution)/shard_map/ppermute | solution.py:356
  46.9 9.5 %collective-permute-start.3 = (bf16[512,1152]{1,0:T(8,128)(2,1)}, bf16[512,1152]{1,0:T(8,128)(2,1)}, u32[]{:S(2)}, u32[]{:S(2)}) collective-permute-start(bf16[512,1152]{1,0:T(8,128)(2,1)} %pad_maximum_fusion), channel_id=1, source_target_pairs={{0,16},{16,0},{1,17},{17,1},{2,18},{18,2},{3,19},{19,3},{4,20},{20... | collective-permute-start | bytes 3538952 | tf_op jit(solution)/shard_map/ppermute | solution.py:381
  54.4 4.7 %collective-permute-start.1 = (bf16[512,1152]{1,0:T(8,128)(2,1)S(1)}, bf16[512,1152]{1,0:T(8,128)(2,1)S(1)}, u32[]{:S(2)}, u32[]{:S(2)}) collective-permute-start(bf16[512,1152]{1,0:T(8,128)(2,1)S(1)} %bitcast.6), channel_id=1, source_target_pairs={{0,16},{16,0},{1,17},{17,1},{2,18},{18,2},{3,19},{19,3},{4,20},{20... | collective-permute-start | bytes 3538952 | tf_op jit(solution)/shard_map/ppermute | solution.py:386
  61.7 23.9 %all-to-all-start.2 = ((bf16[8,64,1152]{2,1,0:T(8,128)(2,1)}), bf16[8,64,1152]{2,1,0:T(8,128)(2,1)S(1)}, u32[]{:S(2)}, u32[]{:S(2)}) async-start(bf16[8,64,1152]{2,1,0:T(8,128)(2,1)} %bitcast.8), calls=%async_computation.2 | async-start | bytes 2359296 | tf_op jit(solution)/shard_map/all_to_all | solution.py:350
  68.3 11.8 %collective-permute-start.5 = (bf16[256,1152]{1,0:T(8,128)(2,1)S(1)}, bf16[256,1152]{1,0:T(8,128)(2,1)S(1)}, u32[]{:S(2)}, u32[]{:S(2)}) collective-permute-start(bf16[256,1152]{1,0:T(8,128)(2,1)S(1)} %shard_map.48), channel_id=1, source_target_pairs={{0,8},{1,9},{2,10},{3,11},{4,12},{5,13},{6,14},{7,15},{8,0},{9,1},... | collective-permute-start | bytes 1769480 | tf_op jit(solution)/shard_map/ppermute | solution.py:356
  81.1 21.9 %copy-start = (bf16[32,1152]{1,0:T(8,128)(2,1)S(1)}, bf16[32,1152]{1,0:T(8,128)(2,1)}, u32[]{:S(2)}) copy-start(bf16[32,1152]{1,0:T(8,128)(2,1)} %images_ref.1) | copy-start | bytes 221188
  81.1 21.9 %copy-start.1 = (bf16[32,1152]{1,0:T(8,128)(2,1)S(1)}, bf16[32,1152]{1,0:T(8,128)(2,1)}, u32[]{:S(2)}) copy-start(bf16[32,1152]{1,0:T(8,128)(2,1)} %texts_ref.1) | copy-start | bytes 221188
  85.5 17.5 %all-to-all-start.3 = ((bf16[8,32,1152]{2,1,0:T(8,128)(2,1)}), bf16[8,32,1152]{2,1,0:T(8,128)(2,1)S(1)}, u32[]{:S(2)}, u32[]{:S(2)}) async-start(bf16[8,32,1152]{2,1,0:T(8,128)(2,1)} %shard_map.49), calls=%async_computation.3 | async-start | bytes 1179648 | tf_op jit(solution)/shard_map/all_to_all | solution.py:350
  89.2 13.8 %collective-permute-start.4 = (bf16[32,1152]{1,0:T(8,128)(2,1)S(1)}, bf16[32,1152]{1,0:T(8,128)(2,1)S(1)}, u32[]{:S(2)}, u32[]{:S(2)}) collective-permute-start(bf16[32,1152]{1,0:T(8,128)(2,1)S(1)} %get-tuple-element.9), channel_id=1, source_target_pairs={{0,264},{1,265},{2,266},{3,267},{4,268},{5,269},{6,270},{7,271},{8... | collective-permute-start | bytes 221192 | tf_op jit(solution)/shard_map/ppermute | solution.py:356

commit v6 on v5

--- a/solution.py
+++ b/solution.py
@@ -16,6 +16,8 @@
 ALL = P(AXES, None)
 SWAP = [(0, 1), (1, 0)]
 LINE = 8
+P_ORDER = (0, 1, 4, 5, 2, 3, 6, 7)
+Q_ORDER = (0, 4, 2, 6, 5, 1, 7, 3)
 
 IN_VMEM = pl.BlockSpec(memory_space=pltpu.VMEM)
 IN_HBM = pl.BlockSpec(memory_space=pltpu.HBM)
@@ -28,16 +30,16 @@
     return (((xh * 8 + y) * 2 + core) * 2 + xl) * 8 + z
 
 
-def line_groups(role):
+def line_groups(role, order):
     groups = []
     for core in range(2):
         for xh in range(2):
             for xl in range(2):
                 for at in range(8):
                     if role(core) == 0:
-                        groups.append([index_of(xh, at, core, xl, z) for z in range(8)])
+                        groups.append([index_of(xh, at, core, xl, z) for z in order])
                     else:
-                        groups.append([index_of(xh, y, core, xl, at) for y in range(8)])
+                        groups.append([index_of(xh, y, core, xl, at) for y in order])
     return groups
 
 
@@ -346,10 +348,15 @@
     return pltpu.with_memory_space_constraint(array, pltpu.VMEM)
 
 
-def trade(blocks, role):
+def trade(blocks, role, order):
+    groups = line_groups(role, order)
     return lax.all_to_all(
-        blocks, AXES, split_axis=0, concat_axis=0, axis_index_groups=line_groups(role), tiled=True
+        blocks, AXES, split_axis=0, concat_axis=0, axis_index_groups=groups, tiled=True
     )
+
+
+def place_in(order, at):
+    return sum(jnp.where(at == where, place, 0) for place, where in enumerate(order))
 
 
 def swap_x(block, role):
@@ -369,14 +376,15 @@
     bf = jnp.bfloat16
     core = lax.axis_index("core")
     y, z = lax.axis_index("y"), lax.axis_index("z")
-    p_place, q_place = jnp.where(core == 0, z, y), jnp.where(core == 0, y, z)
+    p_place = place_in(P_ORDER, jnp.where(core == 0, z, y))
+    q_place = place_in(Q_ORDER, jnp.where(core == 0, y, z))
     core = core.astype(jnp.int32).reshape(1)
 
     copies_p, own_q = open_rows(core, in_hbm(images), in_hbm(texts))
-    near_p = trade(copies_p, p_role).reshape(-1, width)
+    near_p = trade(copies_p, p_role, P_ORDER).reshape(-1, width)
     copies_q = copies(own_q, swap_x(own_q, q_role))
     near_p = hold(near_p, [in_hbm(copies_q)])
-    mine_q = trade(copies_q, q_role)
+    mine_q = trade(copies_q, q_role, Q_ORDER)
     far_p = swap_x(near_p, p_role)
     theirs_p = in_hbm(lax.ppermute(jnp.concatenate([near_p, far_p], 0), "core", SWAP))
 
@@ -386,13 +394,13 @@
     theirs_q = in_vmem(lax.ppermute(mine_q.reshape(-1, width), "core", SWAP))
     sum_q = pull(all_q, [near_p, far_p], at=at_qp, labelled=(0, 0), after=theirs_p, dtype=bf)
     sum_q = pull(all_q, [theirs_q], so_far=sum_q, kind="line", dtype=bf)
-    near, far = sum_rows(trade(sum_q.reshape(mine_q.shape), q_role))
+    near, far = sum_rows(trade(sum_q.reshape(mine_q.shape), q_role, Q_ORDER))
     far = swap_x(far, q_role)
 
     others = [mine_q, theirs_p]
     back_p = swap_x(pull([(far_p, None)], others, load=True, dtype=bf), p_role)
     near_p = pull([(near_p, None)], others, at=at_pq, labelled=(0, 0), load=True)
-    back_p = trade(add_rows(near_p, back_p), p_role)
+    back_p = trade(add_rows(near_p, back_p), p_role, P_ORDER)
     return close_rows(core, near, far, back_p, images, texts)
 
 

time: 105 us -> 97.4 us (0.928)
  waiting for transfers between devices: 46.4 us -> 37.5 us
  starting transfers between devices: 38.6 us -> 40.4 us
    all_to_all x4, waiting for transfers between devices: 26.7 us -> 17.7 us  [trade(): lax.all_to_all(blocks, AXES, split_axis=0, concat_axis=0, axis_index_grou...]
    all_to_all x4, starting transfers between devices: 24.5 us -> 26.3 us  [trade(): lax.all_to_all(blocks, AXES, split_axis=0, concat_axis=0, axis_index_grou...]
  transfers between devices with their start and end apart: 10 -> 10, of which waited for: 8 -> 8; matrix products, arithmetic and copies ran while one was open for 1% -> 1% of each run, Pallas kernels for 11% -> 12%
where the time goes in v6:
time: 97.4 us; the launch traced here: 96.8 us
  starting transfers between devices  40.4 us (41%)
  waiting for transfers between devices  37.5 us (39%)
  Pallas kernels  16.8 us (17%)
  other arithmetic  1.28 us (1%)
    all_to_all x4, starting transfers between devices, trade(): lax.all_to_all(blocks, AXES, split_axis=0, concat_axis=0, axis_index_grou...  26.3 us
    ppermute x4, waiting for transfers between devices, swap_x(): return lax.ppermute(block, AXES, across_x(role))  19.4 us
    all_to_all x4, waiting for transfers between devices, trade(): lax.all_to_all(blocks, AXES, split_axis=0, concat_axis=0, axis_index_grou...  17.7 us
    pallas_call x4, Pallas kernels, pull(): pl.pallas_call(functools.partial(pull_kernel, halves, len(theirs), load,...  11.6 us
    ppermute x4, starting transfers between devices, swap_x(): return lax.ppermute(block, AXES, across_x(role))  10.2 us
    pallas_call x1, Pallas kernels, open_rows(): pl.pallas_call(open_kernel, out_shape=(pltpu.HBM((LINE, *shape), jnp.bflo...  1.95 us
  transfers between devices with their start and end apart: 10, of which 8 were waited for; matrix products, arithmetic and copies ran while one was open for 1% of the time, Pallas kernels for 12%

profile of v6, /device:TPU:6, one launch (start us, length us, event | category | flops | bytes accessed | tf_op | source)
XLA Modules:
  0.0 96.8 jit_solution(5614090562762448354)
XLA Ops:
  0.6 2.0 %shard_map.41 = (bf16[8,32,1152]{2,1,0:T(8,128)(2,1)}, bf16[32,1152]{1,0:T(8,128)(2,1)S(1)}) custom-call(s32[1]{0:T(128)} %bitcast.core_ref, bf16[32,1152]{1,0:T(8,128)(2,1)} %images_ref.1, bf16[32,1152]{1,0:T(8,128)(2,1)} %texts_ref.1), custom_call_target="tpu_custom_call" | custom-call | tf_op jit(solution)/shard_map/pallas_call | solution.py:98
  2.6 10.3 %all-to-all-start.1 = ((bf16[8,32,1152]{2,1,0:T(8,128)(2,1)}), bf16[8,32,1152]{2,1,0:T(8,128)(2,1)S(1)}, u32[]{:S(2)}, u32[]{:S(2)}) async-start(bf16[8,32,1152]{2,1,0:T(8,128)(2,1)} %get-tuple-element.7), calls=%async_computation.1 | async-start | bytes 1179648 | tf_op jit(solution)/shard_map/all_to_all | solution.py:353
  12.9 2.4 %collective-permute-start = (bf16[32,1152]{1,0:T(8,128)(2,1)S(1)}, bf16[32,1152]{1,0:T(8,128)(2,1)S(1)}, u32[]{:S(2)}, u32[]{:S(2)}) collective-permute-start(bf16[32,1152]{1,0:T(8,128)(2,1)S(1)} %get-tuple-element.6.near_ref), channel_id=1, source_target_pairs={{0,264},{1,265},{2,266},{3,267},{4,268},{5,269},{6,270},{7,271},{8... | collective-permute-start | bytes 221192 | tf_op jit(solution)/shard_map/ppermute | solution.py:363
  15.3 5.1 %collective-permute-done.far_ref = bf16[32,1152]{1,0:T(8,128)(2,1)S(1)} collective-permute-done((bf16[32,1152]{1,0:T(8,128)(2,1)S(1)}, bf16[32,1152]{1,0:T(8,128)(2,1)S(1)}, u32[]{:S(2)}, u32[]{:S(2)}) %collective-permute-start) | collective-permute-done | bytes 73760 | tf_op jit(solution)/shard_map/ppermute | solution.py:363
  20.4 1.2 %shard_map.42.refs_1_ = bf16[8,64,1152]{2,1,0:T(8,128)(2,1)} custom-call(bf16[32,1152]{1,0:T(8,128)(2,1)S(1)} %get-tuple-element.6.near_ref, bf16[32,1152]{1,0:T(8,128)(2,1)S(1)} %collective-permute-done.far_ref), custom_call_target="tpu_custom_call" | custom-call | tf_op jit(solution)/shard_map/pallas_call | solution.py:123
  21.6 2.9 %all-to-all-done.1 = bf16[8,32,1152]{2,1,0:T(8,128)(2,1)S(1)} async-done(((bf16[8,32,1152]{2,1,0:T(8,128)(2,1)}), bf16[8,32,1152]{2,1,0:T(8,128)(2,1)S(1)}, u32[]{:S(2)}, u32[]{:S(2)}) %all-to-all-start.1) | async-done | bytes 589856 | tf_op jit(solution)/shard_map/all_to_all | solution.py:353
  24.4 7.1 %all-to-all-start = ((bf16[8,64,1152]{2,1,0:T(8,128)(2,1)}), bf16[8,64,1152]{2,1,0:T(8,128)(2,1)S(1)}, u32[]{:S(2)}, u32[]{:S(2)}) async-start(bf16[8,64,1152]{2,1,0:T(8,128)(2,1)} %shard_map.42.refs_1_), calls=%async_computation | async-start | bytes 2359296 | tf_op jit(solution)/shard_map/all_to_all | solution.py:353
  31.5 2.7 %collective-permute-start.2 = (bf16[256,1152]{1,0:T(8,128)(2,1)S(1)}, bf16[256,1152]{1,0:T(8,128)(2,1)S(1)}, u32[]{:S(2)}, u32[]{:S(2)}) collective-permute-start(bf16[256,1152]{1,0:T(8,128)(2,1)S(1)} %shard_map.43.refs_2_.refs_1_), channel_id=1, source_target_pairs={{0,8},{1,9},{2,10},{3,11},{4,12},{5,13},{6,14},{7,15},{8,0},{9,1},... | collective-permute-start | bytes 1769480 | tf_op jit(solution)/shard_map/ppermute | solution.py:363
  34.3 9.0 %collective-permute-done.2.refs_3_.refs_0_ = bf16[256,1152]{1,0:T(8,128)(2,1)S(1)} collective-permute-done((bf16[256,1152]{1,0:T(8,128)(2,1)S(1)}, bf16[256,1152]{1,0:T(8,128)(2,1)S(1)}, u32[]{:S(2)}, u32[]{:S(2)}) %collective-permute-start.2) | collective-permute-done | bytes 589856 | tf_op jit(solution)/shard_map/ppermute | solution.py:363
  43.3 1.1 %pad_maximum_fusion = bf16[512,1152]{1,0:T(8,128)(2,1)} fusion(bf16[256,1152]{1,0:T(8,128)(2,1)S(1)} %collective-permute-done.2.refs_3_.refs_0_, bf16[256,1152]{1,0:T(8,128)(2,1)S(1)} %shard_map.43.refs_2_.refs_1_), kind=kLoop, calls=%fused_computation | loop fusion | flops 2359296 | bytes 2359296 | tf_op jit(solution)/shard_map/concatenate | solution.py:389
  44.4 1.9 %collective-permute-start.3 = (bf16[512,1152]{1,0:T(8,128)(2,1)}, bf16[512,1152]{1,0:T(8,128)(2,1)}, u32[]{:S(2)}, u32[]{:S(2)}) collective-permute-start(bf16[512,1152]{1,0:T(8,128)(2,1)} %pad_maximum_fusion), channel_id=1, source_target_pairs={{0,16},{16,0},{1,17},{17,1},{2,18},{18,2},{3,19},{19,3},{4,20},{20... | collective-permute-start | bytes 3538952 | tf_op jit(solution)/shard_map/ppermute | solution.py:389
  46.3 3.5 %all-to-all-done.refs_1_.refs_0_.refs_2_ = bf16[8,64,1152]{2,1,0:T(8,128)(2,1)S(1)} async-done(((bf16[8,64,1152]{2,1,0:T(8,128)(2,1)}), bf16[8,64,1152]{2,1,0:T(8,128)(2,1)S(1)}, u32[]{:S(2)}, u32[]{:S(2)}) %all-to-all-start) | async-done | bytes 1179680 | tf_op jit(solution)/shard_map/all_to_all | solution.py:353
  49.8 1.9 %collective-permute-start.1 = (bf16[512,1152]{1,0:T(8,128)(2,1)S(1)}, bf16[512,1152]{1,0:T(8,128)(2,1)S(1)}, u32[]{:S(2)}, u32[]{:S(2)}) collective-permute-start(bf16[512,1152]{1,0:T(8,128)(2,1)S(1)} %bitcast.6), channel_id=1, source_target_pairs={{0,16},{16,0},{1,17},{17,1},{2,18},{18,2},{3,19},{19,3},{4,20},{20... | collective-permute-start | bytes 3538952 | tf_op jit(solution)/shard_map/ppermute | solution.py:394
  51.8 0.1 pad_add_fusion.1.refs_0_
  51.9 0.0 collective-permute-done.3.refs_4_.refs_3_.refs_2_
  51.9 2.4 %shard_map.44.refs_2_ = bf16[512,1152]{1,0:T(8,128)(2,1)S(1)} custom-call(s32[3]{0:T(128)S(1)} %pad_add_fusion.1.refs_0_, bf16[8,64,1152]{2,1,0:T(8,128)(2,1)S(1)} %all-to-all-done.refs_1_.refs_0_.refs_2_, bf16[256,1152]{1,0:T(8,128)(2,1)S(1)} %shard_map.43.refs_2_.refs_1_, bf16[256,1152]{1,0:T(8,128)(2,1)S(1)} %collective-permute-done.2.refs_3_.refs_0_, ...), custom_call_target="tpu_custom_call" | custom-call | flops 1207959552 | bytes 4718592 | tf_op jit(solution)/shard_map/pallas_call | solution.py:255
  54.3 0.3 collective-permute-done.1.refs_1_
  54.6 2.5 %shard_map.45 = bf16[512,1152]{1,0:T(8,128)(2,1)} custom-call(bf16[8,64,1152]{2,1,0:T(8,128)(2,1)S(1)} %all-to-all-done.refs_1_.refs_0_.refs_2_, bf16[512,1152]{1,0:T(8,128)(2,1)S(1)} %collective-permute-done.1.refs_1_, bf16[512,1152]{1,0:T(8,128)(2,1)S(1)} %shard_map.44.refs_2_), custom_call_target="tpu_custom_call" | custom-call | flops 1207959552 | bytes 4718592 | tf_op jit(solution)/shard_map/pallas_call | solution.py:255
  57.1 4.5 %all-to-all-start.2 = ((bf16[8,64,1152]{2,1,0:T(8,128)(2,1)}), bf16[8,64,1152]{2,1,0:T(8,128)(2,1)S(1)}, u32[]{:S(2)}, u32[]{:S(2)}) async-start(bf16[8,64,1152]{2,1,0:T(8,128)(2,1)} %bitcast.8), calls=%async_computation.2 | async-start | bytes 2359296 | tf_op jit(solution)/shard_map/all_to_all | solution.py:353
  61.6 3.1 %shard_map.48 = bf16[256,1152]{1,0:T(8,128)(2,1)S(1)} custom-call(bf16[256,1152]{1,0:T(8,128)(2,1)S(1)} %collective-permute-done.2.refs_3_.refs_0_, bf16[8,64,1152]{2,1,0:T(8,128)(2,1)S(1)} %all-to-all-done.refs_1_.refs_0_.refs_2_, bf16[512,1152]{1,0:T(8,128)(2,1)} %collective-permute-done.3.refs_4_.refs_3_.refs_2_), custom_call_target="tpu_custom_call" | custom-call | flops 1207959552 | bytes 2359296 | tf_op jit(solution)/shard_map/pallas_call | solution.py:255
  64.7 2.7 %collective-permute-start.5 = (bf16[256,1152]{1,0:T(8,128)(2,1)S(1)}, bf16[256,1152]{1,0:T(8,128)(2,1)S(1)}, u32[]{:S(2)}, u32[]{:S(2)}) collective-permute-start(bf16[256,1152]{1,0:T(8,128)(2,1)S(1)} %shard_map.48), channel_id=1, source_target_pairs={{0,8},{1,9},{2,10},{3,11},{4,12},{5,13},{6,14},{7,15},{8,0},{9,1},... | collective-permute-start | bytes 1769480 | tf_op jit(solution)/shard_map/ppermute | solution.py:363
  67.5 0.1 pad_add_fusion.refs_0_
  67.6 3.6 %shard_map.47.one_ref = f32[256,1152]{1,0:T(8,128)S(1)} custom-call(s32[3]{0:T(128)S(1)} %pad_add_fusion.refs_0_, bf16[256,1152]{1,0:T(8,128)(2,1)S(1)} %shard_map.43.refs_2_.refs_1_, bf16[8,64,1152]{2,1,0:T(8,128)(2,1)S(1)} %all-to-all-done.refs_1_.refs_0_.refs_2_, bf16[512,1152]{1,0:T(8,128)(2,1)} %collective-permute-done.3.refs_4_.refs_3_.refs_2_), custom_call_target="tpu_custom_call" | custom-call | flops 1207959552 | bytes 2359296 | tf_op jit(solution)/shard_map/pallas_call | solution.py:255
  71.2 5.3 %collective-permute-done.5.two_ref = bf16[256,1152]{1,0:T(8,128)(2,1)S(1)} collective-permute-done((bf16[256,1152]{1,0:T(8,128)(2,1)S(1)}, bf16[256,1152]{1,0:T(8,128)(2,1)S(1)}, u32[]{:S(2)}, u32[]{:S(2)}) %collective-permute-start.5) | collective-permute-done | bytes 589856 | tf_op jit(solution)/shard_map/ppermute | solution.py:363
  76.5 0.9 shard_map.49
  77.5 0.0 copy-start
  77.5 0.0 copy-start.1
  77.5 2.5 %all-to-all-done.2.back_ref = bf16[8,64,1152]{2,1,0:T(8,128)(2,1)S(1)} async-done(((bf16[8,64,1152]{2,1,0:T(8,128)(2,1)}), bf16[8,64,1152]{2,1,0:T(8,128)(2,1)S(1)}, u32[]{:S(2)}, u32[]{:S(2)}) %all-to-all-start.2) | async-done | bytes 1179680 | tf_op jit(solution)/shard_map/all_to_all | solution.py:353
  79.9 4.4 %all-to-all-start.3 = ((bf16[8,32,1152]{2,1,0:T(8,128)(2,1)}), bf16[8,32,1152]{2,1,0:T(8,128)(2,1)S(1)}, u32[]{:S(2)}, u32[]{:S(2)}) async-start(bf16[8,32,1152]{2,1,0:T(8,128)(2,1)} %shard_map.49), calls=%async_computation.3 | async-start | bytes 1179648 | tf_op jit(solution)/shard_map/all_to_all | solution.py:353
  84.3 0.2 shard_map.46
  84.5 2.4 %collective-permute-start.4 = (bf16[32,1152]{1,0:T(8,128)(2,1)S(1)}, bf16[32,1152]{1,0:T(8,128)(2,1)S(1)}, u32[]{:S(2)}, u32[]{:S(2)}) collective-permute-start(bf16[32,1152]{1,0:T(8,128)(2,1)S(1)} %get-tuple-element.9), channel_id=1, source_target_pairs={{0,264},{1,265},{2,266},{3,267},{4,268},{5,269},{6,270},{7,271},{8... | collective-permute-start | bytes 221192 | tf_op jit(solution)/shard_map/ppermute | solution.py:363
  86.9 9.0 %all-to-all-done.3.back_ref = bf16[8,32,1152]{2,1,0:T(8,128)(2,1)S(1)} async-done(((bf16[8,32,1152]{2,1,0:T(8,128)(2,1)}), bf16[8,32,1152]{2,1,0:T(8,128)(2,1)S(1)}, u32[]{:S(2)}, u32[]{:S(2)}) %all-to-all-start.3) | async-done | bytes 589856 | tf_op jit(solution)/shard_map/all_to_all | solution.py:353
  95.8 0.0 collective-permute-done.4.far_ref
  95.8 0.0 copy-done
  95.8 0.0 copy-done.1
  95.8 0.9 shard_map.50
  (1 shorter events, 0.0 us)
Async XLA Ops:
  2.6 21.8 %all-to-all-start.1 = ((bf16[8,32,1152]{2,1,0:T(8,128)(2,1)}), bf16[8,32,1152]{2,1,0:T(8,128)(2,1)S(1)}, u32[]{:S(2)}, u32[]{:S(2)}) async-start(bf16[8,32,1152]{2,1,0:T(8,128)(2,1)} %get-tuple-element.7), calls=%async_computation.1 | async-start | bytes 1179648 | tf_op jit(solution)/shard_map/all_to_all | solution.py:353
  12.9 7.4 %collective-permute-start = (bf16[32,1152]{1,0:T(8,128)(2,1)S(1)}, bf16[32,1152]{1,0:T(8,128)(2,1)S(1)}, u32[]{:S(2)}, u32[]{:S(2)}) collective-permute-start(bf16[32,1152]{1,0:T(8,128)(2,1)S(1)} %get-tuple-element.6.near_ref), channel_id=1, source_target_pairs={{0,264},{1,265},{2,266},{3,267},{4,268},{5,269},{6,270},{7,271},{8... | collective-permute-start | bytes 221192 | tf_op jit(solution)/shard_map/ppermute | solution.py:363
  24.4 25.4 %all-to-all-start = ((bf16[8,64,1152]{2,1,0:T(8,128)(2,1)}), bf16[8,64,1152]{2,1,0:T(8,128)(2,1)S(1)}, u32[]{:S(2)}, u32[]{:S(2)}) async-start(bf16[8,64,1152]{2,1,0:T(8,128)(2,1)} %shard_map.42.refs_1_), calls=%async_computation | async-start | bytes 2359296 | tf_op jit(solution)/shard_map/all_to_all | solution.py:353
  31.5 11.8 %collective-permute-start.2 = (bf16[256,1152]{1,0:T(8,128)(2,1)S(1)}, bf16[256,1152]{1,0:T(8,128)(2,1)S(1)}, u32[]{:S(2)}, u32[]{:S(2)}) collective-permute-start(bf16[256,1152]{1,0:T(8,128)(2,1)S(1)} %shard_map.43.refs_2_.refs_1_), channel_id=1, source_target_pairs={{0,8},{1,9},{2,10},{3,11},{4,12},{5,13},{6,14},{7,15},{8,0},{9,1},... | collective-permute-start | bytes 1769480 | tf_op jit(solution)/shard_map/ppermute | solution.py:363
  44.4 7.5 %collective-permute-start.3 = (bf16[512,1152]{1,0:T(8,128)(2,1)}, bf16[512,1152]{1,0:T(8,128)(2,1)}, u32[]{:S(2)}, u32[]{:S(2)}) collective-permute-start(bf16[512,1152]{1,0:T(8,128)(2,1)} %pad_maximum_fusion), channel_id=1, source_target_pairs={{0,16},{16,0},{1,17},{17,1},{2,18},{18,2},{3,19},{19,3},{4,20},{20... | collective-permute-start | bytes 3538952 | tf_op jit(solution)/shard_map/ppermute | solution.py:389
  49.8 4.7 %collective-permute-start.1 = (bf16[512,1152]{1,0:T(8,128)(2,1)S(1)}, bf16[512,1152]{1,0:T(8,128)(2,1)S(1)}, u32[]{:S(2)}, u32[]{:S(2)}) collective-permute-start(bf16[512,1152]{1,0:T(8,128)(2,1)S(1)} %bitcast.6), channel_id=1, source_target_pairs={{0,16},{16,0},{1,17},{17,1},{2,18},{18,2},{3,19},{19,3},{4,20},{20... | collective-permute-start | bytes 3538952 | tf_op jit(solution)/shard_map/ppermute | solution.py:394
  57.1 22.8 %all-to-all-start.2 = ((bf16[8,64,1152]{2,1,0:T(8,128)(2,1)}), bf16[8,64,1152]{2,1,0:T(8,128)(2,1)S(1)}, u32[]{:S(2)}, u32[]{:S(2)}) async-start(bf16[8,64,1152]{2,1,0:T(8,128)(2,1)} %bitcast.8), calls=%async_computation.2 | async-start | bytes 2359296 | tf_op jit(solution)/shard_map/all_to_all | solution.py:353
  64.7 11.8 %collective-permute-start.5 = (bf16[256,1152]{1,0:T(8,128)(2,1)S(1)}, bf16[256,1152]{1,0:T(8,128)(2,1)S(1)}, u32[]{:S(2)}, u32[]{:S(2)}) collective-permute-start(bf16[256,1152]{1,0:T(8,128)(2,1)S(1)} %shard_map.48), channel_id=1, source_target_pairs={{0,8},{1,9},{2,10},{3,11},{4,12},{5,13},{6,14},{7,15},{8,0},{9,1},... | collective-permute-start | bytes 1769480 | tf_op jit(solution)/shard_map/ppermute | solution.py:363
  77.5 18.4 %copy-start = (bf16[32,1152]{1,0:T(8,128)(2,1)S(1)}, bf16[32,1152]{1,0:T(8,128)(2,1)}, u32[]{:S(2)}) copy-start(bf16[32,1152]{1,0:T(8,128)(2,1)} %images_ref.1) | copy-start | bytes 221188
  77.5 18.4 %copy-start.1 = (bf16[32,1152]{1,0:T(8,128)(2,1)S(1)}, bf16[32,1152]{1,0:T(8,128)(2,1)}, u32[]{:S(2)}) copy-start(bf16[32,1152]{1,0:T(8,128)(2,1)} %texts_ref.1) | copy-start | bytes 221188
  79.9 15.9 %all-to-all-start.3 = ((bf16[8,32,1152]{2,1,0:T(8,128)(2,1)}), bf16[8,32,1152]{2,1,0:T(8,128)(2,1)S(1)}, u32[]{:S(2)}, u32[]{:S(2)}) async-start(bf16[8,32,1152]{2,1,0:T(8,128)(2,1)} %shard_map.49), calls=%async_computation.3 | async-start | bytes 1179648 | tf_op jit(solution)/shard_map/all_to_all | solution.py:353
  84.5 11.3 %collective-permute-start.4 = (bf16[32,1152]{1,0:T(8,128)(2,1)S(1)}, bf16[32,1152]{1,0:T(8,128)(2,1)S(1)}, u32[]{:S(2)}, u32[]{:S(2)}) collective-permute-start(bf16[32,1152]{1,0:T(8,128)(2,1)S(1)} %get-tuple-element.9), channel_id=1, source_target_pairs={{0,264},{1,265},{2,266},{3,267},{4,268},{5,269},{6,270},{7,271},{8... | collective-permute-start | bytes 221192 | tf_op jit(solution)/shard_map/ppermute | solution.py:363

commit v7 on v6

--- a/solution.py
+++ b/solution.py
@@ -16,8 +16,8 @@
 ALL = P(AXES, None)
 SWAP = [(0, 1), (1, 0)]
 LINE = 8
-P_ORDER = (0, 1, 4, 5, 2, 3, 6, 7)
-Q_ORDER = (0, 4, 2, 6, 5, 1, 7, 3)
+P_ORDER = (0, 4, 2, 6, 3, 7, 1, 5)
+Q_ORDER = (0, 2, 4, 6, 1, 3, 5, 7)
 
 IN_VMEM = pl.BlockSpec(memory_space=pltpu.VMEM)
 IN_HBM = pl.BlockSpec(memory_space=pltpu.HBM)
@@ -84,13 +84,17 @@
             pltpu.make_async_copy(texts_hbm, texts_ref, sems.at[1]),
         ]
     )
-    img = unit_rows(images_ref[...])[0].astype(jnp.bfloat16)
-    txt = unit_rows(texts_ref[...])[0].astype(jnp.bfloat16)
-    unit_ref[...] = jnp.where(first, img, txt)
-    second_ref[...] = jnp.where(first, txt, img)
-    run_all(
-        [pltpu.make_async_copy(unit_ref, copies_ref.at[at], sems.at[at]) for at in range(LINE)]
-    )
+    p_raw = jnp.where(first, images_ref[...], texts_ref[...])
+    q_raw = jnp.where(first, texts_ref[...], images_ref[...])
+    unit_ref[...] = unit_rows(p_raw)[0].astype(jnp.bfloat16)
+    stores = [
+        pltpu.make_async_copy(unit_ref, copies_ref.at[at], sems.at[at]) for at in range(LINE)
+    ]
+    for store in stores:
+        store.start()
+    second_ref[...] = unit_rows(q_raw)[0].astype(jnp.bfloat16)
+    for store in stores:
+        store.wait()
 
 
 def open_rows(core, images, texts):

time: 97.4 us -> 96.7 us (level)
  waiting for transfers between devices: 37.5 us -> 35.9 us
    all_to_all x4, waiting for transfers between devices: 17.7 us -> 16.2 us  [trade(): lax.all_to_all(blocks, AXES, split_axis=0, concat_axis=0, axis_index_grou...]
where the time goes in v7:
time: 96.7 us; the launch traced here: 96 us
  starting transfers between devices  41.2 us (43%)
  waiting for transfers between devices  35.9 us (37%)
  Pallas kernels  16.8 us (17%)
  other arithmetic  1.28 us (1%)
    all_to_all x4, starting transfers between devices, trade(): lax.all_to_all(blocks, AXES, split_axis=0, concat_axis=0, axis_index_grou...  27.1 us
    ppermute x4, waiting for transfers between devices, swap_x(): return lax.ppermute(block, AXES, across_x(role))  19.4 us
    all_to_all x4, waiting for transfers between devices, trade(): lax.all_to_all(blocks, AXES, split_axis=0, concat_axis=0, axis_index_grou...  16.2 us
    pallas_call x4, Pallas kernels, pull(): pl.pallas_call(functools.partial(pull_kernel, halves, len(theirs), load,...  11.6 us
    ppermute x4, starting transfers between devices, swap_x(): return lax.ppermute(block, AXES, across_x(role))  10.3 us
    pallas_call x1, Pallas kernels, open_rows(): pl.pallas_call(open_kernel, out_shape=(pltpu.HBM((LINE, *shape), jnp.bflo...  1.94 us
  transfers between devices with their start and end apart: 10, of which 8 were waited for; matrix products, arithmetic and copies ran while one was open for 1% of the time, Pallas kernels for 12%

profile of v7, /device:TPU:6, one launch (start us, length us, event | category | flops | bytes accessed | tf_op | source)
XLA Modules:
  0.0 96.0 jit_solution(3862477596197736365)
XLA Ops:
  0.6 1.9 %shard_map.41 = (bf16[8,32,1152]{2,1,0:T(8,128)(2,1)}, bf16[32,1152]{1,0:T(8,128)(2,1)S(1)}) custom-call(s32[1]{0:T(128)} %bitcast.core_ref, bf16[32,1152]{1,0:T(8,128)(2,1)} %images_ref.1, bf16[32,1152]{1,0:T(8,128)(2,1)} %texts_ref.1), custom_call_target="tpu_custom_call" | custom-call | tf_op jit(solution)/shard_map/pallas_call | solution.py:102
  2.6 10.3 %all-to-all-start.1 = ((bf16[8,32,1152]{2,1,0:T(8,128)(2,1)}), bf16[8,32,1152]{2,1,0:T(8,128)(2,1)S(1)}, u32[]{:S(2)}, u32[]{:S(2)}) async-start(bf16[8,32,1152]{2,1,0:T(8,128)(2,1)} %get-tuple-element.7), calls=%async_computation.1 | async-start | bytes 1179648 | tf_op jit(solution)/shard_map/all_to_all | solution.py:357
  12.9 2.4 %collective-permute-start = (bf16[32,1152]{1,0:T(8,128)(2,1)S(1)}, bf16[32,1152]{1,0:T(8,128)(2,1)S(1)}, u32[]{:S(2)}, u32[]{:S(2)}) collective-permute-start(bf16[32,1152]{1,0:T(8,128)(2,1)S(1)} %get-tuple-element.6.near_ref), channel_id=1, source_target_pairs={{0,264},{1,265},{2,266},{3,267},{4,268},{5,269},{6,270},{7,271},{8... | collective-permute-start | bytes 221192 | tf_op jit(solution)/shard_map/ppermute | solution.py:367
  15.3 5.1 %collective-permute-done.far_ref = bf16[32,1152]{1,0:T(8,128)(2,1)S(1)} collective-permute-done((bf16[32,1152]{1,0:T(8,128)(2,1)S(1)}, bf16[32,1152]{1,0:T(8,128)(2,1)S(1)}, u32[]{:S(2)}, u32[]{:S(2)}) %collective-permute-start) | collective-permute-done | bytes 73760 | tf_op jit(solution)/shard_map/ppermute | solution.py:367
  20.4 1.2 %shard_map.42.refs_1_ = bf16[8,64,1152]{2,1,0:T(8,128)(2,1)} custom-call(bf16[32,1152]{1,0:T(8,128)(2,1)S(1)} %get-tuple-element.6.near_ref, bf16[32,1152]{1,0:T(8,128)(2,1)S(1)} %collective-permute-done.far_ref), custom_call_target="tpu_custom_call" | custom-call | tf_op jit(solution)/shard_map/pallas_call | solution.py:127
  21.5 2.8 %all-to-all-done.1 = bf16[8,32,1152]{2,1,0:T(8,128)(2,1)S(1)} async-done(((bf16[8,32,1152]{2,1,0:T(8,128)(2,1)}), bf16[8,32,1152]{2,1,0:T(8,128)(2,1)S(1)}, u32[]{:S(2)}, u32[]{:S(2)}) %all-to-all-start.1) | async-done | bytes 589856 | tf_op jit(solution)/shard_map/all_to_all | solution.py:357
  24.3 7.1 %all-to-all-start = ((bf16[8,64,1152]{2,1,0:T(8,128)(2,1)}), bf16[8,64,1152]{2,1,0:T(8,128)(2,1)S(1)}, u32[]{:S(2)}, u32[]{:S(2)}) async-start(bf16[8,64,1152]{2,1,0:T(8,128)(2,1)} %shard_map.42.refs_1_), calls=%async_computation | async-start | bytes 2359296 | tf_op jit(solution)/shard_map/all_to_all | solution.py:357
  31.4 2.7 %collective-permute-start.2 = (bf16[256,1152]{1,0:T(8,128)(2,1)S(1)}, bf16[256,1152]{1,0:T(8,128)(2,1)S(1)}, u32[]{:S(2)}, u32[]{:S(2)}) collective-permute-start(bf16[256,1152]{1,0:T(8,128)(2,1)S(1)} %shard_map.43.refs_2_.refs_1_), channel_id=1, source_target_pairs={{0,8},{1,9},{2,10},{3,11},{4,12},{5,13},{6,14},{7,15},{8,0},{9,1},... | collective-permute-start | bytes 1769480 | tf_op jit(solution)/shard_map/ppermute | solution.py:367
  34.2 9.0 %collective-permute-done.2.refs_3_.refs_0_ = bf16[256,1152]{1,0:T(8,128)(2,1)S(1)} collective-permute-done((bf16[256,1152]{1,0:T(8,128)(2,1)S(1)}, bf16[256,1152]{1,0:T(8,128)(2,1)S(1)}, u32[]{:S(2)}, u32[]{:S(2)}) %collective-permute-start.2) | collective-permute-done | bytes 589856 | tf_op jit(solution)/shard_map/ppermute | solution.py:367
  43.2 1.1 %pad_maximum_fusion = bf16[512,1152]{1,0:T(8,128)(2,1)} fusion(bf16[256,1152]{1,0:T(8,128)(2,1)S(1)} %collective-permute-done.2.refs_3_.refs_0_, bf16[256,1152]{1,0:T(8,128)(2,1)S(1)} %shard_map.43.refs_2_.refs_1_), kind=kLoop, calls=%fused_computation | loop fusion | flops 2359296 | bytes 2359296 | tf_op jit(solution)/shard_map/concatenate | solution.py:393
  44.3 1.9 %collective-permute-start.3 = (bf16[512,1152]{1,0:T(8,128)(2,1)}, bf16[512,1152]{1,0:T(8,128)(2,1)}, u32[]{:S(2)}, u32[]{:S(2)}) collective-permute-start(bf16[512,1152]{1,0:T(8,128)(2,1)} %pad_maximum_fusion), channel_id=1, source_target_pairs={{0,16},{16,0},{1,17},{17,1},{2,18},{18,2},{3,19},{19,3},{4,20},{20... | collective-permute-start | bytes 3538952 | tf_op jit(solution)/shard_map/ppermute | solution.py:393
  46.2 2.8 %all-to-all-done.refs_1_.refs_0_.refs_2_ = bf16[8,64,1152]{2,1,0:T(8,128)(2,1)S(1)} async-done(((bf16[8,64,1152]{2,1,0:T(8,128)(2,1)}), bf16[8,64,1152]{2,1,0:T(8,128)(2,1)S(1)}, u32[]{:S(2)}, u32[]{:S(2)}) %all-to-all-start) | async-done | bytes 1179680 | tf_op jit(solution)/shard_map/all_to_all | solution.py:357
  49.0 1.9 %collective-permute-start.1 = (bf16[512,1152]{1,0:T(8,128)(2,1)S(1)}, bf16[512,1152]{1,0:T(8,128)(2,1)S(1)}, u32[]{:S(2)}, u32[]{:S(2)}) collective-permute-start(bf16[512,1152]{1,0:T(8,128)(2,1)S(1)} %bitcast.6), channel_id=1, source_target_pairs={{0,16},{16,0},{1,17},{17,1},{2,18},{18,2},{3,19},{19,3},{4,20},{20... | collective-permute-start | bytes 3538952 | tf_op jit(solution)/shard_map/ppermute | solution.py:398
  51.0 0.1 pad_add_fusion.1.refs_0_
  51.1 0.0 collective-permute-done.3.refs_4_.refs_3_.refs_2_
  51.1 2.4 %shard_map.44.refs_2_ = bf16[512,1152]{1,0:T(8,128)(2,1)S(1)} custom-call(s32[3]{0:T(128)S(1)} %pad_add_fusion.1.refs_0_, bf16[8,64,1152]{2,1,0:T(8,128)(2,1)S(1)} %all-to-all-done.refs_1_.refs_0_.refs_2_, bf16[256,1152]{1,0:T(8,128)(2,1)S(1)} %shard_map.43.refs_2_.refs_1_, bf16[256,1152]{1,0:T(8,128)(2,1)S(1)} %collective-permute-done.2.refs_3_.refs_0_, ...), custom_call_target="tpu_custom_call" | custom-call | flops 1207959552 | bytes 4718592 | tf_op jit(solution)/shard_map/pallas_call | solution.py:259
  53.5 0.3 collective-permute-done.1.refs_1_
  53.8 2.5 %shard_map.45 = bf16[512,1152]{1,0:T(8,128)(2,1)} custom-call(bf16[8,64,1152]{2,1,0:T(8,128)(2,1)S(1)} %all-to-all-done.refs_1_.refs_0_.refs_2_, bf16[512,1152]{1,0:T(8,128)(2,1)S(1)} %collective-permute-done.1.refs_1_, bf16[512,1152]{1,0:T(8,128)(2,1)S(1)} %shard_map.44.refs_2_), custom_call_target="tpu_custom_call" | custom-call | flops 1207959552 | bytes 4718592 | tf_op jit(solution)/shard_map/pallas_call | solution.py:259
  56.3 5.2 %all-to-all-start.2 = ((bf16[8,64,1152]{2,1,0:T(8,128)(2,1)}), bf16[8,64,1152]{2,1,0:T(8,128)(2,1)S(1)}, u32[]{:S(2)}, u32[]{:S(2)}) async-start(bf16[8,64,1152]{2,1,0:T(8,128)(2,1)} %bitcast.8), calls=%async_computation.2 | async-start | bytes 2359296 | tf_op jit(solution)/shard_map/all_to_all | solution.py:357
  61.5 3.1 %shard_map.48 = bf16[256,1152]{1,0:T(8,128)(2,1)S(1)} custom-call(bf16[256,1152]{1,0:T(8,128)(2,1)S(1)} %collective-permute-done.2.refs_3_.refs_0_, bf16[8,64,1152]{2,1,0:T(8,128)(2,1)S(1)} %all-to-all-done.refs_1_.refs_0_.refs_2_, bf16[512,1152]{1,0:T(8,128)(2,1)} %collective-permute-done.3.refs_4_.refs_3_.refs_2_), custom_call_target="tpu_custom_call" | custom-call | flops 1207959552 | bytes 2359296 | tf_op jit(solution)/shard_map/pallas_call | solution.py:259
  64.6 2.8 %collective-permute-start.5 = (bf16[256,1152]{1,0:T(8,128)(2,1)S(1)}, bf16[256,1152]{1,0:T(8,128)(2,1)S(1)}, u32[]{:S(2)}, u32[]{:S(2)}) collective-permute-start(bf16[256,1152]{1,0:T(8,128)(2,1)S(1)} %shard_map.48), channel_id=1, source_target_pairs={{0,8},{1,9},{2,10},{3,11},{4,12},{5,13},{6,14},{7,15},{8,0},{9,1},... | collective-permute-start | bytes 1769480 | tf_op jit(solution)/shard_map/ppermute | solution.py:367
  67.4 0.1 pad_add_fusion.refs_0_
  67.5 3.6 %shard_map.47.one_ref = f32[256,1152]{1,0:T(8,128)S(1)} custom-call(s32[3]{0:T(128)S(1)} %pad_add_fusion.refs_0_, bf16[256,1152]{1,0:T(8,128)(2,1)S(1)} %shard_map.43.refs_2_.refs_1_, bf16[8,64,1152]{2,1,0:T(8,128)(2,1)S(1)} %all-to-all-done.refs_1_.refs_0_.refs_2_, bf16[512,1152]{1,0:T(8,128)(2,1)} %collective-permute-done.3.refs_4_.refs_3_.refs_2_), custom_call_target="tpu_custom_call" | custom-call | flops 1207959552 | bytes 2359296 | tf_op jit(solution)/shard_map/pallas_call | solution.py:259
  71.1 5.3 %collective-permute-done.5.two_ref = bf16[256,1152]{1,0:T(8,128)(2,1)S(1)} collective-permute-done((bf16[256,1152]{1,0:T(8,128)(2,1)S(1)}, bf16[256,1152]{1,0:T(8,128)(2,1)S(1)}, u32[]{:S(2)}, u32[]{:S(2)}) %collective-permute-start.5) | collective-permute-done | bytes 589856 | tf_op jit(solution)/shard_map/ppermute | solution.py:367
  76.4 0.9 shard_map.49
  77.3 0.0 copy-start
  77.4 0.0 copy-start.1
  77.4 1.8 %all-to-all-done.2.back_ref = bf16[8,64,1152]{2,1,0:T(8,128)(2,1)S(1)} async-done(((bf16[8,64,1152]{2,1,0:T(8,128)(2,1)}), bf16[8,64,1152]{2,1,0:T(8,128)(2,1)S(1)}, u32[]{:S(2)}, u32[]{:S(2)}) %all-to-all-start.2) | async-done | bytes 1179680 | tf_op jit(solution)/shard_map/all_to_all | solution.py:357
  79.2 4.5 %all-to-all-start.3 = ((bf16[8,32,1152]{2,1,0:T(8,128)(2,1)}), bf16[8,32,1152]{2,1,0:T(8,128)(2,1)S(1)}, u32[]{:S(2)}, u32[]{:S(2)}) async-start(bf16[8,32,1152]{2,1,0:T(8,128)(2,1)} %shard_map.49), calls=%async_computation.3 | async-start | bytes 1179648 | tf_op jit(solution)/shard_map/all_to_all | solution.py:357
  83.6 0.2 shard_map.46
  83.8 2.4 %collective-permute-start.4 = (bf16[32,1152]{1,0:T(8,128)(2,1)S(1)}, bf16[32,1152]{1,0:T(8,128)(2,1)S(1)}, u32[]{:S(2)}, u32[]{:S(2)}) collective-permute-start(bf16[32,1152]{1,0:T(8,128)(2,1)S(1)} %get-tuple-element.9), channel_id=1, source_target_pairs={{0,264},{1,265},{2,266},{3,267},{4,268},{5,269},{6,270},{7,271},{8... | collective-permute-start | bytes 221192 | tf_op jit(solution)/shard_map/ppermute | solution.py:367
  86.2 8.9 %all-to-all-done.3.back_ref = bf16[8,32,1152]{2,1,0:T(8,128)(2,1)S(1)} async-done(((bf16[8,32,1152]{2,1,0:T(8,128)(2,1)}), bf16[8,32,1152]{2,1,0:T(8,128)(2,1)S(1)}, u32[]{:S(2)}, u32[]{:S(2)}) %all-to-all-start.3) | async-done | bytes 589856 | tf_op jit(solution)/shard_map/all_to_all | solution.py:357
  95.0 0.0 collective-permute-done.4.far_ref
  95.0 0.0 copy-done
  95.0 0.0 copy-done.1
  95.0 0.9 shard_map.50
  (1 shorter events, 0.0 us)
Async XLA Ops:
  2.6 21.7 %all-to-all-start.1 = ((bf16[8,32,1152]{2,1,0:T(8,128)(2,1)}), bf16[8,32,1152]{2,1,0:T(8,128)(2,1)S(1)}, u32[]{:S(2)}, u32[]{:S(2)}) async-start(bf16[8,32,1152]{2,1,0:T(8,128)(2,1)} %get-tuple-element.7), calls=%async_computation.1 | async-start | bytes 1179648 | tf_op jit(solution)/shard_map/all_to_all | solution.py:357
  12.9 7.4 %collective-permute-start = (bf16[32,1152]{1,0:T(8,128)(2,1)S(1)}, bf16[32,1152]{1,0:T(8,128)(2,1)S(1)}, u32[]{:S(2)}, u32[]{:S(2)}) collective-permute-start(bf16[32,1152]{1,0:T(8,128)(2,1)S(1)} %get-tuple-element.6.near_ref), channel_id=1, source_target_pairs={{0,264},{1,265},{2,266},{3,267},{4,268},{5,269},{6,270},{7,271},{8... | collective-permute-start | bytes 221192 | tf_op jit(solution)/shard_map/ppermute | solution.py:367
  24.3 24.7 %all-to-all-start = ((bf16[8,64,1152]{2,1,0:T(8,128)(2,1)}), bf16[8,64,1152]{2,1,0:T(8,128)(2,1)S(1)}, u32[]{:S(2)}, u32[]{:S(2)}) async-start(bf16[8,64,1152]{2,1,0:T(8,128)(2,1)} %shard_map.42.refs_1_), calls=%async_computation | async-start | bytes 2359296 | tf_op jit(solution)/shard_map/all_to_all | solution.py:357
  31.4 11.8 %collective-permute-start.2 = (bf16[256,1152]{1,0:T(8,128)(2,1)S(1)}, bf16[256,1152]{1,0:T(8,128)(2,1)S(1)}, u32[]{:S(2)}, u32[]{:S(2)}) collective-permute-start(bf16[256,1152]{1,0:T(8,128)(2,1)S(1)} %shard_map.43.refs_2_.refs_1_), channel_id=1, source_target_pairs={{0,8},{1,9},{2,10},{3,11},{4,12},{5,13},{6,14},{7,15},{8,0},{9,1},... | collective-permute-start | bytes 1769480 | tf_op jit(solution)/shard_map/ppermute | solution.py:367
  44.3 6.8 %collective-permute-start.3 = (bf16[512,1152]{1,0:T(8,128)(2,1)}, bf16[512,1152]{1,0:T(8,128)(2,1)}, u32[]{:S(2)}, u32[]{:S(2)}) collective-permute-start(bf16[512,1152]{1,0:T(8,128)(2,1)} %pad_maximum_fusion), channel_id=1, source_target_pairs={{0,16},{16,0},{1,17},{17,1},{2,18},{18,2},{3,19},{19,3},{4,20},{20... | collective-permute-start | bytes 3538952 | tf_op jit(solution)/shard_map/ppermute | solution.py:393
  49.0 4.7 %collective-permute-start.1 = (bf16[512,1152]{1,0:T(8,128)(2,1)S(1)}, bf16[512,1152]{1,0:T(8,128)(2,1)S(1)}, u32[]{:S(2)}, u32[]{:S(2)}) collective-permute-start(bf16[512,1152]{1,0:T(8,128)(2,1)S(1)} %bitcast.6), channel_id=1, source_target_pairs={{0,16},{16,0},{1,17},{17,1},{2,18},{18,2},{3,19},{19,3},{4,20},{20... | collective-permute-start | bytes 3538952 | tf_op jit(solution)/shard_map/ppermute | solution.py:398
  56.3 22.8 %all-to-all-start.2 = ((bf16[8,64,1152]{2,1,0:T(8,128)(2,1)}), bf16[8,64,1152]{2,1,0:T(8,128)(2,1)S(1)}, u32[]{:S(2)}, u32[]{:S(2)}) async-start(bf16[8,64,1152]{2,1,0:T(8,128)(2,1)} %bitcast.8), calls=%async_computation.2 | async-start | bytes 2359296 | tf_op jit(solution)/shard_map/all_to_all | solution.py:357
  64.6 11.8 %collective-permute-start.5 = (bf16[256,1152]{1,0:T(8,128)(2,1)S(1)}, bf16[256,1152]{1,0:T(8,128)(2,1)S(1)}, u32[]{:S(2)}, u32[]{:S(2)}) collective-permute-start(bf16[256,1152]{1,0:T(8,128)(2,1)S(1)} %shard_map.48), channel_id=1, source_target_pairs={{0,8},{1,9},{2,10},{3,11},{4,12},{5,13},{6,14},{7,15},{8,0},{9,1},... | collective-permute-start | bytes 1769480 | tf_op jit(solution)/shard_map/ppermute | solution.py:367
  77.3 17.7 %copy-start = (bf16[32,1152]{1,0:T(8,128)(2,1)S(1)}, bf16[32,1152]{1,0:T(8,128)(2,1)}, u32[]{:S(2)}) copy-start(bf16[32,1152]{1,0:T(8,128)(2,1)} %images_ref.1) | copy-start | bytes 221188
  77.4 17.7 %copy-start.1 = (bf16[32,1152]{1,0:T(8,128)(2,1)S(1)}, bf16[32,1152]{1,0:T(8,128)(2,1)}, u32[]{:S(2)}) copy-start(bf16[32,1152]{1,0:T(8,128)(2,1)} %texts_ref.1) | copy-start | bytes 221188
  79.2 15.9 %all-to-all-start.3 = ((bf16[8,32,1152]{2,1,0:T(8,128)(2,1)}), bf16[8,32,1152]{2,1,0:T(8,128)(2,1)S(1)}, u32[]{:S(2)}, u32[]{:S(2)}) async-start(bf16[8,32,1152]{2,1,0:T(8,128)(2,1)} %shard_map.49), calls=%async_computation.3 | async-start | bytes 1179648 | tf_op jit(solution)/shard_map/all_to_all | solution.py:357
  83.8 11.3 %collective-permute-start.4 = (bf16[32,1152]{1,0:T(8,128)(2,1)S(1)}, bf16[32,1152]{1,0:T(8,128)(2,1)S(1)}, u32[]{:S(2)}, u32[]{:S(2)}) collective-permute-start(bf16[32,1152]{1,0:T(8,128)(2,1)S(1)} %get-tuple-element.9), channel_id=1, source_target_pairs={{0,264},{1,265},{2,266},{3,267},{4,268},{5,269},{6,270},{7,271},{8... | collective-permute-start | bytes 221192 | tf_op jit(solution)/shard_map/ppermute | solution.py:367

commit v8 on v7

--- a/solution.py
+++ b/solution.py
@@ -205,8 +205,8 @@
             out_ref[block * size : (block + 1) * size] = total.astype(out_ref.dtype)
             continue
         stage_ref, sems = refs
-        for half in range(2):
-            rows = slice(half * size // 2, (half + 1) * size // 2)
+        for half, (start, end) in enumerate(((0, size // 2), (size // 2, 3 * size // 4), (3 * size // 4, size))):
+            rows = slice(start, end)
             terms = jnp.dot(
                 coef[rows], block_of(theirs[-1], None), preferred_element_type=jnp.float32
             )
@@ -255,7 +255,7 @@
     if load:
         scratch += [pltpu.VMEM(theirs[-1].shape, jnp.bfloat16), pltpu.SemaphoreType.DMA(())]
     if kind == "line":
-        scratch += [pltpu.VMEM(shape, dtype), pltpu.SemaphoreType.DMA((2,))]
+        scratch += [pltpu.VMEM(shape, dtype), pltpu.SemaphoreType.DMA((3,))]
     return pl.pallas_call(
         functools.partial(
             pull_kernel,

time: 96.7 us -> 96.6 us (level)
  no operation moved by 1% of the time
where the time goes in v8:
time: 96.6 us; the launch traced here: 95.9 us
  starting transfers between devices  41.2 us (43%)
  waiting for transfers between devices  35.9 us (37%)
  Pallas kernels  16.7 us (17%)
  other arithmetic  1.28 us (1%)
    all_to_all x4, starting transfers between devices, trade(): lax.all_to_all(blocks, AXES, split_axis=0, concat_axis=0, axis_index_grou...  27.1 us
    ppermute x4, waiting for transfers between devices, swap_x(): return lax.ppermute(block, AXES, across_x(role))  19.4 us
    all_to_all x4, waiting for transfers between devices, trade(): lax.all_to_all(blocks, AXES, split_axis=0, concat_axis=0, axis_index_grou...  16.2 us
    pallas_call x4, Pallas kernels, pull(): pl.pallas_call(functools.partial(pull_kernel, halves, len(theirs), load,...  11.5 us
    ppermute x4, starting transfers between devices, swap_x(): return lax.ppermute(block, AXES, across_x(role))  10.2 us
    pallas_call x1, Pallas kernels, open_rows(): pl.pallas_call(open_kernel, out_shape=(pltpu.HBM((LINE, *shape), jnp.bflo...  1.94 us
  transfers between devices with their start and end apart: 10, of which 8 were waited for; matrix products, arithmetic and copies ran while one was open for 1% of the time, Pallas kernels for 12%

profile of v8, /device:TPU:6, one launch (start us, length us, event | category | flops | bytes accessed | tf_op | source)
XLA Modules:
  0.0 95.9 jit_solution(11523189896036497000)
XLA Ops:
  0.6 1.9 %shard_map.41 = (bf16[8,32,1152]{2,1,0:T(8,128)(2,1)}, bf16[32,1152]{1,0:T(8,128)(2,1)S(1)}) custom-call(s32[1]{0:T(128)} %bitcast.core_ref, bf16[32,1152]{1,0:T(8,128)(2,1)} %images_ref.1, bf16[32,1152]{1,0:T(8,128)(2,1)} %texts_ref.1), custom_call_target="tpu_custom_call" | custom-call | tf_op jit(solution)/shard_map/pallas_call | solution.py:102
  2.6 10.3 %all-to-all-start.1 = ((bf16[8,32,1152]{2,1,0:T(8,128)(2,1)}), bf16[8,32,1152]{2,1,0:T(8,128)(2,1)S(1)}, u32[]{:S(2)}, u32[]{:S(2)}) async-start(bf16[8,32,1152]{2,1,0:T(8,128)(2,1)} %get-tuple-element.7), calls=%async_computation.1 | async-start | bytes 1179648 | tf_op jit(solution)/shard_map/all_to_all | solution.py:357
  12.9 2.4 %collective-permute-start = (bf16[32,1152]{1,0:T(8,128)(2,1)S(1)}, bf16[32,1152]{1,0:T(8,128)(2,1)S(1)}, u32[]{:S(2)}, u32[]{:S(2)}) collective-permute-start(bf16[32,1152]{1,0:T(8,128)(2,1)S(1)} %get-tuple-element.6.near_ref), channel_id=1, source_target_pairs={{0,264},{1,265},{2,266},{3,267},{4,268},{5,269},{6,270},{7,271},{8... | collective-permute-start | bytes 221192 | tf_op jit(solution)/shard_map/ppermute | solution.py:367
  15.3 5.1 %collective-permute-done.far_ref = bf16[32,1152]{1,0:T(8,128)(2,1)S(1)} collective-permute-done((bf16[32,1152]{1,0:T(8,128)(2,1)S(1)}, bf16[32,1152]{1,0:T(8,128)(2,1)S(1)}, u32[]{:S(2)}, u32[]{:S(2)}) %collective-permute-start) | collective-permute-done | bytes 73760 | tf_op jit(solution)/shard_map/ppermute | solution.py:367
  20.4 1.2 %shard_map.42.refs_1_ = bf16[8,64,1152]{2,1,0:T(8,128)(2,1)} custom-call(bf16[32,1152]{1,0:T(8,128)(2,1)S(1)} %get-tuple-element.6.near_ref, bf16[32,1152]{1,0:T(8,128)(2,1)S(1)} %collective-permute-done.far_ref), custom_call_target="tpu_custom_call" | custom-call | tf_op jit(solution)/shard_map/pallas_call | solution.py:127
  21.5 2.8 %all-to-all-done.1 = bf16[8,32,1152]{2,1,0:T(8,128)(2,1)S(1)} async-done(((bf16[8,32,1152]{2,1,0:T(8,128)(2,1)}), bf16[8,32,1152]{2,1,0:T(8,128)(2,1)S(1)}, u32[]{:S(2)}, u32[]{:S(2)}) %all-to-all-start.1) | async-done | bytes 589856 | tf_op jit(solution)/shard_map/all_to_all | solution.py:357
  24.3 7.1 %all-to-all-start = ((bf16[8,64,1152]{2,1,0:T(8,128)(2,1)}), bf16[8,64,1152]{2,1,0:T(8,128)(2,1)S(1)}, u32[]{:S(2)}, u32[]{:S(2)}) async-start(bf16[8,64,1152]{2,1,0:T(8,128)(2,1)} %shard_map.42.refs_1_), calls=%async_computation | async-start | bytes 2359296 | tf_op jit(solution)/shard_map/all_to_all | solution.py:357
  31.4 2.7 %collective-permute-start.2 = (bf16[256,1152]{1,0:T(8,128)(2,1)S(1)}, bf16[256,1152]{1,0:T(8,128)(2,1)S(1)}, u32[]{:S(2)}, u32[]{:S(2)}) collective-permute-start(bf16[256,1152]{1,0:T(8,128)(2,1)S(1)} %shard_map.43.refs_2_.refs_1_), channel_id=1, source_target_pairs={{0,8},{1,9},{2,10},{3,11},{4,12},{5,13},{6,14},{7,15},{8,0},{9,1},... | collective-permute-start | bytes 1769480 | tf_op jit(solution)/shard_map/ppermute | solution.py:367
  34.2 9.0 %collective-permute-done.2.refs_3_.refs_0_ = bf16[256,1152]{1,0:T(8,128)(2,1)S(1)} collective-permute-done((bf16[256,1152]{1,0:T(8,128)(2,1)S(1)}, bf16[256,1152]{1,0:T(8,128)(2,1)S(1)}, u32[]{:S(2)}, u32[]{:S(2)}) %collective-permute-start.2) | collective-permute-done | bytes 589856 | tf_op jit(solution)/shard_map/ppermute | solution.py:367
  43.2 1.1 %pad_maximum_fusion = bf16[512,1152]{1,0:T(8,128)(2,1)} fusion(bf16[256,1152]{1,0:T(8,128)(2,1)S(1)} %collective-permute-done.2.refs_3_.refs_0_, bf16[256,1152]{1,0:T(8,128)(2,1)S(1)} %shard_map.43.refs_2_.refs_1_), kind=kLoop, calls=%fused_computation | loop fusion | flops 2359296 | bytes 2359296 | tf_op jit(solution)/shard_map/concatenate | solution.py:393
  44.3 1.9 %collective-permute-start.3 = (bf16[512,1152]{1,0:T(8,128)(2,1)}, bf16[512,1152]{1,0:T(8,128)(2,1)}, u32[]{:S(2)}, u32[]{:S(2)}) collective-permute-start(bf16[512,1152]{1,0:T(8,128)(2,1)} %pad_maximum_fusion), channel_id=1, source_target_pairs={{0,16},{16,0},{1,17},{17,1},{2,18},{18,2},{3,19},{19,3},{4,20},{20... | collective-permute-start | bytes 3538952 | tf_op jit(solution)/shard_map/ppermute | solution.py:393
  46.2 2.8 %all-to-all-done.refs_1_.refs_0_.refs_2_ = bf16[8,64,1152]{2,1,0:T(8,128)(2,1)S(1)} async-done(((bf16[8,64,1152]{2,1,0:T(8,128)(2,1)}), bf16[8,64,1152]{2,1,0:T(8,128)(2,1)S(1)}, u32[]{:S(2)}, u32[]{:S(2)}) %all-to-all-start) | async-done | bytes 1179680 | tf_op jit(solution)/shard_map/all_to_all | solution.py:357
  49.0 1.9 %collective-permute-start.1 = (bf16[512,1152]{1,0:T(8,128)(2,1)S(1)}, bf16[512,1152]{1,0:T(8,128)(2,1)S(1)}, u32[]{:S(2)}, u32[]{:S(2)}) collective-permute-start(bf16[512,1152]{1,0:T(8,128)(2,1)S(1)} %bitcast.6), channel_id=1, source_target_pairs={{0,16},{16,0},{1,17},{17,1},{2,18},{18,2},{3,19},{19,3},{4,20},{20... | collective-permute-start | bytes 3538952 | tf_op jit(solution)/shard_map/ppermute | solution.py:398
  51.0 0.1 pad_add_fusion.1.refs_0_
  51.1 0.0 collective-permute-done.3.refs_4_.refs_3_.refs_2_
  51.1 2.4 %shard_map.44.refs_2_ = bf16[512,1152]{1,0:T(8,128)(2,1)S(1)} custom-call(s32[3]{0:T(128)S(1)} %pad_add_fusion.1.refs_0_, bf16[8,64,1152]{2,1,0:T(8,128)(2,1)S(1)} %all-to-all-done.refs_1_.refs_0_.refs_2_, bf16[256,1152]{1,0:T(8,128)(2,1)S(1)} %shard_map.43.refs_2_.refs_1_, bf16[256,1152]{1,0:T(8,128)(2,1)S(1)} %collective-permute-done.2.refs_3_.refs_0_, ...), custom_call_target="tpu_custom_call" | custom-call | flops 1207959552 | bytes 4718592 | tf_op jit(solution)/shard_map/pallas_call | solution.py:259
  53.5 0.3 collective-permute-done.1.refs_1_
  53.8 2.4 %shard_map.45 = bf16[512,1152]{1,0:T(8,128)(2,1)} custom-call(bf16[8,64,1152]{2,1,0:T(8,128)(2,1)S(1)} %all-to-all-done.refs_1_.refs_0_.refs_2_, bf16[512,1152]{1,0:T(8,128)(2,1)S(1)} %collective-permute-done.1.refs_1_, bf16[512,1152]{1,0:T(8,128)(2,1)S(1)} %shard_map.44.refs_2_), custom_call_target="tpu_custom_call" | custom-call | flops 1207959552 | bytes 4718592 | tf_op jit(solution)/shard_map/pallas_call | solution.py:259
  56.2 5.2 %all-to-all-start.2 = ((bf16[8,64,1152]{2,1,0:T(8,128)(2,1)}), bf16[8,64,1152]{2,1,0:T(8,128)(2,1)S(1)}, u32[]{:S(2)}, u32[]{:S(2)}) async-start(bf16[8,64,1152]{2,1,0:T(8,128)(2,1)} %bitcast.8), calls=%async_computation.2 | async-start | bytes 2359296 | tf_op jit(solution)/shard_map/all_to_all | solution.py:357
  61.4 3.1 %shard_map.48 = bf16[256,1152]{1,0:T(8,128)(2,1)S(1)} custom-call(bf16[256,1152]{1,0:T(8,128)(2,1)S(1)} %collective-permute-done.2.refs_3_.refs_0_, bf16[8,64,1152]{2,1,0:T(8,128)(2,1)S(1)} %all-to-all-done.refs_1_.refs_0_.refs_2_, bf16[512,1152]{1,0:T(8,128)(2,1)} %collective-permute-done.3.refs_4_.refs_3_.refs_2_), custom_call_target="tpu_custom_call" | custom-call | flops 1207959552 | bytes 2359296 | tf_op jit(solution)/shard_map/pallas_call | solution.py:259
  64.5 2.7 %collective-permute-start.5 = (bf16[256,1152]{1,0:T(8,128)(2,1)S(1)}, bf16[256,1152]{1,0:T(8,128)(2,1)S(1)}, u32[]{:S(2)}, u32[]{:S(2)}) collective-permute-start(bf16[256,1152]{1,0:T(8,128)(2,1)S(1)} %shard_map.48), channel_id=1, source_target_pairs={{0,8},{1,9},{2,10},{3,11},{4,12},{5,13},{6,14},{7,15},{8,0},{9,1},... | collective-permute-start | bytes 1769480 | tf_op jit(solution)/shard_map/ppermute | solution.py:367
  67.3 0.1 pad_add_fusion.refs_0_
  67.4 3.6 %shard_map.47.one_ref = f32[256,1152]{1,0:T(8,128)S(1)} custom-call(s32[3]{0:T(128)S(1)} %pad_add_fusion.refs_0_, bf16[256,1152]{1,0:T(8,128)(2,1)S(1)} %shard_map.43.refs_2_.refs_1_, bf16[8,64,1152]{2,1,0:T(8,128)(2,1)S(1)} %all-to-all-done.refs_1_.refs_0_.refs_2_, bf16[512,1152]{1,0:T(8,128)(2,1)} %collective-permute-done.3.refs_4_.refs_3_.refs_2_), custom_call_target="tpu_custom_call" | custom-call | flops 1207959552 | bytes 2359296 | tf_op jit(solution)/shard_map/pallas_call | solution.py:259
  71.0 5.3 %collective-permute-done.5.two_ref = bf16[256,1152]{1,0:T(8,128)(2,1)S(1)} collective-permute-done((bf16[256,1152]{1,0:T(8,128)(2,1)S(1)}, bf16[256,1152]{1,0:T(8,128)(2,1)S(1)}, u32[]{:S(2)}, u32[]{:S(2)}) %collective-permute-start.5) | collective-permute-done | bytes 589856 | tf_op jit(solution)/shard_map/ppermute | solution.py:367
  76.3 0.9 shard_map.49
  77.3 0.0 copy-start
  77.3 0.0 copy-start.1
  77.3 1.8 %all-to-all-done.2.back_ref = bf16[8,64,1152]{2,1,0:T(8,128)(2,1)S(1)} async-done(((bf16[8,64,1152]{2,1,0:T(8,128)(2,1)}), bf16[8,64,1152]{2,1,0:T(8,128)(2,1)S(1)}, u32[]{:S(2)}, u32[]{:S(2)}) %all-to-all-start.2) | async-done | bytes 1179680 | tf_op jit(solution)/shard_map/all_to_all | solution.py:357
  79.1 4.5 %all-to-all-start.3 = ((bf16[8,32,1152]{2,1,0:T(8,128)(2,1)}), bf16[8,32,1152]{2,1,0:T(8,128)(2,1)S(1)}, u32[]{:S(2)}, u32[]{:S(2)}) async-start(bf16[8,32,1152]{2,1,0:T(8,128)(2,1)} %shard_map.49), calls=%async_computation.3 | async-start | bytes 1179648 | tf_op jit(solution)/shard_map/all_to_all | solution.py:357
  83.5 0.2 shard_map.46
  83.7 2.4 %collective-permute-start.4 = (bf16[32,1152]{1,0:T(8,128)(2,1)S(1)}, bf16[32,1152]{1,0:T(8,128)(2,1)S(1)}, u32[]{:S(2)}, u32[]{:S(2)}) collective-permute-start(bf16[32,1152]{1,0:T(8,128)(2,1)S(1)} %get-tuple-element.9), channel_id=1, source_target_pairs={{0,264},{1,265},{2,266},{3,267},{4,268},{5,269},{6,270},{7,271},{8... | collective-permute-start | bytes 221192 | tf_op jit(solution)/shard_map/ppermute | solution.py:367
  86.1 8.9 %all-to-all-done.3.back_ref = bf16[8,32,1152]{2,1,0:T(8,128)(2,1)S(1)} async-done(((bf16[8,32,1152]{2,1,0:T(8,128)(2,1)}), bf16[8,32,1152]{2,1,0:T(8,128)(2,1)S(1)}, u32[]{:S(2)}, u32[]{:S(2)}) %all-to-all-start.3) | async-done | bytes 589856 | tf_op jit(solution)/shard_map/all_to_all | solution.py:357
  94.9 0.0 collective-permute-done.4.far_ref
  94.9 0.0 copy-done
  94.9 0.0 copy-done.1
  94.9 0.9 shard_map.50
  (1 shorter events, 0.0 us)
Async XLA Ops:
  2.6 21.7 %all-to-all-start.1 = ((bf16[8,32,1152]{2,1,0:T(8,128)(2,1)}), bf16[8,32,1152]{2,1,0:T(8,128)(2,1)S(1)}, u32[]{:S(2)}, u32[]{:S(2)}) async-start(bf16[8,32,1152]{2,1,0:T(8,128)(2,1)} %get-tuple-element.7), calls=%async_computation.1 | async-start | bytes 1179648 | tf_op jit(solution)/shard_map/all_to_all | solution.py:357
  12.9 7.4 %collective-permute-start = (bf16[32,1152]{1,0:T(8,128)(2,1)S(1)}, bf16[32,1152]{1,0:T(8,128)(2,1)S(1)}, u32[]{:S(2)}, u32[]{:S(2)}) collective-permute-start(bf16[32,1152]{1,0:T(8,128)(2,1)S(1)} %get-tuple-element.6.near_ref), channel_id=1, source_target_pairs={{0,264},{1,265},{2,266},{3,267},{4,268},{5,269},{6,270},{7,271},{8... | collective-permute-start | bytes 221192 | tf_op jit(solution)/shard_map/ppermute | solution.py:367
  24.3 24.7 %all-to-all-start = ((bf16[8,64,1152]{2,1,0:T(8,128)(2,1)}), bf16[8,64,1152]{2,1,0:T(8,128)(2,1)S(1)}, u32[]{:S(2)}, u32[]{:S(2)}) async-start(bf16[8,64,1152]{2,1,0:T(8,128)(2,1)} %shard_map.42.refs_1_), calls=%async_computation | async-start | bytes 2359296 | tf_op jit(solution)/shard_map/all_to_all | solution.py:357
  31.4 11.8 %collective-permute-start.2 = (bf16[256,1152]{1,0:T(8,128)(2,1)S(1)}, bf16[256,1152]{1,0:T(8,128)(2,1)S(1)}, u32[]{:S(2)}, u32[]{:S(2)}) collective-permute-start(bf16[256,1152]{1,0:T(8,128)(2,1)S(1)} %shard_map.43.refs_2_.refs_1_), channel_id=1, source_target_pairs={{0,8},{1,9},{2,10},{3,11},{4,12},{5,13},{6,14},{7,15},{8,0},{9,1},... | collective-permute-start | bytes 1769480 | tf_op jit(solution)/shard_map/ppermute | solution.py:367
  44.3 6.8 %collective-permute-start.3 = (bf16[512,1152]{1,0:T(8,128)(2,1)}, bf16[512,1152]{1,0:T(8,128)(2,1)}, u32[]{:S(2)}, u32[]{:S(2)}) collective-permute-start(bf16[512,1152]{1,0:T(8,128)(2,1)} %pad_maximum_fusion), channel_id=1, source_target_pairs={{0,16},{16,0},{1,17},{17,1},{2,18},{18,2},{3,19},{19,3},{4,20},{20... | collective-permute-start | bytes 3538952 | tf_op jit(solution)/shard_map/ppermute | solution.py:393
  49.0 4.7 %collective-permute-start.1 = (bf16[512,1152]{1,0:T(8,128)(2,1)S(1)}, bf16[512,1152]{1,0:T(8,128)(2,1)S(1)}, u32[]{:S(2)}, u32[]{:S(2)}) collective-permute-start(bf16[512,1152]{1,0:T(8,128)(2,1)S(1)} %bitcast.6), channel_id=1, source_target_pairs={{0,16},{16,0},{1,17},{17,1},{2,18},{18,2},{3,19},{19,3},{4,20},{20... | collective-permute-start | bytes 3538952 | tf_op jit(solution)/shard_map/ppermute | solution.py:398
  56.2 22.8 %all-to-all-start.2 = ((bf16[8,64,1152]{2,1,0:T(8,128)(2,1)}), bf16[8,64,1152]{2,1,0:T(8,128)(2,1)S(1)}, u32[]{:S(2)}, u32[]{:S(2)}) async-start(bf16[8,64,1152]{2,1,0:T(8,128)(2,1)} %bitcast.8), calls=%async_computation.2 | async-start | bytes 2359296 | tf_op jit(solution)/shard_map/all_to_all | solution.py:357
  64.5 11.8 %collective-permute-start.5 = (bf16[256,1152]{1,0:T(8,128)(2,1)S(1)}, bf16[256,1152]{1,0:T(8,128)(2,1)S(1)}, u32[]{:S(2)}, u32[]{:S(2)}) collective-permute-start(bf16[256,1152]{1,0:T(8,128)(2,1)S(1)} %shard_map.48), channel_id=1, source_target_pairs={{0,8},{1,9},{2,10},{3,11},{4,12},{5,13},{6,14},{7,15},{8,0},{9,1},... | collective-permute-start | bytes 1769480 | tf_op jit(solution)/shard_map/ppermute | solution.py:367
  77.3 17.7 %copy-start = (bf16[32,1152]{1,0:T(8,128)(2,1)S(1)}, bf16[32,1152]{1,0:T(8,128)(2,1)}, u32[]{:S(2)}) copy-start(bf16[32,1152]{1,0:T(8,128)(2,1)} %images_ref.1) | copy-start | bytes 221188
  77.3 17.7 %copy-start.1 = (bf16[32,1152]{1,0:T(8,128)(2,1)S(1)}, bf16[32,1152]{1,0:T(8,128)(2,1)}, u32[]{:S(2)}) copy-start(bf16[32,1152]{1,0:T(8,128)(2,1)} %texts_ref.1) | copy-start | bytes 221188
  79.1 15.9 %all-to-all-start.3 = ((bf16[8,32,1152]{2,1,0:T(8,128)(2,1)}), bf16[8,32,1152]{2,1,0:T(8,128)(2,1)S(1)}, u32[]{:S(2)}, u32[]{:S(2)}) async-start(bf16[8,32,1152]{2,1,0:T(8,128)(2,1)} %shard_map.49), calls=%async_computation.3 | async-start | bytes 1179648 | tf_op jit(solution)/shard_map/all_to_all | solution.py:357
  83.7 11.3 %collective-permute-start.4 = (bf16[32,1152]{1,0:T(8,128)(2,1)S(1)}, bf16[32,1152]{1,0:T(8,128)(2,1)S(1)}, u32[]{:S(2)}, u32[]{:S(2)}) collective-permute-start(bf16[32,1152]{1,0:T(8,128)(2,1)S(1)} %get-tuple-element.9), channel_id=1, source_target_pairs={{0,264},{1,265},{2,266},{3,267},{4,268},{5,269},{6,270},{7,271},{8... | collective-permute-start | bytes 221192 | tf_op jit(solution)/shard_map/ppermute | solution.py:367

commit v9 on v7

--- a/solution.py
+++ b/solution.py
@@ -325,23 +325,38 @@
     )(back)
 
 
-def close_kernel(core_ref, near_ref, far_ref, back_ref, images_ref, texts_ref, img_ref, txt_ref):
+def q_grad_kernel(core_ref, near_ref, far_ref, images_ref, texts_ref, out_ref):
+    raw = jnp.where(core_ref[0] == 0, texts_ref[...], images_ref[...])
+    out_ref[...] = raw_grad(near_ref[...] + far_ref[...].astype(jnp.float32), raw)
+
+
+def q_grad(core, near, far, images, texts):
+    return pl.pallas_call(
+        q_grad_kernel,
+        out_shape=jax.ShapeDtypeStruct(near.shape, jnp.float32),
+        in_specs=[IN_SMEM] + [IN_VMEM] * 4,
+        out_specs=IN_VMEM,
+        compiler_params=PARAMS,
+    )(core, near, far, images, texts)
+
+
+def close_kernel(core_ref, q_ref, back_ref, images_ref, texts_ref, img_ref, txt_ref):
     first = core_ref[0] == 0
-    q_sum = near_ref[...] + far_ref[...].astype(jnp.float32)
-    p_sum = line_sum(back_ref, 0, near_ref.shape[0])
-    img_ref[...] = raw_grad(jnp.where(first, p_sum, q_sum), images_ref[...])
-    txt_ref[...] = raw_grad(jnp.where(first, q_sum, p_sum), texts_ref[...])
-
-
-def close_rows(core, near, far, back, images, texts):
-    shape = jax.ShapeDtypeStruct(near.shape, jnp.float32)
+    raw = jnp.where(first, images_ref[...], texts_ref[...])
+    grad = raw_grad(line_sum(back_ref, 0, q_ref.shape[0]), raw)
+    img_ref[...] = jnp.where(first, grad, q_ref[...])
+    txt_ref[...] = jnp.where(first, q_ref[...], grad)
+
+
+def close_rows(core, q, back, images, texts):
+    shape = jax.ShapeDtypeStruct(q.shape, jnp.float32)
     return pl.pallas_call(
         close_kernel,
         out_shape=(shape, shape),
-        in_specs=[IN_SMEM] + [IN_VMEM] * 5,
+        in_specs=[IN_SMEM] + [IN_VMEM] * 4,
         out_specs=(IN_VMEM, IN_VMEM),
         compiler_params=PARAMS,
-    )(core, near, far, back, images, texts)
+    )(core, q, back, images, texts)
 
 
 def in_hbm(array):
@@ -405,7 +420,8 @@
     back_p = swap_x(pull([(far_p, None)], others, load=True, dtype=bf), p_role)
     near_p = pull([(near_p, None)], others, at=at_pq, labelled=(0, 0), load=True)
     back_p = trade(add_rows(near_p, back_p), p_role, P_ORDER)
-    return close_rows(core, near, far, back_p, images, texts)
+    q = q_grad(core, near, far, images, texts)
+    return close_rows(core, q, back_p, images, texts)
 
 
 def solution(mesh):

time: 96.7 us -> 96.7 us (level)
    all_to_all x4, waiting for transfers between devices: 16.2 us -> 10.9 us  [trade(): lax.all_to_all(blocks, AXES, split_axis=0, concat_axis=0, axis_index_grou...]
    ppermute x4, waiting for transfers between devices: 19.4 us -> 24.5 us  [swap_x(): return lax.ppermute(block, AXES, across_x(role))]
  transfers between devices with their start and end apart: 10 -> 10, of which waited for: 8 -> 9; matrix products, arithmetic and copies ran while one was open for 1% -> 1% of each run, Pallas kernels for 12% -> 12%
where the time goes in v9:
time: 96.7 us; the launch traced here: 96 us
  starting transfers between devices  41.2 us (43%)
  waiting for transfers between devices  35.7 us (37%)
  Pallas kernels  17 us (18%)
  other arithmetic  1.28 us (1%)
    all_to_all x4, starting transfers between devices, trade(): lax.all_to_all(blocks, AXES, split_axis=0, concat_axis=0, axis_index_grou...  27.1 us
    ppermute x4, waiting for transfers between devices, swap_x(): return lax.ppermute(block, AXES, across_x(role))  24.5 us
    pallas_call x4, Pallas kernels, pull(): pl.pallas_call(functools.partial(pull_kernel, halves, len(theirs), load,...  11.6 us
    all_to_all x4, waiting for transfers between devices, trade(): lax.all_to_all(blocks, AXES, split_axis=0, concat_axis=0, axis_index_grou...  10.9 us
    ppermute x4, starting transfers between devices, swap_x(): return lax.ppermute(block, AXES, across_x(role))  10.3 us
    pallas_call x1, Pallas kernels, open_rows(): pl.pallas_call(open_kernel, out_shape=(pltpu.HBM((LINE, *shape), jnp.bflo...  1.94 us
  transfers between devices with their start and end apart: 10, of which 9 were waited for; matrix products, arithmetic and copies ran while one was open for 1% of the time, Pallas kernels for 12%

profile of v9, /device:TPU:6, one launch (start us, length us, event | category | flops | bytes accessed | tf_op | source)
XLA Modules:
  0.0 96.0 jit_solution(3800994946147451050)
XLA Ops:
  0.6 1.9 %shard_map.41 = (bf16[8,32,1152]{2,1,0:T(8,128)(2,1)}, bf16[32,1152]{1,0:T(8,128)(2,1)S(1)}) custom-call(s32[1]{0:T(128)} %bitcast.core_ref, bf16[32,1152]{1,0:T(8,128)(2,1)} %images_ref.3, bf16[32,1152]{1,0:T(8,128)(2,1)} %texts_ref.3), custom_call_target="tpu_custom_call" | custom-call | tf_op jit(solution)/shard_map/pallas_call | solution.py:102
  2.6 10.3 %all-to-all-start.1 = ((bf16[8,32,1152]{2,1,0:T(8,128)(2,1)}), bf16[8,32,1152]{2,1,0:T(8,128)(2,1)S(1)}, u32[]{:S(2)}, u32[]{:S(2)}) async-start(bf16[8,32,1152]{2,1,0:T(8,128)(2,1)} %get-tuple-element.7), calls=%async_computation.1 | async-start | bytes 1179648 | tf_op jit(solution)/shard_map/all_to_all | solution.py:372
  12.9 2.4 %collective-permute-start = (bf16[32,1152]{1,0:T(8,128)(2,1)S(1)}, bf16[32,1152]{1,0:T(8,128)(2,1)S(1)}, u32[]{:S(2)}, u32[]{:S(2)}) collective-permute-start(bf16[32,1152]{1,0:T(8,128)(2,1)S(1)} %get-tuple-element.6.near_ref), channel_id=1, source_target_pairs={{0,264},{1,265},{2,266},{3,267},{4,268},{5,269},{6,270},{7,271},{8... | collective-permute-start | bytes 221192 | tf_op jit(solution)/shard_map/ppermute | solution.py:382
  15.3 5.1 %collective-permute-done.far_ref = bf16[32,1152]{1,0:T(8,128)(2,1)S(1)} collective-permute-done((bf16[32,1152]{1,0:T(8,128)(2,1)S(1)}, bf16[32,1152]{1,0:T(8,128)(2,1)S(1)}, u32[]{:S(2)}, u32[]{:S(2)}) %collective-permute-start) | collective-permute-done | bytes 73760 | tf_op jit(solution)/shard_map/ppermute | solution.py:382
  20.4 1.2 %shard_map.42.refs_1_ = bf16[8,64,1152]{2,1,0:T(8,128)(2,1)} custom-call(bf16[32,1152]{1,0:T(8,128)(2,1)S(1)} %get-tuple-element.6.near_ref, bf16[32,1152]{1,0:T(8,128)(2,1)S(1)} %collective-permute-done.far_ref), custom_call_target="tpu_custom_call" | custom-call | tf_op jit(solution)/shard_map/pallas_call | solution.py:127
  21.5 2.8 %all-to-all-done.1 = bf16[8,32,1152]{2,1,0:T(8,128)(2,1)S(1)} async-done(((bf16[8,32,1152]{2,1,0:T(8,128)(2,1)}), bf16[8,32,1152]{2,1,0:T(8,128)(2,1)S(1)}, u32[]{:S(2)}, u32[]{:S(2)}) %all-to-all-start.1) | async-done | bytes 589856 | tf_op jit(solution)/shard_map/all_to_all | solution.py:372
  24.3 7.1 %all-to-all-start = ((bf16[8,64,1152]{2,1,0:T(8,128)(2,1)}), bf16[8,64,1152]{2,1,0:T(8,128)(2,1)S(1)}, u32[]{:S(2)}, u32[]{:S(2)}) async-start(bf16[8,64,1152]{2,1,0:T(8,128)(2,1)} %shard_map.42.refs_1_), calls=%async_computation | async-start | bytes 2359296 | tf_op jit(solution)/shard_map/all_to_all | solution.py:372
  31.4 2.7 %collective-permute-start.2 = (bf16[256,1152]{1,0:T(8,128)(2,1)S(1)}, bf16[256,1152]{1,0:T(8,128)(2,1)S(1)}, u32[]{:S(2)}, u32[]{:S(2)}) collective-permute-start(bf16[256,1152]{1,0:T(8,128)(2,1)S(1)} %shard_map.43.refs_2_.refs_1_), channel_id=1, source_target_pairs={{0,8},{1,9},{2,10},{3,11},{4,12},{5,13},{6,14},{7,15},{8,0},{9,1},... | collective-permute-start | bytes 1769480 | tf_op jit(solution)/shard_map/ppermute | solution.py:382
  34.2 9.0 %collective-permute-done.2.refs_3_.refs_0_ = bf16[256,1152]{1,0:T(8,128)(2,1)S(1)} collective-permute-done((bf16[256,1152]{1,0:T(8,128)(2,1)S(1)}, bf16[256,1152]{1,0:T(8,128)(2,1)S(1)}, u32[]{:S(2)}, u32[]{:S(2)}) %collective-permute-start.2) | collective-permute-done | bytes 589856 | tf_op jit(solution)/shard_map/ppermute | solution.py:382
  43.2 1.1 %pad_maximum_fusion = bf16[512,1152]{1,0:T(8,128)(2,1)} fusion(bf16[256,1152]{1,0:T(8,128)(2,1)S(1)} %collective-permute-done.2.refs_3_.refs_0_, bf16[256,1152]{1,0:T(8,128)(2,1)S(1)} %shard_map.43.refs_2_.refs_1_), kind=kLoop, calls=%fused_computation | loop fusion | flops 2359296 | bytes 2359296 | tf_op jit(solution)/shard_map/concatenate | solution.py:408
  44.3 1.9 %collective-permute-start.3 = (bf16[512,1152]{1,0:T(8,128)(2,1)}, bf16[512,1152]{1,0:T(8,128)(2,1)}, u32[]{:S(2)}, u32[]{:S(2)}) collective-permute-start(bf16[512,1152]{1,0:T(8,128)(2,1)} %pad_maximum_fusion), channel_id=1, source_target_pairs={{0,16},{16,0},{1,17},{17,1},{2,18},{18,2},{3,19},{19,3},{4,20},{20... | collective-permute-start | bytes 3538952 | tf_op jit(solution)/shard_map/ppermute | solution.py:408
  46.2 2.8 %all-to-all-done.refs_1_.refs_0_.refs_2_ = bf16[8,64,1152]{2,1,0:T(8,128)(2,1)S(1)} async-done(((bf16[8,64,1152]{2,1,0:T(8,128)(2,1)}), bf16[8,64,1152]{2,1,0:T(8,128)(2,1)S(1)}, u32[]{:S(2)}, u32[]{:S(2)}) %all-to-all-start) | async-done | bytes 1179680 | tf_op jit(solution)/shard_map/all_to_all | solution.py:372
  49.0 1.9 %collective-permute-start.1 = (bf16[512,1152]{1,0:T(8,128)(2,1)S(1)}, bf16[512,1152]{1,0:T(8,128)(2,1)S(1)}, u32[]{:S(2)}, u32[]{:S(2)}) collective-permute-start(bf16[512,1152]{1,0:T(8,128)(2,1)S(1)} %bitcast.6), channel_id=1, source_target_pairs={{0,16},{16,0},{1,17},{17,1},{2,18},{18,2},{3,19},{19,3},{4,20},{20... | collective-permute-start | bytes 3538952 | tf_op jit(solution)/shard_map/ppermute | solution.py:413
  51.0 0.1 pad_add_fusion.1.refs_0_
  51.1 0.0 collective-permute-done.3.refs_4_.refs_3_.refs_2_
  51.1 2.4 %shard_map.44.refs_2_ = bf16[512,1152]{1,0:T(8,128)(2,1)S(1)} custom-call(s32[3]{0:T(128)S(1)} %pad_add_fusion.1.refs_0_, bf16[8,64,1152]{2,1,0:T(8,128)(2,1)S(1)} %all-to-all-done.refs_1_.refs_0_.refs_2_, bf16[256,1152]{1,0:T(8,128)(2,1)S(1)} %shard_map.43.refs_2_.refs_1_, bf16[256,1152]{1,0:T(8,128)(2,1)S(1)} %collective-permute-done.2.refs_3_.refs_0_, ...), custom_call_target="tpu_custom_call" | custom-call | flops 1207959552 | bytes 4718592 | tf_op jit(solution)/shard_map/pallas_call | solution.py:259
  53.5 0.3 collective-permute-done.1.refs_1_
  53.8 2.5 %shard_map.45 = bf16[512,1152]{1,0:T(8,128)(2,1)} custom-call(bf16[8,64,1152]{2,1,0:T(8,128)(2,1)S(1)} %all-to-all-done.refs_1_.refs_0_.refs_2_, bf16[512,1152]{1,0:T(8,128)(2,1)S(1)} %collective-permute-done.1.refs_1_, bf16[512,1152]{1,0:T(8,128)(2,1)S(1)} %shard_map.44.refs_2_), custom_call_target="tpu_custom_call" | custom-call | flops 1207959552 | bytes 4718592 | tf_op jit(solution)/shard_map/pallas_call | solution.py:259
  56.3 5.2 %all-to-all-start.2 = ((bf16[8,64,1152]{2,1,0:T(8,128)(2,1)}), bf16[8,64,1152]{2,1,0:T(8,128)(2,1)S(1)}, u32[]{:S(2)}, u32[]{:S(2)}) async-start(bf16[8,64,1152]{2,1,0:T(8,128)(2,1)} %bitcast.8), calls=%async_computation.2 | async-start | bytes 2359296 | tf_op jit(solution)/shard_map/all_to_all | solution.py:372
  61.5 3.1 %shard_map.49 = bf16[256,1152]{1,0:T(8,128)(2,1)S(1)} custom-call(bf16[256,1152]{1,0:T(8,128)(2,1)S(1)} %collective-permute-done.2.refs_3_.refs_0_, bf16[8,64,1152]{2,1,0:T(8,128)(2,1)S(1)} %all-to-all-done.refs_1_.refs_0_.refs_2_, bf16[512,1152]{1,0:T(8,128)(2,1)} %collective-permute-done.3.refs_4_.refs_3_.refs_2_), custom_call_target="tpu_custom_call" | custom-call | flops 1207959552 | bytes 2359296 | tf_op jit(solution)/shard_map/pallas_call | solution.py:259
  64.6 2.8 %collective-permute-start.5 = (bf16[256,1152]{1,0:T(8,128)(2,1)S(1)}, bf16[256,1152]{1,0:T(8,128)(2,1)S(1)}, u32[]{:S(2)}, u32[]{:S(2)}) collective-permute-start(bf16[256,1152]{1,0:T(8,128)(2,1)S(1)} %shard_map.49), channel_id=1, source_target_pairs={{0,8},{1,9},{2,10},{3,11},{4,12},{5,13},{6,14},{7,15},{8,0},{9,1},... | collective-permute-start | bytes 1769480 | tf_op jit(solution)/shard_map/ppermute | solution.py:382
  67.4 0.1 pad_add_fusion.refs_0_
  67.5 3.6 %shard_map.48.one_ref = f32[256,1152]{1,0:T(8,128)S(1)} custom-call(s32[3]{0:T(128)S(1)} %pad_add_fusion.refs_0_, bf16[256,1152]{1,0:T(8,128)(2,1)S(1)} %shard_map.43.refs_2_.refs_1_, bf16[8,64,1152]{2,1,0:T(8,128)(2,1)S(1)} %all-to-all-done.refs_1_.refs_0_.refs_2_, bf16[512,1152]{1,0:T(8,128)(2,1)} %collective-permute-done.3.refs_4_.refs_3_.refs_2_), custom_call_target="tpu_custom_call" | custom-call | flops 1207959552 | bytes 2359296 | tf_op jit(solution)/shard_map/pallas_call | solution.py:259
  71.1 5.3 %collective-permute-done.5.two_ref = bf16[256,1152]{1,0:T(8,128)(2,1)S(1)} collective-permute-done((bf16[256,1152]{1,0:T(8,128)(2,1)S(1)}, bf16[256,1152]{1,0:T(8,128)(2,1)S(1)}, u32[]{:S(2)}, u32[]{:S(2)}) %collective-permute-start.5) | collective-permute-done | bytes 589856 | tf_op jit(solution)/shard_map/ppermute | solution.py:382
  76.4 0.9 shard_map.50
  77.3 0.0 copy-start
  77.4 0.0 copy-start.1
  77.4 1.8 %all-to-all-done.2.back_ref = bf16[8,64,1152]{2,1,0:T(8,128)(2,1)S(1)} async-done(((bf16[8,64,1152]{2,1,0:T(8,128)(2,1)}), bf16[8,64,1152]{2,1,0:T(8,128)(2,1)S(1)}, u32[]{:S(2)}, u32[]{:S(2)}) %all-to-all-start.2) | async-done | bytes 1179680 | tf_op jit(solution)/shard_map/all_to_all | solution.py:372
  79.2 4.5 %all-to-all-start.3 = ((bf16[8,32,1152]{2,1,0:T(8,128)(2,1)}), bf16[8,32,1152]{2,1,0:T(8,128)(2,1)S(1)}, u32[]{:S(2)}, u32[]{:S(2)}) async-start(bf16[8,32,1152]{2,1,0:T(8,128)(2,1)} %shard_map.50), calls=%async_computation.3 | async-start | bytes 1179648 | tf_op jit(solution)/shard_map/all_to_all | solution.py:372
  83.6 0.2 shard_map.46
  83.8 2.4 %collective-permute-start.4 = (bf16[32,1152]{1,0:T(8,128)(2,1)S(1)}, bf16[32,1152]{1,0:T(8,128)(2,1)S(1)}, u32[]{:S(2)}, u32[]{:S(2)}) collective-permute-start(bf16[32,1152]{1,0:T(8,128)(2,1)S(1)} %get-tuple-element.9), channel_id=1, source_target_pairs={{0,264},{1,265},{2,266},{3,267},{4,268},{5,269},{6,270},{7,271},{8... | collective-permute-start | bytes 221192 | tf_op jit(solution)/shard_map/ppermute | solution.py:382
  86.2 5.1 %collective-permute-done.4.far_ref = bf16[32,1152]{1,0:T(8,128)(2,1)S(1)} collective-permute-done((bf16[32,1152]{1,0:T(8,128)(2,1)S(1)}, bf16[32,1152]{1,0:T(8,128)(2,1)S(1)}, u32[]{:S(2)}, u32[]{:S(2)}) %collective-permute-start.4) | collective-permute-done | bytes 73760 | tf_op jit(solution)/shard_map/ppermute | solution.py:382
  91.2 0.0 copy-done
  91.2 0.0 copy-done.1
  91.2 0.2 shard_map.47.q_ref
  91.5 3.6 %all-to-all-done.3.back_ref = bf16[8,32,1152]{2,1,0:T(8,128)(2,1)S(1)} async-done(((bf16[8,32,1152]{2,1,0:T(8,128)(2,1)}), bf16[8,32,1152]{2,1,0:T(8,128)(2,1)S(1)}, u32[]{:S(2)}, u32[]{:S(2)}) %all-to-all-start.3) | async-done | bytes 589856 | tf_op jit(solution)/shard_map/all_to_all | solution.py:372
  95.0 0.9 shard_map.51
  (1 shorter events, 0.0 us)
Async XLA Ops:
  2.6 21.7 %all-to-all-start.1 = ((bf16[8,32,1152]{2,1,0:T(8,128)(2,1)}), bf16[8,32,1152]{2,1,0:T(8,128)(2,1)S(1)}, u32[]{:S(2)}, u32[]{:S(2)}) async-start(bf16[8,32,1152]{2,1,0:T(8,128)(2,1)} %get-tuple-element.7), calls=%async_computation.1 | async-start | bytes 1179648 | tf_op jit(solution)/shard_map/all_to_all | solution.py:372
  12.9 7.4 %collective-permute-start = (bf16[32,1152]{1,0:T(8,128)(2,1)S(1)}, bf16[32,1152]{1,0:T(8,128)(2,1)S(1)}, u32[]{:S(2)}, u32[]{:S(2)}) collective-permute-start(bf16[32,1152]{1,0:T(8,128)(2,1)S(1)} %get-tuple-element.6.near_ref), channel_id=1, source_target_pairs={{0,264},{1,265},{2,266},{3,267},{4,268},{5,269},{6,270},{7,271},{8... | collective-permute-start | bytes 221192 | tf_op jit(solution)/shard_map/ppermute | solution.py:382
  24.3 24.7 %all-to-all-start = ((bf16[8,64,1152]{2,1,0:T(8,128)(2,1)}), bf16[8,64,1152]{2,1,0:T(8,128)(2,1)S(1)}, u32[]{:S(2)}, u32[]{:S(2)}) async-start(bf16[8,64,1152]{2,1,0:T(8,128)(2,1)} %shard_map.42.refs_1_), calls=%async_computation | async-start | bytes 2359296 | tf_op jit(solution)/shard_map/all_to_all | solution.py:372
  31.4 11.8 %collective-permute-start.2 = (bf16[256,1152]{1,0:T(8,128)(2,1)S(1)}, bf16[256,1152]{1,0:T(8,128)(2,1)S(1)}, u32[]{:S(2)}, u32[]{:S(2)}) collective-permute-start(bf16[256,1152]{1,0:T(8,128)(2,1)S(1)} %shard_map.43.refs_2_.refs_1_), channel_id=1, source_target_pairs={{0,8},{1,9},{2,10},{3,11},{4,12},{5,13},{6,14},{7,15},{8,0},{9,1},... | collective-permute-start | bytes 1769480 | tf_op jit(solution)/shard_map/ppermute | solution.py:382
  44.3 6.8 %collective-permute-start.3 = (bf16[512,1152]{1,0:T(8,128)(2,1)}, bf16[512,1152]{1,0:T(8,128)(2,1)}, u32[]{:S(2)}, u32[]{:S(2)}) collective-permute-start(bf16[512,1152]{1,0:T(8,128)(2,1)} %pad_maximum_fusion), channel_id=1, source_target_pairs={{0,16},{16,0},{1,17},{17,1},{2,18},{18,2},{3,19},{19,3},{4,20},{20... | collective-permute-start | bytes 3538952 | tf_op jit(solution)/shard_map/ppermute | solution.py:408
  49.0 4.7 %collective-permute-start.1 = (bf16[512,1152]{1,0:T(8,128)(2,1)S(1)}, bf16[512,1152]{1,0:T(8,128)(2,1)S(1)}, u32[]{:S(2)}, u32[]{:S(2)}) collective-permute-start(bf16[512,1152]{1,0:T(8,128)(2,1)S(1)} %bitcast.6), channel_id=1, source_target_pairs={{0,16},{16,0},{1,17},{17,1},{2,18},{18,2},{3,19},{19,3},{4,20},{20... | collective-permute-start | bytes 3538952 | tf_op jit(solution)/shard_map/ppermute | solution.py:413
  56.3 22.8 %all-to-all-start.2 = ((bf16[8,64,1152]{2,1,0:T(8,128)(2,1)}), bf16[8,64,1152]{2,1,0:T(8,128)(2,1)S(1)}, u32[]{:S(2)}, u32[]{:S(2)}) async-start(bf16[8,64,1152]{2,1,0:T(8,128)(2,1)} %bitcast.8), calls=%async_computation.2 | async-start | bytes 2359296 | tf_op jit(solution)/shard_map/all_to_all | solution.py:372
  64.6 11.8 %collective-permute-start.5 = (bf16[256,1152]{1,0:T(8,128)(2,1)S(1)}, bf16[256,1152]{1,0:T(8,128)(2,1)S(1)}, u32[]{:S(2)}, u32[]{:S(2)}) collective-permute-start(bf16[256,1152]{1,0:T(8,128)(2,1)S(1)} %shard_map.49), channel_id=1, source_target_pairs={{0,8},{1,9},{2,10},{3,11},{4,12},{5,13},{6,14},{7,15},{8,0},{9,1},... | collective-permute-start | bytes 1769480 | tf_op jit(solution)/shard_map/ppermute | solution.py:382
  77.3 13.9 %copy-start = (bf16[32,1152]{1,0:T(8,128)(2,1)S(1)}, bf16[32,1152]{1,0:T(8,128)(2,1)}, u32[]{:S(2)}) copy-start(bf16[32,1152]{1,0:T(8,128)(2,1)} %images_ref.3) | copy-start | bytes 221188
  77.4 13.9 %copy-start.1 = (bf16[32,1152]{1,0:T(8,128)(2,1)S(1)}, bf16[32,1152]{1,0:T(8,128)(2,1)}, u32[]{:S(2)}) copy-start(bf16[32,1152]{1,0:T(8,128)(2,1)} %texts_ref.3) | copy-start | bytes 221188
  79.2 15.9 %all-to-all-start.3 = ((bf16[8,32,1152]{2,1,0:T(8,128)(2,1)}), bf16[8,32,1152]{2,1,0:T(8,128)(2,1)S(1)}, u32[]{:S(2)}, u32[]{:S(2)}) async-start(bf16[8,32,1152]{2,1,0:T(8,128)(2,1)} %shard_map.50), calls=%async_computation.3 | async-start | bytes 1179648 | tf_op jit(solution)/shard_map/all_to_all | solution.py:372
  83.8 7.5 %collective-permute-start.4 = (bf16[32,1152]{1,0:T(8,128)(2,1)S(1)}, bf16[32,1152]{1,0:T(8,128)(2,1)S(1)}, u32[]{:S(2)}, u32[]{:S(2)}) collective-permute-start(bf16[32,1152]{1,0:T(8,128)(2,1)S(1)} %get-tuple-element.9), channel_id=1, source_target_pairs={{0,264},{1,265},{2,266},{3,267},{4,268},{5,269},{6,270},{7,271},{8... | collective-permute-start | bytes 221192 | tf_op jit(solution)/shard_map/ppermute | solution.py:382

commit v10 on v7

--- a/solution.py
+++ b/solution.py
@@ -16,7 +16,7 @@
 ALL = P(AXES, None)
 SWAP = [(0, 1), (1, 0)]
 LINE = 8
-P_ORDER = (0, 4, 2, 6, 3, 7, 1, 5)
+P_ORDER = (0, 2, 4, 6, 1, 3, 5, 7)
 Q_ORDER = (0, 2, 4, 6, 1, 3, 5, 7)
 
 IN_VMEM = pl.BlockSpec(memory_space=pltpu.VMEM)

time: 96.7 us -> 96.9 us (level)
  no operation moved by 1% of the time
where the time goes in v10:
time: 96.9 us; the launch traced here: 95.9 us
  starting transfers between devices  41.3 us (43%)
  waiting for transfers between devices  35.7 us (37%)
  Pallas kernels  16.8 us (17%)
  other arithmetic  1.28 us (1%)
    all_to_all x4, starting transfers between devices, trade(): lax.all_to_all(blocks, AXES, split_axis=0, concat_axis=0, axis_index_grou...  27.2 us
    ppermute x4, waiting for transfers between devices, swap_x(): return lax.ppermute(block, AXES, across_x(role))  19.4 us
    all_to_all x4, waiting for transfers between devices, trade(): lax.all_to_all(blocks, AXES, split_axis=0, concat_axis=0, axis_index_grou...  16 us
    pallas_call x4, Pallas kernels, pull(): pl.pallas_call(functools.partial(pull_kernel, halves, len(theirs), load,...  11.6 us
    ppermute x4, starting transfers between devices, swap_x(): return lax.ppermute(block, AXES, across_x(role))  10.2 us
    pallas_call x1, Pallas kernels, open_rows(): pl.pallas_call(open_kernel, out_shape=(pltpu.HBM((LINE, *shape), jnp.bflo...  1.94 us
  transfers between devices with their start and end apart: 10, of which 8 were waited for; matrix products, arithmetic and copies ran while one was open for 1% of the time, Pallas kernels for 12%

profile of v10, /device:TPU:6, one launch (start us, length us, event | category | flops | bytes accessed | tf_op | source)
XLA Modules:
  0.0 95.9 jit_solution(15715502920331985518)
XLA Ops:
  0.6 1.9 %shard_map.41 = (bf16[8,32,1152]{2,1,0:T(8,128)(2,1)}, bf16[32,1152]{1,0:T(8,128)(2,1)S(1)}) custom-call(s32[1]{0:T(128)} %bitcast.core_ref, bf16[32,1152]{1,0:T(8,128)(2,1)} %images_ref.1, bf16[32,1152]{1,0:T(8,128)(2,1)} %texts_ref.1), custom_call_target="tpu_custom_call" | custom-call | tf_op jit(solution)/shard_map/pallas_call | solution.py:102
  2.6 10.3 %all-to-all-start.1 = ((bf16[8,32,1152]{2,1,0:T(8,128)(2,1)}), bf16[8,32,1152]{2,1,0:T(8,128)(2,1)S(1)}, u32[]{:S(2)}, u32[]{:S(2)}) async-start(bf16[8,32,1152]{2,1,0:T(8,128)(2,1)} %get-tuple-element.7), calls=%async_computation.1 | async-start | bytes 1179648 | tf_op jit(solution)/shard_map/all_to_all | solution.py:357
  12.9 2.4 %collective-permute-start = (bf16[32,1152]{1,0:T(8,128)(2,1)S(1)}, bf16[32,1152]{1,0:T(8,128)(2,1)S(1)}, u32[]{:S(2)}, u32[]{:S(2)}) collective-permute-start(bf16[32,1152]{1,0:T(8,128)(2,1)S(1)} %get-tuple-element.6.near_ref), channel_id=1, source_target_pairs={{0,264},{1,265},{2,266},{3,267},{4,268},{5,269},{6,270},{7,271},{8... | collective-permute-start | bytes 221192 | tf_op jit(solution)/shard_map/ppermute | solution.py:367
  15.3 5.1 %collective-permute-done.far_ref = bf16[32,1152]{1,0:T(8,128)(2,1)S(1)} collective-permute-done((bf16[32,1152]{1,0:T(8,128)(2,1)S(1)}, bf16[32,1152]{1,0:T(8,128)(2,1)S(1)}, u32[]{:S(2)}, u32[]{:S(2)}) %collective-permute-start) | collective-permute-done | bytes 73760 | tf_op jit(solution)/shard_map/ppermute | solution.py:367
  20.4 1.2 %shard_map.42.refs_1_ = bf16[8,64,1152]{2,1,0:T(8,128)(2,1)} custom-call(bf16[32,1152]{1,0:T(8,128)(2,1)S(1)} %get-tuple-element.6.near_ref, bf16[32,1152]{1,0:T(8,128)(2,1)S(1)} %collective-permute-done.far_ref), custom_call_target="tpu_custom_call" | custom-call | tf_op jit(solution)/shard_map/pallas_call | solution.py:127
  21.5 2.7 %all-to-all-done.1 = bf16[8,32,1152]{2,1,0:T(8,128)(2,1)S(1)} async-done(((bf16[8,32,1152]{2,1,0:T(8,128)(2,1)}), bf16[8,32,1152]{2,1,0:T(8,128)(2,1)S(1)}, u32[]{:S(2)}, u32[]{:S(2)}) %all-to-all-start.1) | async-done | bytes 589856 | tf_op jit(solution)/shard_map/all_to_all | solution.py:357
  24.2 7.1 %all-to-all-start = ((bf16[8,64,1152]{2,1,0:T(8,128)(2,1)}), bf16[8,64,1152]{2,1,0:T(8,128)(2,1)S(1)}, u32[]{:S(2)}, u32[]{:S(2)}) async-start(bf16[8,64,1152]{2,1,0:T(8,128)(2,1)} %shard_map.42.refs_1_), calls=%async_computation | async-start | bytes 2359296 | tf_op jit(solution)/shard_map/all_to_all | solution.py:357
  31.3 2.7 %collective-permute-start.2 = (bf16[256,1152]{1,0:T(8,128)(2,1)S(1)}, bf16[256,1152]{1,0:T(8,128)(2,1)S(1)}, u32[]{:S(2)}, u32[]{:S(2)}) collective-permute-start(bf16[256,1152]{1,0:T(8,128)(2,1)S(1)} %shard_map.43.refs_2_.refs_1_), channel_id=1, source_target_pairs={{0,8},{1,9},{2,10},{3,11},{4,12},{5,13},{6,14},{7,15},{8,0},{9,1},... | collective-permute-start | bytes 1769480 | tf_op jit(solution)/shard_map/ppermute | solution.py:367
  34.1 9.0 %collective-permute-done.2.refs_3_.refs_0_ = bf16[256,1152]{1,0:T(8,128)(2,1)S(1)} collective-permute-done((bf16[256,1152]{1,0:T(8,128)(2,1)S(1)}, bf16[256,1152]{1,0:T(8,128)(2,1)S(1)}, u32[]{:S(2)}, u32[]{:S(2)}) %collective-permute-start.2) | collective-permute-done | bytes 589856 | tf_op jit(solution)/shard_map/ppermute | solution.py:367
  43.1 1.1 %pad_maximum_fusion = bf16[512,1152]{1,0:T(8,128)(2,1)} fusion(bf16[256,1152]{1,0:T(8,128)(2,1)S(1)} %collective-permute-done.2.refs_3_.refs_0_, bf16[256,1152]{1,0:T(8,128)(2,1)S(1)} %shard_map.43.refs_2_.refs_1_), kind=kLoop, calls=%fused_computation | loop fusion | flops 2359296 | bytes 2359296 | tf_op jit(solution)/shard_map/concatenate | solution.py:393
  44.2 1.9 %collective-permute-start.3 = (bf16[512,1152]{1,0:T(8,128)(2,1)}, bf16[512,1152]{1,0:T(8,128)(2,1)}, u32[]{:S(2)}, u32[]{:S(2)}) collective-permute-start(bf16[512,1152]{1,0:T(8,128)(2,1)} %pad_maximum_fusion), channel_id=1, source_target_pairs={{0,16},{16,0},{1,17},{17,1},{2,18},{18,2},{3,19},{19,3},{4,20},{20... | collective-permute-start | bytes 3538952 | tf_op jit(solution)/shard_map/ppermute | solution.py:393
  46.1 2.8 %all-to-all-done.refs_1_.refs_0_.refs_2_ = bf16[8,64,1152]{2,1,0:T(8,128)(2,1)S(1)} async-done(((bf16[8,64,1152]{2,1,0:T(8,128)(2,1)}), bf16[8,64,1152]{2,1,0:T(8,128)(2,1)S(1)}, u32[]{:S(2)}, u32[]{:S(2)}) %all-to-all-start) | async-done | bytes 1179680 | tf_op jit(solution)/shard_map/all_to_all | solution.py:357
  48.9 1.9 %collective-permute-start.1 = (bf16[512,1152]{1,0:T(8,128)(2,1)S(1)}, bf16[512,1152]{1,0:T(8,128)(2,1)S(1)}, u32[]{:S(2)}, u32[]{:S(2)}) collective-permute-start(bf16[512,1152]{1,0:T(8,128)(2,1)S(1)} %bitcast.6), channel_id=1, source_target_pairs={{0,16},{16,0},{1,17},{17,1},{2,18},{18,2},{3,19},{19,3},{4,20},{20... | collective-permute-start | bytes 3538952 | tf_op jit(solution)/shard_map/ppermute | solution.py:398
  50.9 0.1 pad_add_fusion.1.refs_0_
  51.0 0.0 collective-permute-done.3.refs_4_.refs_3_.refs_2_
  51.0 2.4 %shard_map.44.refs_2_ = bf16[512,1152]{1,0:T(8,128)(2,1)S(1)} custom-call(s32[3]{0:T(128)S(1)} %pad_add_fusion.1.refs_0_, bf16[8,64,1152]{2,1,0:T(8,128)(2,1)S(1)} %all-to-all-done.refs_1_.refs_0_.refs_2_, bf16[256,1152]{1,0:T(8,128)(2,1)S(1)} %shard_map.43.refs_2_.refs_1_, bf16[256,1152]{1,0:T(8,128)(2,1)S(1)} %collective-permute-done.2.refs_3_.refs_0_, ...), custom_call_target="tpu_custom_call" | custom-call | flops 1207959552 | bytes 4718592 | tf_op jit(solution)/shard_map/pallas_call | solution.py:259
  53.4 0.3 collective-permute-done.1.refs_1_
  53.7 2.5 %shard_map.45 = bf16[512,1152]{1,0:T(8,128)(2,1)} custom-call(bf16[8,64,1152]{2,1,0:T(8,128)(2,1)S(1)} %all-to-all-done.refs_1_.refs_0_.refs_2_, bf16[512,1152]{1,0:T(8,128)(2,1)S(1)} %collective-permute-done.1.refs_1_, bf16[512,1152]{1,0:T(8,128)(2,1)S(1)} %shard_map.44.refs_2_), custom_call_target="tpu_custom_call" | custom-call | flops 1207959552 | bytes 4718592 | tf_op jit(solution)/shard_map/pallas_call | solution.py:259
  56.2 5.2 %all-to-all-start.2 = ((bf16[8,64,1152]{2,1,0:T(8,128)(2,1)}), bf16[8,64,1152]{2,1,0:T(8,128)(2,1)S(1)}, u32[]{:S(2)}, u32[]{:S(2)}) async-start(bf16[8,64,1152]{2,1,0:T(8,128)(2,1)} %bitcast.8), calls=%async_computation.2 | async-start | bytes 2359296 | tf_op jit(solution)/shard_map/all_to_all | solution.py:357
  61.4 3.1 %shard_map.48 = bf16[256,1152]{1,0:T(8,128)(2,1)S(1)} custom-call(bf16[256,1152]{1,0:T(8,128)(2,1)S(1)} %collective-permute-done.2.refs_3_.refs_0_, bf16[8,64,1152]{2,1,0:T(8,128)(2,1)S(1)} %all-to-all-done.refs_1_.refs_0_.refs_2_, bf16[512,1152]{1,0:T(8,128)(2,1)} %collective-permute-done.3.refs_4_.refs_3_.refs_2_), custom_call_target="tpu_custom_call" | custom-call | flops 1207959552 | bytes 2359296 | tf_op jit(solution)/shard_map/pallas_call | solution.py:259
  64.5 2.7 %collective-permute-start.5 = (bf16[256,1152]{1,0:T(8,128)(2,1)S(1)}, bf16[256,1152]{1,0:T(8,128)(2,1)S(1)}, u32[]{:S(2)}, u32[]{:S(2)}) collective-permute-start(bf16[256,1152]{1,0:T(8,128)(2,1)S(1)} %shard_map.48), channel_id=1, source_target_pairs={{0,8},{1,9},{2,10},{3,11},{4,12},{5,13},{6,14},{7,15},{8,0},{9,1},... | collective-permute-start | bytes 1769480 | tf_op jit(solution)/shard_map/ppermute | solution.py:367
  67.3 0.1 pad_add_fusion.refs_0_
  67.3 3.6 %shard_map.47.one_ref = f32[256,1152]{1,0:T(8,128)S(1)} custom-call(s32[3]{0:T(128)S(1)} %pad_add_fusion.refs_0_, bf16[256,1152]{1,0:T(8,128)(2,1)S(1)} %shard_map.43.refs_2_.refs_1_, bf16[8,64,1152]{2,1,0:T(8,128)(2,1)S(1)} %all-to-all-done.refs_1_.refs_0_.refs_2_, bf16[512,1152]{1,0:T(8,128)(2,1)} %collective-permute-done.3.refs_4_.refs_3_.refs_2_), custom_call_target="tpu_custom_call" | custom-call | flops 1207959552 | bytes 2359296 | tf_op jit(solution)/shard_map/pallas_call | solution.py:259
  71.0 5.3 %collective-permute-done.5.two_ref = bf16[256,1152]{1,0:T(8,128)(2,1)S(1)} collective-permute-done((bf16[256,1152]{1,0:T(8,128)(2,1)S(1)}, bf16[256,1152]{1,0:T(8,128)(2,1)S(1)}, u32[]{:S(2)}, u32[]{:S(2)}) %collective-permute-start.5) | collective-permute-done | bytes 589856 | tf_op jit(solution)/shard_map/ppermute | solution.py:367
  76.3 0.9 shard_map.49
  77.2 0.0 copy-start
  77.3 0.0 copy-start.1
  77.3 1.8 %all-to-all-done.2.back_ref = bf16[8,64,1152]{2,1,0:T(8,128)(2,1)S(1)} async-done(((bf16[8,64,1152]{2,1,0:T(8,128)(2,1)}), bf16[8,64,1152]{2,1,0:T(8,128)(2,1)S(1)}, u32[]{:S(2)}, u32[]{:S(2)}) %all-to-all-start.2) | async-done | bytes 1179680 | tf_op jit(solution)/shard_map/all_to_all | solution.py:357
  79.1 4.6 %all-to-all-start.3 = ((bf16[8,32,1152]{2,1,0:T(8,128)(2,1)}), bf16[8,32,1152]{2,1,0:T(8,128)(2,1)S(1)}, u32[]{:S(2)}, u32[]{:S(2)}) async-start(bf16[8,32,1152]{2,1,0:T(8,128)(2,1)} %shard_map.49), calls=%async_computation.3 | async-start | bytes 1179648 | tf_op jit(solution)/shard_map/all_to_all | solution.py:357
  83.6 0.2 shard_map.46
  83.8 2.4 %collective-permute-start.4 = (bf16[32,1152]{1,0:T(8,128)(2,1)S(1)}, bf16[32,1152]{1,0:T(8,128)(2,1)S(1)}, u32[]{:S(2)}, u32[]{:S(2)}) collective-permute-start(bf16[32,1152]{1,0:T(8,128)(2,1)S(1)} %get-tuple-element.9), channel_id=1, source_target_pairs={{0,264},{1,265},{2,266},{3,267},{4,268},{5,269},{6,270},{7,271},{8... | collective-permute-start | bytes 221192 | tf_op jit(solution)/shard_map/ppermute | solution.py:367
  86.2 8.8 %all-to-all-done.3.back_ref = bf16[8,32,1152]{2,1,0:T(8,128)(2,1)S(1)} async-done(((bf16[8,32,1152]{2,1,0:T(8,128)(2,1)}), bf16[8,32,1152]{2,1,0:T(8,128)(2,1)S(1)}, u32[]{:S(2)}, u32[]{:S(2)}) %all-to-all-start.3) | async-done | bytes 589856 | tf_op jit(solution)/shard_map/all_to_all | solution.py:357
  94.9 0.0 collective-permute-done.4.far_ref
  94.9 0.0 copy-done
  95.0 0.0 copy-done.1
  95.0 0.9 shard_map.50
  (1 shorter events, 0.0 us)
Async XLA Ops:
  2.6 21.6 %all-to-all-start.1 = ((bf16[8,32,1152]{2,1,0:T(8,128)(2,1)}), bf16[8,32,1152]{2,1,0:T(8,128)(2,1)S(1)}, u32[]{:S(2)}, u32[]{:S(2)}) async-start(bf16[8,32,1152]{2,1,0:T(8,128)(2,1)} %get-tuple-element.7), calls=%async_computation.1 | async-start | bytes 1179648 | tf_op jit(solution)/shard_map/all_to_all | solution.py:357
  12.9 7.4 %collective-permute-start = (bf16[32,1152]{1,0:T(8,128)(2,1)S(1)}, bf16[32,1152]{1,0:T(8,128)(2,1)S(1)}, u32[]{:S(2)}, u32[]{:S(2)}) collective-permute-start(bf16[32,1152]{1,0:T(8,128)(2,1)S(1)} %get-tuple-element.6.near_ref), channel_id=1, source_target_pairs={{0,264},{1,265},{2,266},{3,267},{4,268},{5,269},{6,270},{7,271},{8... | collective-permute-start | bytes 221192 | tf_op jit(solution)/shard_map/ppermute | solution.py:367
  24.2 24.7 %all-to-all-start = ((bf16[8,64,1152]{2,1,0:T(8,128)(2,1)}), bf16[8,64,1152]{2,1,0:T(8,128)(2,1)S(1)}, u32[]{:S(2)}, u32[]{:S(2)}) async-start(bf16[8,64,1152]{2,1,0:T(8,128)(2,1)} %shard_map.42.refs_1_), calls=%async_computation | async-start | bytes 2359296 | tf_op jit(solution)/shard_map/all_to_all | solution.py:357
  31.3 11.8 %collective-permute-start.2 = (bf16[256,1152]{1,0:T(8,128)(2,1)S(1)}, bf16[256,1152]{1,0:T(8,128)(2,1)S(1)}, u32[]{:S(2)}, u32[]{:S(2)}) collective-permute-start(bf16[256,1152]{1,0:T(8,128)(2,1)S(1)} %shard_map.43.refs_2_.refs_1_), channel_id=1, source_target_pairs={{0,8},{1,9},{2,10},{3,11},{4,12},{5,13},{6,14},{7,15},{8,0},{9,1},... | collective-permute-start | bytes 1769480 | tf_op jit(solution)/shard_map/ppermute | solution.py:367
  44.2 6.8 %collective-permute-start.3 = (bf16[512,1152]{1,0:T(8,128)(2,1)}, bf16[512,1152]{1,0:T(8,128)(2,1)}, u32[]{:S(2)}, u32[]{:S(2)}) collective-permute-start(bf16[512,1152]{1,0:T(8,128)(2,1)} %pad_maximum_fusion), channel_id=1, source_target_pairs={{0,16},{16,0},{1,17},{17,1},{2,18},{18,2},{3,19},{19,3},{4,20},{20... | collective-permute-start | bytes 3538952 | tf_op jit(solution)/shard_map/ppermute | solution.py:393
  48.9 4.7 %collective-permute-start.1 = (bf16[512,1152]{1,0:T(8,128)(2,1)S(1)}, bf16[512,1152]{1,0:T(8,128)(2,1)S(1)}, u32[]{:S(2)}, u32[]{:S(2)}) collective-permute-start(bf16[512,1152]{1,0:T(8,128)(2,1)S(1)} %bitcast.6), channel_id=1, source_target_pairs={{0,16},{16,0},{1,17},{17,1},{2,18},{18,2},{3,19},{19,3},{4,20},{20... | collective-permute-start | bytes 3538952 | tf_op jit(solution)/shard_map/ppermute | solution.py:398
  56.2 22.8 %all-to-all-start.2 = ((bf16[8,64,1152]{2,1,0:T(8,128)(2,1)}), bf16[8,64,1152]{2,1,0:T(8,128)(2,1)S(1)}, u32[]{:S(2)}, u32[]{:S(2)}) async-start(bf16[8,64,1152]{2,1,0:T(8,128)(2,1)} %bitcast.8), calls=%async_computation.2 | async-start | bytes 2359296 | tf_op jit(solution)/shard_map/all_to_all | solution.py:357
  64.5 11.8 %collective-permute-start.5 = (bf16[256,1152]{1,0:T(8,128)(2,1)S(1)}, bf16[256,1152]{1,0:T(8,128)(2,1)S(1)}, u32[]{:S(2)}, u32[]{:S(2)}) collective-permute-start(bf16[256,1152]{1,0:T(8,128)(2,1)S(1)} %shard_map.48), channel_id=1, source_target_pairs={{0,8},{1,9},{2,10},{3,11},{4,12},{5,13},{6,14},{7,15},{8,0},{9,1},... | collective-permute-start | bytes 1769480 | tf_op jit(solution)/shard_map/ppermute | solution.py:367
  77.2 17.7 %copy-start = (bf16[32,1152]{1,0:T(8,128)(2,1)S(1)}, bf16[32,1152]{1,0:T(8,128)(2,1)}, u32[]{:S(2)}) copy-start(bf16[32,1152]{1,0:T(8,128)(2,1)} %images_ref.1) | copy-start | bytes 221188
  77.3 17.7 %copy-start.1 = (bf16[32,1152]{1,0:T(8,128)(2,1)S(1)}, bf16[32,1152]{1,0:T(8,128)(2,1)}, u32[]{:S(2)}) copy-start(bf16[32,1152]{1,0:T(8,128)(2,1)} %texts_ref.1) | copy-start | bytes 221188
  79.1 15.9 %all-to-all-start.3 = ((bf16[8,32,1152]{2,1,0:T(8,128)(2,1)}), bf16[8,32,1152]{2,1,0:T(8,128)(2,1)S(1)}, u32[]{:S(2)}, u32[]{:S(2)}) async-start(bf16[8,32,1152]{2,1,0:T(8,128)(2,1)} %shard_map.49), calls=%async_computation.3 | async-start | bytes 1179648 | tf_op jit(solution)/shard_map/all_to_all | solution.py:357
  83.8 11.2 %collective-permute-start.4 = (bf16[32,1152]{1,0:T(8,128)(2,1)S(1)}, bf16[32,1152]{1,0:T(8,128)(2,1)S(1)}, u32[]{:S(2)}, u32[]{:S(2)}) collective-permute-start(bf16[32,1152]{1,0:T(8,128)(2,1)S(1)} %get-tuple-element.9), channel_id=1, source_target_pairs={{0,264},{1,265},{2,266},{3,267},{4,268},{5,269},{6,270},{7,271},{8... | collective-permute-start | bytes 221192 | tf_op jit(solution)/shard_map/ppermute | solution.py:367
